TPU v7x, 512 devices: a whole 4x4x16 slice. The times are simulated.
512 devices in a mesh: cfg: 2 (over y_lo), seq: 128 (over z, x, core), head: 2 (over y_hi).
Axes of the slice: x: 4, y: 4 (y_hi: 2, y_lo: 2; y = y_hi * 2 + y_lo), z: 16, core: 2. Of those that a mesh axis runs over, the one named last changes fastest.
Arguments:
- queries: bfloat16 [2, 4096, 20, 128], P('cfg', 'seq', 'head'), may hold values from -16 to 16
- self_keys: bfloat16 [2, 4096, 20, 128], P('cfg', 'seq', 'head'), may hold values from -16 to 16
- self_values: bfloat16 [2, 4096, 20, 128], P('cfg', 'seq', 'head'), may hold values from -6 to 6
- cross_queries: bfloat16 [2, 4096, 20, 128], P('cfg', 'seq', 'head'), may hold values from -16 to 16
- text_keys: bfloat16 [2, 512, 20, 128], P('cfg', None, 'head'), may hold values from -16 to 16
- text_values: bfloat16 [2, 512, 20, 128], P('cfg', None, 'head'), may hold values from -6 to 6
- out_weight: bfloat16 [20, 128, 64], P('head'), may hold values from -0.5 to 0.5
- latent: float32 [4096, 64], P('seq', 'cfg'), may hold values from -6 to 6
Outputs:
- guided: float32 [4096, 64], P('seq', 'cfg')
- latent_next: float32 [4096, 64], P('seq', 'cfg')
All inputs are finite; a program needn't handle non-finite values.
Results may differ from a plain program's by a relative error of at most 0.013.
Values may be sent and summed in bfloat16 or wider, within the bound.
No kernel may reach another device: no remote copies, remote signals or barrier semaphores. Data moves between devices by JAX's collectives and lax.ppermute only.
A program may use at most 128 MiB of HBM per device.

v0:
```python
import jax
import jax.numpy as jnp
from jax import lax
from jax.sharding import PartitionSpec as P

HEAD_DIM = 128


guidance = 5.0
step_size = 0.1


def partner_2(block, axis, apart):
    count = lax.axis_size(axis)
    route = []
    for low in range(count):
        high = low | 1 << apart
        if high != low and high < count:
            route += [(low, high), (high, low)]
    return lax.ppermute(block, axis, route)


def start_carry(queries):
    rows, heads_here, width = queries.shape
    weighted = jnp.zeros((heads_here, rows, width), jnp.float32)
    row_top = jnp.full((heads_here, rows), -1e30, jnp.float32)
    row_total = jnp.zeros((heads_here, rows), jnp.float32)
    return (weighted, row_top, row_total)


def fold_step(queries, carry, piece):
    weighted, row_top, row_total = carry
    key_piece, value_piece = piece
    scores = jnp.einsum(
        "qhd,khd->hqk", queries, key_piece, preferred_element_type=jnp.float32
    ) * HEAD_DIM ** (-0.5)
    new_top = jnp.maximum(row_top, jnp.max(scores, axis=-1))
    powers = jnp.exp(scores - new_top[..., None])
    row_total = jnp.sum(powers, axis=-1)
    weighted = jnp.einsum(
        "hqk,khd->hqd", powers.astype(jnp.bfloat16), value_piece, preferred_element_type=jnp.float32
    )
    return (weighted, new_top, row_total)


def finish(carry):
    weighted, row_top, row_total = carry
    result = weighted / row_total[..., None]
    return jnp.transpose(result, (1, 0, 2)).astype(jnp.bfloat16)


def shards(
    queries, self_keys, self_values, cross_queries, text_keys, text_values, out_weight, latent
):
    own_queries = queries[0]
    own_keys = self_keys[0]
    own_values = self_values[0]
    carry = fold_step(
        own_queries,
        start_carry(own_queries),
        (
            lax.all_gather(own_keys, "seq", axis=0, tiled=True),
            lax.all_gather(own_values, "seq", axis=0, tiled=True),
        ),
    )
    self_out = finish(carry)
    own_cross = cross_queries[0]
    cross_out = finish(fold_step(own_cross, start_carry(own_cross), (text_keys[0], text_values[0])))
    feature = (self_out.astype(jnp.float32) + cross_out.astype(jnp.float32)).astype(jnp.bfloat16)
    partial_velocity = jnp.einsum(
        "qhd,hdp->qp", feature, out_weight, preferred_element_type=jnp.float32
    )
    branch_index = lax.axis_index("cfg")
    half_width = latent.shape[1]
    own_start = branch_index * half_width
    other_start = (1 - branch_index) * half_width
    velocity = lax.psum(partial_velocity, "head")
    own_half = lax.dynamic_slice_in_dim(velocity, own_start, half_width, 1)
    outgoing = lax.dynamic_slice_in_dim(velocity, other_start, half_width, 1)
    partner = partner_2(outgoing, "cfg", 0)
    cond = jnp.where(branch_index == 0, own_half, partner)
    uncond = jnp.where(branch_index == 0, partner, own_half)
    guided = uncond + guidance * (cond - uncond)
    return (guided, latent + step_size * guided)


def solution(mesh):
    placed = (
        P("cfg", "seq", "head", None),
        P("cfg", "seq", "head", None),
        P("cfg", "seq", "head", None),
        P("cfg", "seq", "head", None),
        P("cfg", None, "head", None),
        P("cfg", None, "head", None),
        P("head", None, None),
        P("seq", "cfg"),
    )
    return jax.shard_map(
        shards,
        mesh=mesh,
        in_specs=placed,
        out_specs=(P("seq", "cfg"), P("seq", "cfg")),
        check_vma=False,
    )
```

profile of v0, /device:TPU:1, one launch (start us, length us, event | category | flops | bytes accessed | tf_op | source)
XLA Modules:
  0.0 349.6 jit_solution(16553028959384554707)
XLA Ops:
  7.2 0.0 copy-start
  7.2 0.0 all-gather.5.cloned.1.call-start
  7.2 0.7 all-gather.5.cloned.1.call-update
  7.9 0.0 all-gather.7.cloned.1.call-start
  8.0 0.7 all-gather.7.cloned.1.call-update
  8.7 0.0 copy-done
  8.7 1.5 fusion.77
  10.2 0.2 fusion.70
  10.4 1.7 fusion.57
  12.1 158.5 %all-gather.5.cloned.1.call-done = bf16[1,4096,10,128]{3,1,2,0:T(8,128)(2,1)} async-done(((bf16[1,32,10,128]{3,1,2,0:T(8,128)(2,1)}), bf16[1,4096,10,128]{3,1,2,0:T(8,128)(2,1)}) %all-gather.5.cloned.1.call-update) | async-done | bytes 10485776 | tf_op jit(solution)/shard_map/all_gather | solution.py:62
  170.6 6.5 %fusion.78 = (f32[10,32]{1,0:T(8,128)S(1)}, f32[10,32,4096]{2,1,0:T(8,128)S(1)}) fusion(bf16[1,4096,10,128]{3,1,2,0:T(8,128)(2,1)} %all-gather.5.cloned.1.call-done, bf16[1,32,10,128]{3,1,2,0:T(8,128)(2,1)} %param.8), kind=kOutput, calls=%fused_computation.39 | convolution fusion | flops 338165440 | bytes 15811840 | tf_op jit(solution)/shard_map/qhd,khd->hqk/dot_general | solution.py:34
  177.1 0.0 copy-start.1
  177.1 0.0 copy-start.2
  177.1 2.3 copy-done.1
  179.5 0.8 fusion.7
  180.3 141.3 %all-gather.7.cloned.1.call-done = bf16[1,4096,10,128]{3,1,2,0:T(8,128)(2,1)} async-done(((bf16[1,32,10,128]{3,1,2,0:T(8,128)(2,1)}), bf16[1,4096,10,128]{3,1,2,0:T(8,128)(2,1)}) %all-gather.7.cloned.1.call-update) | async-done | bytes 10485776 | tf_op jit(solution)/shard_map/all_gather | solution.py:63
  321.6 0.0 copy-done.2
  321.6 0.0 copy-start.3
  321.6 6.7 %fusion.65 = f32[32,64]{1,0:T(8,128)S(1)} fusion(bf16[10,128,64]{1,2,0:T(8,128)(2,1)S(1)} %copy-done.2, f32[32,10,128]{2,0,1:T(8,128)S(1)} %fusion.57, bf16[1,4096,10,128]{3,1,2,0:T(8,128)(2,1)} %all-gather.7.cloned.1.call-done, f32[10,32,4096]{2,1,0:T(8,128)} %copy-done.1, f32[10,32]{1,0:T(8,128)S(1)} %broadcast_maximum_fusion.1, f32[32,10]{0,1:T(8,128)S(1)} %bitcast.83), kind=kOutput, calls=%fused_computation.25 | convolution fusion | flops 343613440 | bytes 16067072 | tf_op jit(solution)/shard_map/qhd,hdp->qp/dot_general | solution.py:70
  328.3 9.2 %psum.7 = f32[32,64]{1,0:T(8,128)S(1)} all-reduce(f32[32,64]{1,0:T(8,128)S(1)} %fusion.65), channel_id=1, replica_groups=mesh['cfg'=2,'seq'=128,'head'=2] {'head'}, use_global_device_ids=true, to_apply=%region_4.0 | all-reduce | flops 2048 | bytes 16384 | tf_op jit(solution)/shard_map/psum | solution.py:77
  337.5 0.1 constant_dynamic-slice_fusion
  337.5 2.2 collective-permute-start
  339.8 2.3 collective-permute-done
  342.0 0.0 copy-done.3
  342.0 0.7 multiply_add_fusion
  (2 shorter events, 0.0 us)
Async XLA Ops:
  7.2 1.5 copy-start
  7.2 163.5 %all-gather.5.cloned.1.call-start = ((), (), s32[]{:S(2)}) async-start(), calls=%async_computation | async-start | bytes 10567680 | tf_op jit(solution)/shard_map/all_gather | solution.py:62
  7.9 313.7 %all-gather.7.cloned.1.call-start = ((), (), s32[]{:S(2)}) async-start(), calls=%async_computation.1 | async-start | bytes 10567680 | tf_op jit(solution)/shard_map/all_gather | solution.py:63
  177.1 2.4 copy-start.1
  177.1 144.5 %copy-start.2 = (bf16[10,128,64]{1,2,0:T(8,128)(2,1)S(1)}, bf16[10,128,64]{1,2,0:T(8,128)(2,1)}, u32[]{:S(2)}) copy-start(bf16[10,128,64]{1,2,0:T(8,128)(2,1)} %param.14) | copy-start | bytes 491524
  321.6 20.4 %copy-start.3 = (f32[32,32]{1,0:T(8,128)S(1)}, f32[32,32]{1,0:T(8,128)}, u32[]{:S(2)}) copy-start(f32[32,32]{1,0:T(8,128)} %param.15) | copy-start | bytes 12292
  337.5 4.5 %collective-permute-start = (f32[32,32]{1,0:T(8,128)S(1)}, f32[32,32]{1,0:T(8,128)S(1)}, u32[]{:S(2)}, u32[]{:S(2)}) collective-permute-start(f32[32,32]{1,0:T(8,128)S(1)} %constant_dynamic-slice_fusion), channel_id=1, source_target_pairs={{0,256},{256,0},{1,257},{257,1},{2,258},{258,2},{3,259},{259,3},{4... | collective-permute-start | bytes 12296 | tf_op jit(solution)/shard_map/ppermute | solution.py:20
Sparse Core Ops, SparseCore 0:
  11.0 159.5 all-gather.4
  173.7 147.9 all-gather.6
where the time goes:
time: 351 us; the launch traced here: 350 us
  waiting for transfers between devices  303 us (86%)
  matrix products  16.3 us (5%)
  between operations  14.1 us (4%)
  blocking collectives  9.16 us (3%)
    all_gather x1, waiting for transfers between devices, shards(): lax.all_gather(own_keys, 'seq', axis=0, tiled=True)  159 us
    all_gather x1, waiting for transfers between devices, shards(): lax.all_gather(own_values, 'seq', axis=0, tiled=True)  141 us
    psum x1, blocking collectives, shards(): velocity = lax.psum(partial_velocity, 'head')  9.16 us
    dot_general x2, matrix products, fold_step(): jnp.einsum('qhd,khd->hqk', queries, key_piece, preferred_element_type=jnp...  7.97 us
  transfers between devices with their start and end apart: 3, of which 3 were waited for; matrix products, arithmetic and copies ran while one was open for 3% of the time, Pallas kernels for 0%

commit v1 on v0

v1 whole, which is shorter than its diff:
```python
import math

import jax
import jax.numpy as jnp
from jax import lax
from jax.experimental import pallas as pl
from jax.experimental.pallas import tpu as pltpu
from jax.sharding import Mesh, PartitionSpec as P

HEAD_DIM = 128
HEADS_HERE = 10
ROWS = 32
SPREAD = 16
BLOCK = 80
KV_ROWS = 48
GUIDANCE = 5.0
STEP = 0.1
EXP2_SCALE = math.log2(math.e) / math.sqrt(HEAD_DIM)
VMEM_LIMIT = 56 * 1024 * 1024


def vmem():
    return pl.BlockSpec(memory_space=pltpu.VMEM)


def params():
    return pltpu.CompilerParams(vmem_limit_bytes=VMEM_LIMIT)


def pack_kernel(q_ref, k_ref, v_ref, w_ref, out_ref):
    for h in range(HEADS_HERE):
        out_ref[h, 0:32, :] = q_ref[h]
        out_ref[h, 32:64, :] = k_ref[h]
        projected = lax.dot_general(
            v_ref[h], w_ref[h], (((1,), (1,)), ((), ())), preferred_element_type=jnp.float32
        )
        packed = jnp.concatenate([projected[0:16], projected[16:32]], axis=1)
        out_ref[h, 64:80, :] = packed.astype(jnp.bfloat16)
    for h in range(HEADS_HERE, SPREAD):
        out_ref[h] = jnp.zeros((BLOCK, HEAD_DIM), jnp.bfloat16)


def pack(q, k, v, w):
    return pl.pallas_call(
        pack_kernel,
        out_shape=jax.ShapeDtypeStruct((SPREAD, BLOCK, HEAD_DIM), jnp.bfloat16),
        in_specs=[vmem()] * 4,
        out_specs=vmem(),
        compiler_params=params(),
        name="pack",
    )(q, k, v, w)


def scores(q, keys):
    return lax.dot_general(q, keys, (((1,), (1,)), ((), ())), preferred_element_type=jnp.float32)


def attend_kernel(where_ref, recv_ref, own_ref, other_ref, cross_ref, out_ref, total_ref):
    z = where_ref[0]
    branch = where_ref[1]
    active = z < HEADS_HERE
    keys, values = [], []
    for ref in (own_ref, other_ref):
        keys.append((ref[:, 0:16, :].reshape(1024, HEAD_DIM), ref[:, 16:32, :].reshape(1024, HEAD_DIM)))
        values.append(ref[:, 32:48, :].reshape(1024, HEAD_DIM))
    step = 256
    for first in range(0, SPREAD * ROWS, step):
        q = recv_ref[first // ROWS:(first + step) // ROWS, 0:32, :].reshape(step, HEAD_DIM)
        found = [[scores(q, part) for part in pair] for pair in keys]
        top = None
        for pair in found:
            for s in pair:
                t = jnp.max(s, axis=1, keepdims=True)
                top = t if top is None else jnp.maximum(top, t)
        top = top * EXP2_SCALE
        weight_sum = jnp.zeros((step, 1), jnp.float32)
        halves = [jnp.zeros((step, HEAD_DIM), jnp.float32) for _ in range(2)]
        for pair, value in zip(found, values):
            for i, s in enumerate(pair):
                p = jnp.exp2(s * EXP2_SCALE - top)
                weight_sum = weight_sum + jnp.sum(p, axis=1, keepdims=True)
                halves[i] = halves[i] + jnp.dot(p.astype(jnp.bfloat16), value, preferred_element_type=jnp.float32)
        summed = halves[0] + pltpu.roll(halves[1], 64, 1)
        total_ref[first:first + step, :] = jnp.where(active, summed / weight_sum, 0.0)
    mine = pl.ds(pl.multiple_of(z * ROWS, ROWS), ROWS)
    total_ref[mine, :] = total_ref[mine, :] + cross_ref[...]
    total = total_ref[...] * jnp.where(branch == 0, GUIDANCE, 1.0 - GUIDANCE)
    total = total.reshape(SPREAD, 4, 8, HEAD_DIM)
    lane_group = lax.broadcasted_iota(jnp.int32, (SPREAD * 8, HEAD_DIM), 1) // 32
    blocks = []
    for half in range(2):
        block = jnp.zeros((SPREAD * 8, HEAD_DIM), jnp.float32)
        for g in range(4):
            piece = total[:, g].reshape(SPREAD * 8, HEAD_DIM)
            shift = (32 * g - 32 * half) % HEAD_DIM
            if shift:
                piece = pltpu.roll(piece, shift, 1)
            block = jnp.where(lane_group == g, piece, block)
        blocks.append(block.reshape(SPREAD, 1, 8, HEAD_DIM))
    out = jnp.concatenate([blocks[0], blocks[0], blocks[1], blocks[1]], axis=1)
    out_ref[...] = out.reshape(SPREAD * 32, HEAD_DIM).astype(jnp.bfloat16)


def attend(where, recv, own, other, cross):
    return pl.pallas_call(
        attend_kernel,
        out_shape=jax.ShapeDtypeStruct((SPREAD * 32, HEAD_DIM), jnp.bfloat16),
        in_specs=[pl.BlockSpec(memory_space=pltpu.SMEM)] + [vmem()] * 4,
        out_specs=vmem(),
        scratch_shapes=[pltpu.VMEM((SPREAD * ROWS, HEAD_DIM), jnp.float32)],
        compiler_params=params(),
        name="attend",
    )(where, recv, own, other, cross)


def finish_kernel(parts_ref, latent_ref, guided_ref, next_ref):
    parts = parts_ref[...].astype(jnp.float32).reshape(64, 8, HEAD_DIM)
    summed = jnp.sum(parts, axis=0)
    pieces = [summed] + [pltpu.roll(summed, HEAD_DIM - 32 * g, 1) for g in range(1, 4)]
    for g, piece in enumerate(pieces):
        rows = slice(8 * g, 8 * g + 8)
        guided_ref[rows, :] = piece[:, 0:32]
        next_ref[rows, :] = latent_ref[rows, :] + STEP * piece[:, 0:32]


def finish(parts, latent):
    shape = jax.ShapeDtypeStruct(latent.shape, jnp.float32)
    return pl.pallas_call(
        finish_kernel,
        out_shape=(shape, shape),
        in_specs=[vmem()] * 2,
        out_specs=(vmem(), vmem()),
        compiler_params=params(),
        name="finish",
    )(parts, latent)


def cross_velocity(queries, keys, values, w):
    s = jnp.einsum("hqd,hkd->hqk", queries, keys, preferred_element_type=jnp.float32) * HEAD_DIM ** (-0.5)
    top = jnp.max(s, axis=-1, keepdims=True)
    p = jnp.exp(s - top)
    out = jnp.einsum("hqk,hkd->hqd", p.astype(jnp.bfloat16), values, preferred_element_type=jnp.float32)
    out = (out / jnp.sum(p, axis=-1, keepdims=True)).astype(jnp.bfloat16)
    return jnp.einsum("hqd,hpd->qp", out, w, preferred_element_type=jnp.float32)


def heads_first(block):
    return jnp.transpose(block, (1, 0, 2))


def shards(queries, self_keys, self_values, cross_queries, text_keys, text_values, out_weight, latent):
    w = jnp.transpose(out_weight, (0, 2, 1))
    packed = pack(heads_first(queries[0]), heads_first(self_keys[0]), heads_first(self_values[0]), w)
    recv = lax.all_to_all(packed, "z", 0, 0, tiled=True)
    cross = cross_velocity(
        heads_first(cross_queries[0]), heads_first(text_keys[0]), heads_first(text_values[0]), w
    )
    cross = jnp.pad(cross, ((0, 0), (0, 64)))
    kv = jnp.broadcast_to(recv[None, :, 32:80, :], (4, SPREAD, KV_ROWS, HEAD_DIM))
    own = lax.all_to_all(kv, "x", 0, 0, tiled=True).reshape(64, KV_ROWS, HEAD_DIM)
    other = lax.ppermute(own, "c", [(0, 1), (1, 0)])
    where = jnp.stack([lax.axis_index("z"), lax.axis_index("cfg")]).astype(jnp.int32)
    back = attend(where, recv, own, other, cross)
    parts = lax.all_to_all(back, ("z", "cfg", "head"), 0, 0, tiled=True)
    return finish(parts, latent)


def solution(mesh):
    split = Mesh(mesh.devices.reshape(2, SPREAD, 4, 2, 2), ("cfg", "z", "x", "c", "head"))
    seq = ("z", "x", "c")
    tokens = P("cfg", seq, "head", None)
    text = P("cfg", None, "head", None)
    placed = (tokens, tokens, tokens, tokens, text, text, P("head", None, None), P(seq, "cfg"))
    return jax.shard_map(
        shards,
        mesh=split,
        in_specs=placed,
        out_specs=(P(seq, "cfg"), P(seq, "cfg")),
        check_vma=False,
    )
```

time: 351 us -> 99.8 us (0.28)
  waiting for transfers between devices: 303 us -> 0.01 us
  blocking collectives: 9.16 us -> 71.5 us
  between operations: 14.1 us -> 0.69 us
  matrix products: 16.3 us -> 3.94 us
  Pallas kernels: 0 us -> 10 us
  starting transfers between devices: 2.28 us -> 9.83 us
    all_gather x2 -> x0, waiting for transfers between devices: 300 us -> none  [the longest x1 159 us: shards(): lax.all_gather(own_keys, 'seq', axis=0, tiled=True)]
    all_to_all x0 -> x3, blocking collectives: none -> 71.5 us  [the longest x1 31 us: shards(): recv = lax.all_to_all(packed, 'z', 0, 0, tiled=True)]
    dot_general x4 -> x2, matrix products: 16.3 us -> 3.94 us  [the longest x1 2.43 us: cross_velocity(): return jnp.einsum('hqd,hpd->qp', out, w, preferred_element_type=jnp.float32)]
    pallas_call x0 -> x3, Pallas kernels: none -> 10 us  [the longest x1 6.25 us: attend(): pl.pallas_call(attend_kernel, out_shape=jax.ShapeDtypeStruct((SPREAD * 32...]
    psum x1 -> x0, blocking collectives: 9.16 us -> none  [shards(): velocity = lax.psum(partial_velocity, 'head')]
    ppermute x1, starting transfers between devices: 2.2 us -> 9.83 us  [shards(): other = lax.ppermute(own, 'c', [(0, 1), (1, 0)])]
  transfers between devices with their start and end apart: 3 -> 1, of which waited for: 3 -> 0; matrix products, arithmetic and copies ran while one was open for 3% -> 6% of each run, Pallas kernels for 0% -> 0%
where the time goes in v1:
time: 99.8 us; the launch traced here: 99.2 us
  blocking collectives  71.5 us (72%)
  Pallas kernels  10 us (10%)
  starting transfers between devices  9.83 us (10%)
  matrix products  3.94 us (4%)
  local copies, waits for them, and re-layouts  2.36 us (2%)
    all_to_all x1, blocking collectives, shards(): recv = lax.all_to_all(packed, 'z', 0, 0, tiled=True)  31 us
    all_to_all x1, blocking collectives, shards(): parts = lax.all_to_all(back, ('z', 'cfg', 'head'), 0, 0, tiled=True)  28.4 us
    all_to_all x1, blocking collectives, shards(): lax.all_to_all(kv, 'x', 0, 0, tiled=True).reshape(64, KV_ROWS, HEAD_DIM)  12.2 us
    ppermute x1, starting transfers between devices, shards(): other = lax.ppermute(own, 'c', [(0, 1), (1, 0)])  9.83 us
    pallas_call x1, Pallas kernels, attend(): pl.pallas_call(attend_kernel, out_shape=jax.ShapeDtypeStruct((SPREAD * 32...  6.25 us
    dot_general x1, matrix products, cross_velocity(): return jnp.einsum('hqd,hpd->qp', out, w, preferred_element_type=jnp.float32)  2.43 us
    pallas_call x1, Pallas kernels, pack(): pl.pallas_call(pack_kernel, out_shape=jax.ShapeDtypeStruct((SPREAD, BLOCK...  2.12 us
  transfers between devices with their start and end apart: 1, of which 0 were waited for; matrix products, arithmetic and copies ran while one was open for 6% of the time, Pallas kernels for 0%

profile of v1, /device:TPU:1, one launch (start us, length us, event | category | flops | bytes accessed | tf_op | source)
XLA Modules:
  0.0 99.2 jit_solution(18389184557103774766)
XLA Ops:
  0.6 0.0 copy-start
  0.6 2.1 %pack.1 = bf16[16,80,128]{2,1,0:T(8,128)(2,1)} custom-call(bf16[10,32,128]{2,1,0:T(8,128)(2,1)} %bitcast.53, bf16[10,32,128]{2,1,0:T(8,128)(2,1)} %bitcast.54, bf16[10,32,128]{2,1,0:T(8,128)(2,1)} %bitcast.55, bf16[10,64,128]{2,1,0:T(8,128)(2,1)} %bitcast.50), custom_call_target="tpu_custom_call" | custom-call | tf_op jit(solution)/shard_map/pack/pallas_call | solution.py:44
  2.8 31.0 %all_to_all.21.recv_ref = bf16[16,80,128]{2,1,0:T(8,128)(2,1)S(1)} all-to-all(bf16[16,80,128]{2,1,0:T(8,128)(2,1)} %pack.1), channel_id=1, replica_groups=mesh['cfg'=2,'z'=16,'x'=4,'c'=2,'head'=2] {'z'}, dimensions={0} | all-to-all | bytes 655360 | tf_op jit(solution)/shard_map/all_to_all | solution.py:154
  33.7 0.0 copy-start.2
  33.8 0.1 broadcast_in_dim.2
  33.9 12.2 %all_to_all.22 = bf16[4,16,48,128]{3,2,1,0:T(8,128)(2,1)S(1)} all-to-all(bf16[4,16,48,128]{3,2,1,0:T(8,128)(2,1)S(1)} %broadcast_in_dim.2), channel_id=1, replica_groups=mesh['cfg'=2,'z'=16,'x'=4,'c'=2,'head'=2] {'x'}, dimensions={0} | all-to-all | bytes 1572864 | tf_op jit(solution)/shard_map/all_to_all | solution.py:160
  46.0 0.0 copy-done.2
  46.0 0.0 copy-start.1
  46.0 9.8 %collective-permute-start = (bf16[64,48,128]{2,1,0:T(8,128)(2,1)S(1)}, bf16[64,48,128]{2,1,0:T(8,128)(2,1)S(1)}, u32[]{:S(2)}, u32[]{:S(2)}) collective-permute-start(bf16[64,48,128]{2,1,0:T(8,128)(2,1)S(1)} %bitcast.48), channel_id=1, source_target_pairs={{0,2},{2,0},{1,3},{3,1},{4,6},{6,4},{5,7},{7,5},{8,10},{10,8},{9,1... | collective-permute-start | bytes 2359304 | tf_op jit(solution)/shard_map/ppermute | solution.py:161
  55.9 0.0 copy-done
  55.9 1.5 %fusion.28 = (f32[10,32]{1,0:T(8,128)S(1)}, f32[10,32,512]{2,1,0:T(8,128)S(1)}) fusion(bf16[1,512,10,128]{3,1,2,0:T(8,128)(2,1)S(1)} %copy-done, bf16[1,32,10,128]{3,1,2,0:T(8,128)(2,1)} %param.11), kind=kOutput, calls=%fused_computation.17 | convolution fusion | flops 42270400 | bytes 2049280 | tf_op jit(solution)/shard_map/hqd,hkd->hqk/dot_general | solution.py:139
  57.4 0.2 fusion.19
  57.6 0.0 copy-done.1
  57.6 2.4 %fusion.16 = f32[32,64]{1,0:T(8,128)} fusion(bf16[1,512,10,128]{3,1,2,0:T(8,128)(2,1)} %param.13, f32[10,32,512]{2,1,0:T(8,128)S(1)} %get-tuple-element.3, f32[10,32]{1,0:T(8,128)S(1)} %get-tuple-element.2, f32[10,32]{1,0:T(8,128)S(1)} %fusion.19, bf16[10,128,64]{1,2,0:T(8,128)(2,1)} %param.14), kind=kOutput, calls=%fused_computation.8 | convolution fusion | flops 47595520 | bytes 2140672 | tf_op jit(solution)/shard_map/hqd,hpd->qp/dot_general | solution.py:144
  60.1 1.3 %pad.4.cross_ref = f32[32,128]{1,0:T(8,128)} pad(f32[32,64]{1,0:T(8,128)} %fusion.16, f32[]{:T(128)} %constant.18.clone.1), padding=0_0x0_64 | pad | bytes 24580 | tf_op jit(solution)/shard_map/jit(_pad)/pad | solution.py:158
  61.4 0.6 pad_add_fusion.where_ref
  62.0 0.0 collective-permute-done.other_ref
  62.0 0.0 copy-start.3
  62.0 0.9 copy-done.3
  62.9 6.3 %attend.1 = bf16[512,128]{1,0:T(8,128)(2,1)} custom-call(s32[2]{0:T(128)} %pad_add_fusion.where_ref, bf16[16,80,128]{2,1,0:T(8,128)(2,1)} %copy-done.2, bf16[64,48,128]{2,1,0:T(8,128)(2,1)} %bitcast.49, bf16[64,48,128]{2,1,0:T(8,128)(2,1)} %copy-done.3, f32[32,128]{1,0:T(8,128)} %pad.4.cross_ref), custom_call_target="tpu_custom_call" | custom-call | tf_op jit(solution)/shard_map/attend/pallas_call | solution.py:105
  69.2 28.4 %all_to_all.23 = bf16[64,8,128]{2,1,0:T(8,128)(2,1)} all-to-all(bf16[64,8,128]{2,1,0:T(8,128)(2,1)} %bitcast.51), channel_id=1, replica_groups=mesh['cfg'=2,'z'=16,'x'=4,'c'=2,'head'=2] {'z','cfg','head'}, dimensions={0} | all-to-all | bytes 262144 | tf_op jit(solution)/shard_map/all_to_all | solution.py:164
  97.5 1.7 %finish.1 = (f32[32,32]{1,0:T(8,128)}, f32[32,32]{1,0:T(8,128)}) custom-call(bf16[512,128]{1,0:T(8,128)(2,1)} %bitcast.52, f32[32,32]{1,0:T(8,128)} %latent_ref.1), custom_call_target="tpu_custom_call" | custom-call | tf_op jit(solution)/shard_map/finish/pallas_call | solution.py:128
  (1 shorter events, 0.0 us)
Async XLA Ops:
  0.6 55.2 %copy-start = (bf16[1,512,10,128]{3,1,2,0:T(8,128)(2,1)S(1)}, bf16[1,512,10,128]{3,1,2,0:T(8,128)(2,1)}, u32[]{:S(2)}) copy-start(bf16[1,512,10,128]{3,1,2,0:T(8,128)(2,1)} %param.12) | copy-start | bytes 3932164
  33.7 12.3 %copy-start.2 = (bf16[16,80,128]{2,1,0:T(8,128)(2,1)}, bf16[16,80,128]{2,1,0:T(8,128)(2,1)S(1)}, u32[]{:S(2)}) copy-start(bf16[16,80,128]{2,1,0:T(8,128)(2,1)S(1)} %all_to_all.21.recv_ref) | copy-start | bytes 983044
  46.0 11.6 %copy-start.1 = (bf16[4,16,48,128]{3,2,1,0:T(8,128)(2,1)}, bf16[4,16,48,128]{3,2,1,0:T(8,128)(2,1)S(1)}, u32[]{:S(2)}) copy-start(bf16[4,16,48,128]{3,2,1,0:T(8,128)(2,1)S(1)} %all_to_all.22) | copy-start | bytes 2359300
  46.0 16.0 %collective-permute-start = (bf16[64,48,128]{2,1,0:T(8,128)(2,1)S(1)}, bf16[64,48,128]{2,1,0:T(8,128)(2,1)S(1)}, u32[]{:S(2)}, u32[]{:S(2)}) collective-permute-start(bf16[64,48,128]{2,1,0:T(8,128)(2,1)S(1)} %bitcast.48), channel_id=1, source_target_pairs={{0,2},{2,0},{1,3},{3,1},{4,6},{6,4},{5,7},{7,5},{8,10},{10,8},{9,1... | collective-permute-start | bytes 2359304 | tf_op jit(solution)/shard_map/ppermute | solution.py:161
  62.0 0.9 copy-start.3

commit v2 on v1

v2 whole, which is shorter than its diff:
```python
import math

import jax
import jax.numpy as jnp
import numpy as np
from jax import lax
from jax.experimental import pallas as pl
from jax.experimental.pallas import tpu as pltpu
from jax.sharding import Mesh, PartitionSpec as P

HEAD_DIM = 128
HEADS_HERE = 10
ROWS = 32
SPREAD = 16
BLOCK = 80
KV_ROWS = 48
FIRST_PLANE = 10
PLANES = [(FIRST_PLANE + i) % SPREAD for i in range(SPREAD)]
AXES = ("cfg", "z", "x", "c", "head")
GUIDANCE = 5.0
STEP = 0.1
EXP2_SCALE = math.log2(math.e) / math.sqrt(HEAD_DIM)
VMEM_LIMIT = 36 * 1024 * 1024


def vmem():
    return pl.BlockSpec(memory_space=pltpu.VMEM)


def params():
    return pltpu.CompilerParams(vmem_limit_bytes=VMEM_LIMIT)


def pack_kernel(q_ref, k_ref, v_ref, w_ref, out_ref, blocks, v_scratch, w_scratch, sems):
    loads = [
        pltpu.make_async_copy(v_ref, v_scratch, sems.at[0]),
        pltpu.make_async_copy(w_ref, w_scratch, sems.at[1]),
        pltpu.make_async_copy(q_ref, blocks.at[0:HEADS_HERE, 0:32, :], sems.at[2]),
        pltpu.make_async_copy(k_ref, blocks.at[0:HEADS_HERE, 32:64, :], sems.at[3]),
    ]
    for load in loads:
        load.start()
    for h in range(HEADS_HERE, SPREAD):
        blocks[h] = jnp.zeros((BLOCK, HEAD_DIM), jnp.bfloat16)
    loads[0].wait()
    loads[1].wait()
    for h in range(HEADS_HERE):
        projected = lax.dot_general(
            v_scratch[h], w_scratch[h], (((1,), (1,)), ((), ())), preferred_element_type=jnp.float32
        )
        packed = jnp.concatenate([projected[0:16], projected[16:32]], axis=1)
        blocks[h, 64:80, :] = packed.astype(jnp.bfloat16)
    loads[2].wait()
    loads[3].wait()
    store = pltpu.make_async_copy(blocks, out_ref, sems.at[4])
    store.start()
    store.wait()


def pack(q, k, v, w):
    anywhere = pl.BlockSpec(memory_space=pl.ANY)
    return pl.pallas_call(
        pack_kernel,
        out_shape=jax.ShapeDtypeStruct((SPREAD, BLOCK, HEAD_DIM), jnp.bfloat16),
        in_specs=[anywhere] * 4,
        out_specs=anywhere,
        scratch_shapes=[
            pltpu.VMEM((SPREAD, BLOCK, HEAD_DIM), jnp.bfloat16),
            pltpu.VMEM((HEADS_HERE, ROWS, HEAD_DIM), jnp.bfloat16),
            pltpu.VMEM((HEADS_HERE, 64, HEAD_DIM), jnp.bfloat16),
            pltpu.SemaphoreType.DMA((5,)),
        ],
        compiler_params=pltpu.CompilerParams(vmem_limit_bytes=60 * 1024 * 1024),
        name="pack",
    )(q, k, v, w)


def cross_kernel(q_ref, k_ref, v_ref, w_ref, sum_ref, zero_ref):
    total = jnp.zeros((ROWS, 64), jnp.float32)
    for h in range(HEADS_HERE):
        s = scores(q_ref[h], k_ref[h])
        top = jnp.max(s, axis=1, keepdims=True) * EXP2_SCALE
        p = jnp.exp2(s * EXP2_SCALE - top)
        o = jnp.dot(p.astype(jnp.bfloat16), v_ref[h], preferred_element_type=jnp.float32)
        o = o / jnp.sum(p, axis=1, keepdims=True)
        total = total + scores(o.astype(jnp.bfloat16), w_ref[h])
    sum_ref[...] = jnp.concatenate([total, jnp.zeros((ROWS, 64), jnp.float32)], axis=1)
    zero_ref[0] = 0


def cross(q, k, v, w):
    return pl.pallas_call(
        cross_kernel,
        out_shape=(
            jax.ShapeDtypeStruct((ROWS, HEAD_DIM), jnp.float32),
            jax.ShapeDtypeStruct((1,), jnp.int32),
        ),
        in_specs=[vmem()] * 4,
        out_specs=(vmem(), pl.BlockSpec(memory_space=pltpu.SMEM)),
        compiler_params=params(),
        cost_estimate=pl.CostEstimate(flops=90_000_000, bytes_accessed=3_200_000, transcendentals=170_000),
        name="cross",
    )(q, k, v, w)


def scores(q, keys):
    return lax.dot_general(q, keys, (((1,), (1,)), ((), ())), preferred_element_type=jnp.float32)


def load_keys(ref):
    even, odd = ref[:, 0:16, :], ref[:, 16:32, :]
    return [part.reshape(1024, HEAD_DIM) for part in (even, odd)], ref[:, 32:48, :].reshape(1024, HEAD_DIM)


def half_attention(q, keys, value, found_top=None):
    found = [scores(q, part) for part in keys]
    top = jnp.max(jnp.maximum(found[0], found[1]), axis=1, keepdims=True) * EXP2_SCALE
    if found_top is not None:
        top = jnp.maximum(top, found_top)
    weights = [jnp.exp2(s * EXP2_SCALE - top) for s in found]
    weight_sum = jnp.sum(weights[0] + weights[1], axis=1, keepdims=True)
    even, odd = [jnp.dot(p.astype(jnp.bfloat16), value, preferred_element_type=jnp.float32) for p in weights]
    return even + pltpu.roll(odd, 64, 1), weight_sum, top


STEP_ROWS = 256


def first_kernel(q_ref, own_ref, sum_ref, stat_ref):
    keys, value = load_keys(own_ref)
    for first in range(0, SPREAD * ROWS, STEP_ROWS):
        rows = slice(first, first + STEP_ROWS)
        q = q_ref[first // ROWS:(first + STEP_ROWS) // ROWS, 0:32, :].reshape(STEP_ROWS, HEAD_DIM)
        summed, weight_sum, top = half_attention(q, keys, value)
        sum_ref[rows, :] = summed
        stat_ref[rows, :] = jnp.concatenate(
            [jnp.broadcast_to(weight_sum, (STEP_ROWS, 64)), jnp.broadcast_to(top, (STEP_ROWS, 64))], axis=1
        )


def first_half(recv, own):
    shape = jax.ShapeDtypeStruct((SPREAD * ROWS, HEAD_DIM), jnp.float32)
    return pl.pallas_call(
        first_kernel,
        out_shape=(shape, shape),
        in_specs=[vmem()] * 2,
        out_specs=(vmem(), vmem()),
        compiler_params=params(),
        cost_estimate=pl.CostEstimate(flops=540_000_000, bytes_accessed=1_600_000, transcendentals=1_000_000),
        name="first_half",
    )(recv, own)


def attend_kernel(where_ref, recv_ref, other_ref, sum_ref, stat_ref, cross_ref, out_ref, total_ref):
    slot = where_ref[0]
    branch = where_ref[1]
    active = slot < HEADS_HERE
    keys, value = load_keys(other_ref)
    for first in range(0, SPREAD * ROWS, STEP_ROWS):
        rows = slice(first, first + STEP_ROWS)
        q = recv_ref[first // ROWS:(first + STEP_ROWS) // ROWS, 0:32, :].reshape(STEP_ROWS, HEAD_DIM)
        first_sum, first_top = stat_ref[rows, 0:1], stat_ref[rows, 64:65]
        summed, weight_sum, top = half_attention(q, keys, value, first_top)
        scale = jnp.exp2(first_top - top)
        summed = summed + sum_ref[rows, :] * scale
        weight_sum = weight_sum + first_sum * scale
        total_ref[rows, :] = jnp.where(active, summed / weight_sum, 0.0)
    mine = pl.ds(pl.multiple_of(slot * ROWS, ROWS), ROWS)
    total_ref[mine, :] = total_ref[mine, :] + cross_ref[...]
    total = total_ref[...] * jnp.where(branch == 0, GUIDANCE, 1.0 - GUIDANCE)
    total = total.reshape(SPREAD, 4, 8, HEAD_DIM)
    lane_group = lax.broadcasted_iota(jnp.int32, (SPREAD * 8, HEAD_DIM), 1) // 32
    blocks = []
    for half in range(2):
        block = jnp.zeros((SPREAD * 8, HEAD_DIM), jnp.float32)
        for g in range(4):
            piece = total[:, g].reshape(SPREAD * 8, HEAD_DIM)
            shift = (32 * g - 32 * half) % HEAD_DIM
            if shift:
                piece = pltpu.roll(piece, shift, 1)
            block = jnp.where(lane_group == g, piece, block)
        blocks.append(block.reshape(SPREAD, 1, 8, HEAD_DIM))
    out = jnp.concatenate([blocks[0], blocks[0], blocks[1], blocks[1]], axis=1)
    out_ref[...] = out.reshape(SPREAD * 32, HEAD_DIM).astype(jnp.bfloat16)


def attend(where, recv, other, summed, stat, cross):
    return pl.pallas_call(
        attend_kernel,
        out_shape=jax.ShapeDtypeStruct((SPREAD * 32, HEAD_DIM), jnp.bfloat16),
        in_specs=[pl.BlockSpec(memory_space=pltpu.SMEM)] + [vmem()] * 5,
        out_specs=vmem(),
        scratch_shapes=[pltpu.VMEM((SPREAD * ROWS, HEAD_DIM), jnp.float32)],
        compiler_params=params(),
        name="attend",
    )(where, recv, other, summed, stat, cross)


def finish_kernel(parts_ref, latent_ref, guided_ref, next_ref):
    parts = parts_ref[...].astype(jnp.float32).reshape(64, 8, HEAD_DIM)
    summed = jnp.sum(parts, axis=0)
    pieces = [summed] + [pltpu.roll(summed, HEAD_DIM - 32 * g, 1) for g in range(1, 4)]
    for g, piece in enumerate(pieces):
        rows = slice(8 * g, 8 * g + 8)
        guided_ref[rows, :] = piece[:, 0:32]
        next_ref[rows, :] = latent_ref[rows, :] + STEP * piece[:, 0:32]


def finish(parts, latent):
    shape = jax.ShapeDtypeStruct(latent.shape, jnp.float32)
    return pl.pallas_call(
        finish_kernel,
        out_shape=(shape, shape),
        in_specs=[vmem()] * 2,
        out_specs=(vmem(), vmem()),
        compiler_params=params(),
        name="finish",
    )(parts, latent)


def back_groups():
    index = np.arange(512).reshape(2, SPREAD, 4, 2, 2)
    return [
        [int(index[f, z, x, c, h]) for z in PLANES for f in range(2) for h in range(2)]
        for x in range(4)
        for c in range(2)
    ]


def heads_first(block):
    return jnp.transpose(block, (1, 0, 2))


def shards(queries, self_keys, self_values, cross_queries, text_keys, text_values, out_weight, latent):
    w = jnp.transpose(out_weight, (0, 2, 1))
    packed = pack(heads_first(queries[0]), heads_first(self_keys[0]), heads_first(self_values[0]), w)
    recv = lax.all_to_all(packed, "z", 0, 0, tiled=True, axis_index_groups=[PLANES])
    crossed, zero = cross(heads_first(cross_queries[0]), heads_first(text_keys[0]), heads_first(text_values[0]), w)
    kv = jnp.where(zero[0] == 0, recv[:, 32:80, :], jnp.zeros((), recv.dtype))
    kv = jnp.broadcast_to(kv[None], (4, SPREAD, KV_ROWS, HEAD_DIM))
    own = lax.all_to_all(kv, "x", 0, 0, tiled=True).reshape(64, KV_ROWS, HEAD_DIM)
    other = lax.ppermute(own, "c", [(0, 1), (1, 0)])
    summed, stat = first_half(recv, own)
    slot = lax.rem(lax.axis_index("z") + (SPREAD - FIRST_PLANE), SPREAD)
    where = jnp.stack([slot, lax.axis_index("cfg")]).astype(jnp.int32)
    back = attend(where, recv, other, summed, stat, crossed)
    parts = lax.all_to_all(back, AXES, 0, 0, tiled=True, axis_index_groups=back_groups())
    return finish(parts, latent)


def solution(mesh):
    split = Mesh(mesh.devices.reshape(2, SPREAD, 4, 2, 2), ("cfg", "z", "x", "c", "head"))
    seq = ("z", "x", "c")
    tokens = P("cfg", seq, "head", None)
    text = P("cfg", None, "head", None)
    placed = (tokens, tokens, tokens, tokens, text, text, P("head", None, None), P(seq, "cfg"))
    return jax.shard_map(
        shards,
        mesh=split,
        in_specs=placed,
        out_specs=(P(seq, "cfg"), P(seq, "cfg")),
        check_vma=False,
    )
```

time: 99.8 us -> 85.2 us (0.85)
  blocking collectives: 71.5 us -> 37.9 us
  starting transfers between devices: 9.83 us -> 22.6 us
  waiting for transfers between devices: 0.01 us -> 8.72 us
  matrix products: 3.94 us -> 0 us
  Pallas kernels: 10 us -> 11.8 us
    all_to_all x2 -> x1, blocking collectives: 59.4 us -> 24.2 us  [shards(): lax.all_to_all(back, AXES, 0, 0, tiled=True, axis_index_groups=back_group...]
    all_to_all x0 -> x1, starting transfers between devices: none -> 17.3 us  [shards(): lax.all_to_all(packed, 'z', 0, 0, tiled=True, axis_index_groups=[PLANES])]
    all_to_all x0 -> x1, waiting for transfers between devices: none -> 8.72 us  [shards(): lax.all_to_all(packed, 'z', 0, 0, tiled=True, axis_index_groups=[PLANES])]
    pallas_call x0 -> x2, Pallas kernels: none -> 6 us  [the longest x1 3.99 us: cross(): pl.pallas_call(cross_kernel, out_shape=(jax.ShapeDtypeStruct((ROWS, HEAD_...]
    ppermute x1, starting transfers between devices: 9.83 us -> 5.25 us  [shards(): other = lax.ppermute(own, 'c', [(0, 1), (1, 0)])]
    dot_general x2 -> x0, matrix products: 3.94 us -> none  [the longest x1 2.43 us: cross_velocity(): return jnp.einsum('hqd,hpd->qp', out, w, preferred_element_type=jnp.float32)]
    pallas_call x1, Pallas kernels: 6.25 us -> 2.96 us  [attend(): pl.pallas_call(attend_kernel, out_shape=jax.ShapeDtypeStruct((SPREAD * 32...]
    all_to_all x1, blocking collectives: 12.2 us -> 13.7 us  [shards(): lax.all_to_all(kv, 'x', 0, 0, tiled=True).reshape(64, KV_ROWS, HEAD_DIM)]
  transfers between devices with their start and end apart: 1 -> 2, of which waited for: 0 -> 1; matrix products, arithmetic and copies ran while one was open for 6% -> 0% of each run, Pallas kernels for 0% -> 7%
where the time goes in v2:
time: 85.2 us; the launch traced here: 84.9 us
  blocking collectives  37.9 us (44%)
  starting transfers between devices  22.6 us (27%)
  Pallas kernels  11.8 us (14%)
  waiting for transfers between devices  8.72 us (10%)
  local copies, waits for them, and re-layouts  2.34 us (3%)
  between operations  1.39 us (2%)
    all_to_all x1, blocking collectives, shards(): lax.all_to_all(back, AXES, 0, 0, tiled=True, axis_index_groups=back_group...  24.2 us
    all_to_all x1, starting transfers between devices, shards(): lax.all_to_all(packed, 'z', 0, 0, tiled=True, axis_index_groups=[PLANES])  17.3 us
    all_to_all x1, blocking collectives, shards(): lax.all_to_all(kv, 'x', 0, 0, tiled=True).reshape(64, KV_ROWS, HEAD_DIM)  13.7 us
    all_to_all x1, waiting for transfers between devices, shards(): lax.all_to_all(packed, 'z', 0, 0, tiled=True, axis_index_groups=[PLANES])  8.72 us
    ppermute x1, starting transfers between devices, shards(): other = lax.ppermute(own, 'c', [(0, 1), (1, 0)])  5.25 us
    pallas_call x1, Pallas kernels, cross(): pl.pallas_call(cross_kernel, out_shape=(jax.ShapeDtypeStruct((ROWS, HEAD_...  3.99 us
    pallas_call x1, Pallas kernels, attend(): pl.pallas_call(attend_kernel, out_shape=jax.ShapeDtypeStruct((SPREAD * 32...  2.96 us
    unnamed x10, local copies, waits for them, and re-layouts  2.24 us
  transfers between devices with their start and end apart: 2, of which 1 were waited for; matrix products, arithmetic and copies ran while one was open for 0% of the time, Pallas kernels for 7%

profile of v2, /device:TPU:1, one launch (start us, length us, event | category | flops | bytes accessed | tf_op | source)
XLA Modules:
  0.0 84.9 jit_solution(3798945754621673059)
XLA Ops:
  0.6 0.0 copy-start.3
  0.6 0.0 copy-start
  0.7 2.1 %pack.1 = bf16[16,80,128]{2,1,0:T(8,128)(2,1)} custom-call(bf16[10,32,128]{2,1,0:T(8,128)(2,1)} %bitcast.34, bf16[10,32,128]{2,1,0:T(8,128)(2,1)} %bitcast.35, bf16[10,32,128]{2,1,0:T(8,128)(2,1)} %bitcast.36, bf16[10,64,128]{2,1,0:T(8,128)(2,1)} %bitcast.29), custom_call_target="tpu_custom_call" | custom-call | tf_op jit(solution)/shard_map/pack/pallas_call | solution.py:62
  2.8 17.3 %all-to-all-start = ((bf16[16,80,128]{2,1,0:T(8,128)(2,1)}), bf16[16,80,128]{2,1,0:T(8,128)(2,1)S(1)}, u32[]{:S(2)}, u32[]{:S(2)}) async-start(bf16[16,80,128]{2,1,0:T(8,128)(2,1)} %pack.1), calls=%async_computation | async-start | bytes 655360 | tf_op jit(solution)/shard_map/all_to_all | solution.py:237
  20.1 0.0 copy-done.3
  20.1 0.0 copy-done
  20.1 0.0 copy-start.1
  20.1 1.3 %copy-done.1 = bf16[1,512,10,128]{3,1,2,0:T(8,128)(2,1)S(1)} copy-done((bf16[1,512,10,128]{3,1,2,0:T(8,128)(2,1)S(1)}, bf16[1,512,10,128]{3,1,2,0:T(8,128)(2,1)}, u32[]{:S(2)}) %copy-start.1) | copy-done | bytes 1310744
  21.4 0.0 copy-start.2
  21.4 0.9 %copy-done.2 = bf16[10,128,64]{1,2,0:T(8,128)(2,1)S(1)} copy-done((bf16[10,128,64]{1,2,0:T(8,128)(2,1)S(1)}, bf16[10,128,64]{1,2,0:T(8,128)(2,1)}, u32[]{:S(2)}) %copy-start.2) | copy-done | bytes 163864
  22.3 4.0 %cross.1 = (f32[32,128]{1,0:T(8,128)S(1)}, s32[1]{0:T(128)}) custom-call(bf16[10,32,128]{2,1,0:T(8,128)(2,1)S(1)} %bitcast.33, bf16[10,512,128]{2,1,0:T(8,128)(2,1)S(1)} %bitcast.25, bf16[10,512,128]{2,1,0:T(8,128)(2,1)S(1)} %bitcast.26, bf16[10,64,128]{2,1,0:T(8,128)(2,1)S(1)} %bitcast.30), custom_call_target="tpu_custom_call" | custom-call | flops 90000000 | bytes 3200000 | tf_op jit(solution)/shard_map/cross/pallas_call | solution.py:92
  27.0 8.7 %all-to-all-done.q_ref.recv_ref = bf16[16,80,128]{2,1,0:T(8,128)(2,1)S(1)} async-done(((bf16[16,80,128]{2,1,0:T(8,128)(2,1)}), bf16[16,80,128]{2,1,0:T(8,128)(2,1)S(1)}, u32[]{:S(2)}, u32[]{:S(2)}) %all-to-all-start) | async-done | bytes 327712 | tf_op jit(solution)/shard_map/all_to_all | solution.py:237
  35.7 0.1 broadcast_in_dim.11
  35.8 13.7 %all_to_all.21 = bf16[4,16,48,128]{3,2,1,0:T(8,128)(2,1)S(1)} all-to-all(bf16[4,16,48,128]{3,2,1,0:T(8,128)(2,1)S(1)} %broadcast_in_dim.11), channel_id=1, replica_groups=mesh['cfg'=2,'z'=16,'x'=4,'c'=2,'head'=2] {'x'}, dimensions={0} | all-to-all | bytes 1572864 | tf_op jit(solution)/shard_map/all_to_all | solution.py:241
  49.5 5.3 %collective-permute-start = (bf16[64,48,128]{2,1,0:T(8,128)(2,1)S(1)}, bf16[64,48,128]{2,1,0:T(8,128)(2,1)S(1)}, u32[]{:S(2)}, u32[]{:S(2)}) collective-permute-start(bf16[64,48,128]{2,1,0:T(8,128)(2,1)S(1)} %bitcast.27), channel_id=1, source_target_pairs={{0,2},{2,0},{1,3},{3,1},{4,6},{6,4},{5,7},{7,5},{8,10},{10,8},{9,1... | collective-permute-start | bytes 2359304 | tf_op jit(solution)/shard_map/ppermute | solution.py:242
  54.8 0.1 pad_add_fusion.where_ref
  54.9 2.0 %first_half.1 = (f32[512,128]{1,0:T(8,128)S(1)}, f32[512,128]{1,0:T(8,128)S(1)}) custom-call(bf16[16,80,128]{2,1,0:T(8,128)(2,1)S(1)} %all-to-all-done.q_ref.recv_ref, bf16[64,48,128]{2,1,0:T(8,128)(2,1)S(1)} %bitcast.28), custom_call_target="tpu_custom_call" | custom-call | flops 540000000 | bytes 1600000 | tf_op jit(solution)/shard_map/first_half/pallas_call | solution.py:143
  56.9 0.0 copy-start.4
  56.9 0.0 collective-permute-done.other_ref
  56.9 3.0 %attend.1 = bf16[512,128]{1,0:T(8,128)(2,1)S(1)} custom-call(s32[2]{0:T(128)S(1)} %pad_add_fusion.where_ref, bf16[16,80,128]{2,1,0:T(8,128)(2,1)S(1)} %all-to-all-done.q_ref.recv_ref, bf16[64,48,128]{2,1,0:T(8,128)(2,1)S(1)} %collective-permute-done.other_ref, f32[512,128]{1,0:T(8,128)S(1)} %get-tuple-element.7.sum_ref, ...), custom_call_target="tpu_custom_call" | custom-call | tf_op jit(solution)/shard_map/attend/pallas_call | solution.py:188
  59.9 24.2 %all_to_all.22 = bf16[64,8,128]{2,1,0:T(8,128)(2,1)S(1)} all-to-all(bf16[64,8,128]{2,1,0:T(8,128)(2,1)S(1)} %bitcast.32), channel_id=1, replica_groups={{160,161,416,417,176,177,432,433,192,193,448,449,208,209,464,465,224,22..., dimensions={0} | all-to-all | bytes 262144 | tf_op jit(solution)/shard_map/all_to_all | solution.py:247
  84.1 0.0 copy-done.4
  84.1 0.8 finish.1
  (1 shorter events, 0.0 us)
Async XLA Ops:
  0.6 19.5 %copy-start.3 = (bf16[1,32,10,128]{3,1,2,0:T(8,128)(2,1)S(1)}, bf16[1,32,10,128]{3,1,2,0:T(8,128)(2,1)}, u32[]{:S(2)}) copy-start(bf16[1,32,10,128]{3,1,2,0:T(8,128)(2,1)} %param.11) | copy-start | bytes 245764
  0.6 19.5 %copy-start = (bf16[1,512,10,128]{3,1,2,0:T(8,128)(2,1)S(1)}, bf16[1,512,10,128]{3,1,2,0:T(8,128)(2,1)}, u32[]{:S(2)}) copy-start(bf16[1,512,10,128]{3,1,2,0:T(8,128)(2,1)} %param.12) | copy-start | bytes 3932164
  2.8 33.0 %all-to-all-start = ((bf16[16,80,128]{2,1,0:T(8,128)(2,1)}), bf16[16,80,128]{2,1,0:T(8,128)(2,1)S(1)}, u32[]{:S(2)}, u32[]{:S(2)}) async-start(bf16[16,80,128]{2,1,0:T(8,128)(2,1)} %pack.1), calls=%async_computation | async-start | bytes 655360 | tf_op jit(solution)/shard_map/all_to_all | solution.py:237
  20.1 1.3 %copy-start.1 = (bf16[1,512,10,128]{3,1,2,0:T(8,128)(2,1)S(1)}, bf16[1,512,10,128]{3,1,2,0:T(8,128)(2,1)}, u32[]{:S(2)}) copy-start(bf16[1,512,10,128]{3,1,2,0:T(8,128)(2,1)} %param.13) | copy-start | bytes 3932164
  21.4 0.9 %copy-start.2 = (bf16[10,128,64]{1,2,0:T(8,128)(2,1)S(1)}, bf16[10,128,64]{1,2,0:T(8,128)(2,1)}, u32[]{:S(2)}) copy-start(bf16[10,128,64]{1,2,0:T(8,128)(2,1)} %param.14) | copy-start | bytes 491524
  49.5 7.4 %collective-permute-start = (bf16[64,48,128]{2,1,0:T(8,128)(2,1)S(1)}, bf16[64,48,128]{2,1,0:T(8,128)(2,1)S(1)}, u32[]{:S(2)}, u32[]{:S(2)}) collective-permute-start(bf16[64,48,128]{2,1,0:T(8,128)(2,1)S(1)} %bitcast.27), channel_id=1, source_target_pairs={{0,2},{2,0},{1,3},{3,1},{4,6},{6,4},{5,7},{7,5},{8,10},{10,8},{9,1... | collective-permute-start | bytes 2359304 | tf_op jit(solution)/shard_map/ppermute | solution.py:242
  56.9 27.2 %copy-start.4 = (f32[32,32]{1,0:T(8,128)S(1)}, f32[32,32]{1,0:T(8,128)}, u32[]{:S(2)}) copy-start(f32[32,32]{1,0:T(8,128)} %latent_ref.1) | copy-start | bytes 12292

commit v3 on v2

v3 whole, which is shorter than its diff:
```python
import math

import jax
import jax.numpy as jnp
import numpy as np
from jax import lax
from jax.experimental import pallas as pl
from jax.experimental.pallas import tpu as pltpu
from jax.sharding import Mesh, PartitionSpec as P

HEAD_DIM = 128
HEADS_HERE = 10
ROWS = 32
SPREAD = 16
BLOCK = 64
KV_ROWS = 48
FIRST_PLANE = 10
PLANES = [(FIRST_PLANE + i) % SPREAD for i in range(SPREAD)]
AXES = ("cfg", "z", "x", "c", "head")
GUIDANCE = 5.0
STEP = 0.1
EXP2_SCALE = math.log2(math.e) / math.sqrt(HEAD_DIM)
VMEM_LIMIT = 36 * 1024 * 1024


def vmem():
    return pl.BlockSpec(memory_space=pltpu.VMEM)


def params():
    return pltpu.CompilerParams(vmem_limit_bytes=VMEM_LIMIT)


def key_slot(head):
    return 3 * (head // 2) + 2 * (head % 2)


def pack_kernel(q_ref, k_ref, v_ref, w_ref, out_ref, blocks, q_scratch, k_scratch, v_scratch, w_scratch, sems):
    loads = [
        pltpu.make_async_copy(v_ref, v_scratch, sems.at[0]),
        pltpu.make_async_copy(w_ref, w_scratch, sems.at[1]),
        pltpu.make_async_copy(q_ref, q_scratch, sems.at[2]),
        pltpu.make_async_copy(k_ref, k_scratch, sems.at[3]),
    ]
    for load in loads:
        load.start()
    for h in range(HEADS_HERE):
        blocks[key_slot(h), KV_ROWS:BLOCK, :] = jnp.zeros((BLOCK - KV_ROWS, HEAD_DIM), jnp.bfloat16)
    blocks[SPREAD - 1] = jnp.zeros((BLOCK, HEAD_DIM), jnp.bfloat16)
    for load in loads:
        load.wait()
    for h in range(HEADS_HERE):
        blocks[key_slot(h), 0:32, :] = k_scratch[h]
        blocks[3 * (h // 2) + 1, 32 * (h % 2):32 * (h % 2) + 32, :] = q_scratch[h]
        projected = lax.dot_general(
            v_scratch[h], w_scratch[h], (((1,), (1,)), ((), ())), preferred_element_type=jnp.float32
        )
        packed = jnp.concatenate([projected[0:16], projected[16:32]], axis=1)
        blocks[key_slot(h), 32:KV_ROWS, :] = packed.astype(jnp.bfloat16)
    store = pltpu.make_async_copy(blocks, out_ref, sems.at[4])
    store.start()
    store.wait()


def pack(q, k, v, w):
    anywhere = pl.BlockSpec(memory_space=pl.ANY)
    return pl.pallas_call(
        pack_kernel,
        out_shape=jax.ShapeDtypeStruct((SPREAD, BLOCK, HEAD_DIM), jnp.bfloat16),
        in_specs=[anywhere] * 4,
        out_specs=anywhere,
        scratch_shapes=[
            pltpu.VMEM((SPREAD, BLOCK, HEAD_DIM), jnp.bfloat16),
            pltpu.VMEM((HEADS_HERE, ROWS, HEAD_DIM), jnp.bfloat16),
            pltpu.VMEM((HEADS_HERE, ROWS, HEAD_DIM), jnp.bfloat16),
            pltpu.VMEM((HEADS_HERE, ROWS, HEAD_DIM), jnp.bfloat16),
            pltpu.VMEM((HEADS_HERE, 64, HEAD_DIM), jnp.bfloat16),
            pltpu.SemaphoreType.DMA((5,)),
        ],
        compiler_params=pltpu.CompilerParams(vmem_limit_bytes=60 * 1024 * 1024),
        name="pack",
    )(q, k, v, w)


def cross_kernel(q_ref, k_ref, v_ref, w_ref, sum_ref, zero_ref):
    total = jnp.zeros((ROWS, 64), jnp.float32)
    for h in range(HEADS_HERE):
        s = scores(q_ref[h], k_ref[h])
        top = jnp.max(s, axis=1, keepdims=True) * EXP2_SCALE
        p = jnp.exp2(s * EXP2_SCALE - top)
        o = jnp.dot(p.astype(jnp.bfloat16), v_ref[h], preferred_element_type=jnp.float32)
        o = o / jnp.sum(p, axis=1, keepdims=True)
        total = total + scores(o.astype(jnp.bfloat16), w_ref[h])
    columns = jnp.concatenate([total, jnp.zeros((ROWS, 64), jnp.float32)], axis=1).T
    columns = jnp.concatenate([columns, jnp.zeros((HEAD_DIM, HEAD_DIM - ROWS), jnp.float32)], axis=1)
    lane_group = lax.broadcasted_iota(jnp.int32, (8, HEAD_DIM), 1) // 32
    for half in range(2):
        block = columns[32 * half:32 * half + 8]
        for g in range(1, 4):
            piece = pltpu.roll(columns[32 * half + 8 * g:32 * half + 8 * g + 8], 32 * g, 1)
            block = jnp.where(lane_group == g, piece, block)
        sum_ref[16 * half:16 * half + 8, :] = block
        sum_ref[16 * half + 8:16 * half + 16, :] = block
    zero_ref[0] = 0


def cross(q, k, v, w):
    return pl.pallas_call(
        cross_kernel,
        out_shape=(
            jax.ShapeDtypeStruct((ROWS, HEAD_DIM), jnp.float32),
            jax.ShapeDtypeStruct((1,), jnp.int32),
        ),
        in_specs=[vmem()] * 4,
        out_specs=(vmem(), pl.BlockSpec(memory_space=pltpu.SMEM)),
        compiler_params=params(),
        cost_estimate=pl.CostEstimate(flops=90_000_000, bytes_accessed=3_200_000, transcendentals=170_000),
        name="cross",
    )(q, k, v, w)


def scores(q, keys):
    return lax.dot_general(q, keys, (((1,), (1,)), ((), ())), preferred_element_type=jnp.float32)


def load_keys(ref):
    even, odd = ref[:, 0:16, :], ref[:, 16:32, :]
    return [part.reshape(1024, HEAD_DIM) for part in (even, odd)], ref[:, 32:48, :].reshape(1024, HEAD_DIM)


def half_attention(q, keys, value, found_top=None):
    found = [scores(part, q) for part in keys]
    top = jnp.max(jnp.maximum(found[0], found[1]), axis=0, keepdims=True) * EXP2_SCALE
    if found_top is not None:
        top = jnp.maximum(top, found_top)
    weights = [jnp.exp2(s * EXP2_SCALE - top) for s in found]
    weight_sum = jnp.sum(weights[0] + weights[1], axis=0, keepdims=True)
    even, odd = [
        lax.dot_general(
            value, p.astype(jnp.bfloat16), (((0,), (0,)), ((), ())), preferred_element_type=jnp.float32
        )
        for p in weights
    ]
    return even[0:64] + odd[64:128], weight_sum, top


QUERIES = SPREAD * ROWS


def first_kernel(q_ref, own_ref, sum_ref, stat_ref):
    keys, value = load_keys(own_ref)
    summed, weight_sum, top = half_attention(q_ref[...].reshape(QUERIES, HEAD_DIM), keys, value)
    sum_ref[...] = summed
    stat_ref[0:8, :] = jnp.broadcast_to(weight_sum, (8, QUERIES))
    stat_ref[8:16, :] = jnp.broadcast_to(top, (8, QUERIES))


def first_half(q, own):
    return pl.pallas_call(
        first_kernel,
        out_shape=(
            jax.ShapeDtypeStruct((64, QUERIES), jnp.float32),
            jax.ShapeDtypeStruct((16, QUERIES), jnp.float32),
        ),
        in_specs=[vmem()] * 2,
        out_specs=(vmem(), vmem()),
        compiler_params=params(),
        cost_estimate=pl.CostEstimate(flops=540_000_000, bytes_accessed=1_600_000, transcendentals=1_000_000),
        name="first_half",
    )(q, own)


def attend_kernel(where_ref, q_ref, other_ref, sum_ref, stat_ref, cross_ref, out_ref, blocks):
    slot = where_ref[0]
    branch = where_ref[1]
    active = (slot < SPREAD - 1) & (where_ref[2] != 1)
    keys, value = load_keys(other_ref)
    first_sum, first_top = stat_ref[0:1, :], stat_ref[8:9, :]
    summed, weight_sum, top = half_attention(q_ref[...].reshape(QUERIES, HEAD_DIM), keys, value, first_top)
    scale = jnp.exp2(first_top - top)
    factor = jnp.where(branch == 0, GUIDANCE, 1.0 - GUIDANCE)
    total = (summed + sum_ref[...] * scale) * (factor / (weight_sum + first_sum * scale))
    total = jnp.where(active, total, 0.0)
    lane_group = lax.broadcasted_iota(jnp.int32, (32, HEAD_DIM), 1) // 32
    halves = []
    for half in range(2):
        groups = []
        for g in range(4):
            rows = total[32 * half + 8 * g:32 * half + 8 * g + 8]
            groups.append(jnp.concatenate([rows[:, 128 * t:128 * t + 128] for t in range(4)], axis=0))
        places = []
        for i in range(4):
            block = groups[i]
            for g in range(4):
                if g != i:
                    block = jnp.where(lane_group == g, pltpu.roll(groups[g], 32 * ((g - i) % 4), 1), block)
            places.append(block.reshape(4, 1, 1, 8, HEAD_DIM))
        halves.append(jnp.concatenate(places, axis=1))
    blocks[...] = jnp.concatenate([halves[0], halves[0], halves[1], halves[1]], axis=2).reshape(QUERIES, HEAD_DIM)
    mine = pl.ds(pl.multiple_of(slot * 32, 32), 32)
    blocks[mine, :] = blocks[mine, :] + cross_ref[...] * factor
    out_ref[...] = blocks[...].astype(jnp.bfloat16)


def attend(where, q, other, summed, stat, cross):
    return pl.pallas_call(
        attend_kernel,
        out_shape=jax.ShapeDtypeStruct((QUERIES, HEAD_DIM), jnp.bfloat16),
        in_specs=[pl.BlockSpec(memory_space=pltpu.SMEM)] + [vmem()] * 5,
        out_specs=vmem(),
        scratch_shapes=[pltpu.VMEM((QUERIES, HEAD_DIM), jnp.float32)],
        compiler_params=params(),
        name="attend",
    )(where, q, other, summed, stat, cross)


def finish_kernel(parts_ref, latent_ref, guided_ref, next_ref):
    parts = parts_ref[...].astype(jnp.float32).reshape(64, 8, HEAD_DIM)
    summed = jnp.sum(parts, axis=0)
    columns = jnp.concatenate([summed] + [pltpu.roll(summed, HEAD_DIM - 32 * g, 1) for g in range(1, 4)], axis=0)
    guided = columns.T[0:32]
    guided_ref[...] = guided
    next_ref[...] = latent_ref[...] + STEP * guided


def finish(parts, latent):
    shape = jax.ShapeDtypeStruct(latent.shape, jnp.float32)
    return pl.pallas_call(
        finish_kernel,
        out_shape=(shape, shape),
        in_specs=[vmem()] * 2,
        out_specs=(vmem(), vmem()),
        compiler_params=params(),
        name="finish",
    )(parts, latent)


def back_groups():
    index = np.arange(512).reshape(2, SPREAD, 4, 2, 2)
    return [
        [int(index[f, z, x, c, h]) for z in PLANES for f in range(2) for h in range(2)]
        for x in range(4)
        for c in range(2)
    ]


def heads_first(block):
    return jnp.transpose(block, (1, 0, 2))


def shards(queries, self_keys, self_values, cross_queries, text_keys, text_values, out_weight, latent):
    w = jnp.transpose(out_weight, (0, 2, 1))
    packed = pack(heads_first(queries[0]), heads_first(self_keys[0]), heads_first(self_values[0]), w)
    recv = lax.all_to_all(packed, "z", 0, 0, tiled=True, axis_index_groups=[PLANES])
    crossed, zero = cross(heads_first(cross_queries[0]), heads_first(text_keys[0]), heads_first(text_values[0]), w)
    kv = jnp.where(zero[0] == 0, recv[:, 0:KV_ROWS, :], jnp.zeros((), recv.dtype))
    kv = jnp.broadcast_to(kv[None], (4, SPREAD, KV_ROWS, HEAD_DIM))
    own = lax.all_to_all(kv, "x", 0, 0, tiled=True).reshape(64, KV_ROWS, HEAD_DIM)
    left = lax.ppermute(recv[:, 0:32, :], "z", [(PLANES[3 * i + 1], PLANES[3 * i]) for i in range(5)])
    right = lax.ppermute(recv[:, 32:64, :], "z", [(PLANES[3 * i + 1], PLANES[3 * i + 2]) for i in range(5)])
    slot = lax.rem(lax.axis_index("z") + (SPREAD - FIRST_PLANE), SPREAD)
    q = jnp.where(lax.rem(slot, 3) == 0, left, right)
    ready = q[0:1, 0:1, :] == q[0:1, 0:1, :]
    other = lax.ppermute(jnp.where(ready, own, jnp.zeros((), own.dtype)), "c", [(0, 1), (1, 0)])
    where = jnp.stack([slot, lax.axis_index("cfg"), lax.rem(slot, 3)]).astype(jnp.int32)
    summed, stat = first_half(q, own)
    back = attend(where, q, other, summed, stat, crossed)
    parts = lax.all_to_all(back, AXES, 0, 0, tiled=True, axis_index_groups=back_groups())
    return finish(parts, latent)


def solution(mesh):
    split = Mesh(mesh.devices.reshape(2, SPREAD, 4, 2, 2), ("cfg", "z", "x", "c", "head"))
    seq = ("z", "x", "c")
    tokens = P("cfg", seq, "head", None)
    text = P("cfg", None, "head", None)
    placed = (tokens, tokens, tokens, tokens, text, text, P("head", None, None), P(seq, "cfg"))
    return jax.shard_map(
        shards,
        mesh=split,
        in_specs=placed,
        out_specs=(P(seq, "cfg"), P(seq, "cfg")),
        check_vma=False,
    )
```

time: 85.2 us -> 82.4 us (0.967)
  blocking collectives: 37.9 us -> 23.6 us
  starting transfers between devices: 22.6 us -> 28.9 us
  waiting for transfers between devices: 8.72 us -> 12.3 us
  local copies, waits for them, and re-layouts: 2.34 us -> 4.55 us
  Pallas kernels: 11.8 us -> 10.8 us
    all_to_all x1 -> x0, blocking collectives: 13.7 us -> none  [shards(): lax.all_to_all(kv, 'x', 0, 0, tiled=True).reshape(64, KV_ROWS, HEAD_DIM)]
    ppermute x1 -> x3, waiting for transfers between devices: 0.01 us -> 6.15 us  [the longest x1 6.04 us: shards(): lax.ppermute(recv[:, 0:32, :], 'z', [(PLANES[3 * i + 1], PLANES[3 * i]) f...]
    all_to_all x0 -> x1, starting transfers between devices: none -> 4.01 us  [shards(): lax.all_to_all(kv, 'x', 0, 0, tiled=True).reshape(64, KV_ROWS, HEAD_DIM)]
    all_to_all x1, waiting for transfers between devices: 8.72 us -> 4.72 us  [shards(): lax.all_to_all(packed, 'z', 0, 0, tiled=True, axis_index_groups=[PLANES])]
    ppermute x1 -> x3, starting transfers between devices: 5.25 us -> 7.59 us  [the longest x1 5.63 us: shards(): lax.ppermute(jnp.where(ready, own, jnp.zeros((), own.dtype)), 'c', [(0, 1...]
    all_to_all x0 -> x1, waiting for transfers between devices: none -> 1.42 us  [shards(): lax.all_to_all(kv, 'x', 0, 0, tiled=True).reshape(64, KV_ROWS, HEAD_DIM)]
    unnamed x10, local copies, waits for them, and re-layouts: 2.24 us -> 3.52 us
    pallas_call x2, Pallas kernels: 4.97 us -> 4.05 us  [the longest x1 2.35 us: attend(): pl.pallas_call(attend_kernel, out_shape=jax.ShapeDtypeStruct((QUERIES, HE...]
  transfers between devices with their start and end apart: 2 -> 5, of which waited for: 1 -> 4; matrix products, arithmetic and copies ran while one was open for 0% -> 0% of each run, Pallas kernels for 7% -> 7%
where the time goes in v3:
time: 82.4 us; the launch traced here: 81.9 us
  starting transfers between devices  28.9 us (35%)
  blocking collectives  23.6 us (29%)
  waiting for transfers between devices  12.3 us (15%)
  Pallas kernels  10.8 us (13%)
  local copies, waits for them, and re-layouts  4.55 us (6%)
  between operations  1.41 us (2%)
    all_to_all x1, blocking collectives, shards(): lax.all_to_all(back, AXES, 0, 0, tiled=True, axis_index_groups=back_group...  23.6 us
    all_to_all x1, starting transfers between devices, shards(): lax.all_to_all(packed, 'z', 0, 0, tiled=True, axis_index_groups=[PLANES])  17.3 us
    ppermute x1, waiting for transfers between devices, shards(): lax.ppermute(recv[:, 0:32, :], 'z', [(PLANES[3 * i + 1], PLANES[3 * i]) f...  6.04 us
    ppermute x1, starting transfers between devices, shards(): lax.ppermute(jnp.where(ready, own, jnp.zeros((), own.dtype)), 'c', [(0, 1...  5.63 us
    all_to_all x1, waiting for transfers between devices, shards(): lax.all_to_all(packed, 'z', 0, 0, tiled=True, axis_index_groups=[PLANES])  4.72 us
    all_to_all x1, starting transfers between devices, shards(): lax.all_to_all(kv, 'x', 0, 0, tiled=True).reshape(64, KV_ROWS, HEAD_DIM)  4.01 us
    pallas_call x1, Pallas kernels, cross(): pl.pallas_call(cross_kernel, out_shape=(jax.ShapeDtypeStruct((ROWS, HEAD_...  3.88 us
    unnamed x10, local copies, waits for them, and re-layouts  3.52 us
  transfers between devices with their start and end apart: 5, of which 4 were waited for; matrix products, arithmetic and copies ran while one was open for 0% of the time, Pallas kernels for 7%

profile of v3, /device:TPU:1, one launch (start us, length us, event | category | flops | bytes accessed | tf_op | source)
XLA Modules:
  0.0 81.9 jit_solution(702720672127183773)
XLA Ops:
  0.6 0.0 copy-start.2
  0.6 2.1 %pack.1 = bf16[16,64,128]{2,1,0:T(8,128)(2,1)} custom-call(bf16[10,32,128]{2,1,0:T(8,128)(2,1)} %bitcast.37, bf16[10,32,128]{2,1,0:T(8,128)(2,1)} %bitcast.38, bf16[10,32,128]{2,1,0:T(8,128)(2,1)} %bitcast.39, bf16[10,64,128]{2,1,0:T(8,128)(2,1)} %bitcast.32), custom_call_target="tpu_custom_call" | custom-call | tf_op jit(solution)/shard_map/pack/pallas_call | solution.py:67
  2.7 17.3 %all-to-all-start = ((bf16[16,64,128]{2,1,0:T(8,128)(2,1)}), bf16[16,64,128]{2,1,0:T(8,128)(2,1)S(1)}, u32[]{:S(2)}, u32[]{:S(2)}) async-start(bf16[16,64,128]{2,1,0:T(8,128)(2,1)} %pack.1), calls=%async_computation | async-start | bytes 524288 | tf_op jit(solution)/shard_map/all_to_all | solution.py:254
  20.1 0.0 copy-done.2
  20.1 0.0 copy-start
  20.1 1.3 %copy-done = bf16[1,512,10,128]{3,1,2,0:T(8,128)(2,1)S(1)} copy-done((bf16[1,512,10,128]{3,1,2,0:T(8,128)(2,1)S(1)}, bf16[1,512,10,128]{3,1,2,0:T(8,128)(2,1)}, u32[]{:S(2)}) %copy-start) | copy-done | bytes 1310744
  21.4 0.0 copy-start.1
  21.4 1.3 %copy-done.1 = bf16[1,512,10,128]{3,1,2,0:T(8,128)(2,1)S(1)} copy-done((bf16[1,512,10,128]{3,1,2,0:T(8,128)(2,1)S(1)}, bf16[1,512,10,128]{3,1,2,0:T(8,128)(2,1)}, u32[]{:S(2)}) %copy-start.1) | copy-done | bytes 1310744
  22.7 0.0 copy-start.3
  22.7 0.9 %copy-done.3 = bf16[1,32,10,128]{3,1,2,0:T(8,128)(2,1)S(1)} copy-done((bf16[1,32,10,128]{3,1,2,0:T(8,128)(2,1)S(1)}, bf16[1,32,10,128]{3,1,2,0:T(8,128)(2,1)}, u32[]{:S(2)}) %copy-start.3) | copy-done | bytes 81944
  23.6 3.9 %cross.1 = (f32[32,128]{1,0:T(8,128)S(1)}, s32[1]{0:T(128)}) custom-call(bf16[10,32,128]{2,1,0:T(8,128)(2,1)S(1)} %bitcast.36, bf16[10,512,128]{2,1,0:T(8,128)(2,1)S(1)} %bitcast.30, bf16[10,512,128]{2,1,0:T(8,128)(2,1)S(1)} %bitcast.31, bf16[10,64,128]{2,1,0:T(8,128)(2,1)S(1)} %bitcast.33), custom_call_target="tpu_custom_call" | custom-call | flops 90000000 | bytes 3200000 | tf_op jit(solution)/shard_map/cross/pallas_call | solution.py:108
  28.1 4.7 %all-to-all-done = bf16[16,64,128]{2,1,0:T(8,128)(2,1)S(1)} async-done(((bf16[16,64,128]{2,1,0:T(8,128)(2,1)}), bf16[16,64,128]{2,1,0:T(8,128)(2,1)S(1)}, u32[]{:S(2)}, u32[]{:S(2)}) %all-to-all-start) | async-done | bytes 262176 | tf_op jit(solution)/shard_map/all_to_all | solution.py:254
  32.9 1.0 %broadcast_in_dim.27 = bf16[4,16,48,128]{3,2,1,0:T(8,128)(2,1)} broadcast(bf16[16,48,128]{2,1,0:T(8,128)(2,1)S(1)} %slice_select_fusion), dimensions={1,2,3} | broadcast | bytes 983040 | tf_op jit(solution)/shard_map/broadcast_in_dim | solution.py:257
  33.9 4.0 %all-to-all-start.1 = ((bf16[4,16,48,128]{3,2,1,0:T(8,128)(2,1)}), bf16[4,16,48,128]{3,2,1,0:T(8,128)(2,1)S(1)}, u32[]{:S(2)}, u32[]{:S(2)}) async-start(bf16[4,16,48,128]{3,2,1,0:T(8,128)(2,1)} %broadcast_in_dim.27), calls=%async_computation.1 | async-start | bytes 1572864 | tf_op jit(solution)/shard_map/all_to_all | solution.py:258
  37.9 0.7 collective-permute-start.1
  38.6 1.3 %collective-permute-start = (bf16[16,32,128]{2,1,0:T(8,128)(2,1)S(1)}, bf16[16,32,128]{2,1,0:T(8,128)(2,1)S(1)}, u32[]{:S(2)}, u32[]{:S(2)}) collective-permute-start(bf16[16,32,128]{2,1,0:T(8,128)(2,1)S(1)} %get-tuple-element.11), channel_id=1, source_target_pairs={{176,160},{224,208},{16,0},{64,48},{112,96},{177,161},{225,209},{1... | collective-permute-start | bytes 393224 | tf_op jit(solution)/shard_map/ppermute | solution.py:259
  39.9 0.0 collective-permute-done.1
  39.9 6.0 %collective-permute-done = bf16[16,32,128]{2,1,0:T(8,128)(2,1)S(1)} collective-permute-done((bf16[16,32,128]{2,1,0:T(8,128)(2,1)S(1)}, bf16[16,32,128]{2,1,0:T(8,128)(2,1)S(1)}, u32[]{:S(2)}, u32[]{:S(2)}) %collective-permute-start) | collective-permute-done | bytes 131104 | tf_op jit(solution)/shard_map/ppermute | solution.py:259
  46.0 1.4 %all-to-all-done.1 = bf16[4,16,48,128]{3,2,1,0:T(8,128)(2,1)S(1)} async-done(((bf16[4,16,48,128]{3,2,1,0:T(8,128)(2,1)}), bf16[4,16,48,128]{3,2,1,0:T(8,128)(2,1)S(1)}, u32[]{:S(2)}, u32[]{:S(2)}) %all-to-all-start.1) | async-done | bytes 786464 | tf_op jit(solution)/shard_map/all_to_all | solution.py:258
  47.4 0.1 broadcast_select_fusion
  47.5 5.6 %collective-permute-start.2 = (bf16[64,48,128]{2,1,0:T(8,128)(2,1)S(1)}, bf16[64,48,128]{2,1,0:T(8,128)(2,1)S(1)}, u32[]{:S(2)}, u32[]{:S(2)}) collective-permute-start(bf16[64,48,128]{2,1,0:T(8,128)(2,1)S(1)} %broadcast_select_fusion), channel_id=1, source_target_pairs={{0,2},{2,0},{1,3},{3,1},{4,6},{6,4},{5,7},{7,5},{8,10},{10,8},{9,1... | collective-permute-start | bytes 2359304 | tf_op jit(solution)/shard_map/ppermute | solution.py:264
  53.2 0.1 pad_add_fusion.where_ref
  53.3 0.0 copy-start.4
  53.3 1.7 %first_half.1 = (f32[64,512]{1,0:T(8,128)S(1)}, f32[16,512]{1,0:T(8,128)S(1)}) custom-call(bf16[16,32,128]{2,1,0:T(8,128)(2,1)S(1)} %broadcast_select_fusion.1.q_ref, bf16[64,48,128]{2,1,0:T(8,128)(2,1)S(1)} %bitcast.29), custom_call_target="tpu_custom_call" | custom-call | flops 540000000 | bytes 1600000 | tf_op jit(solution)/shard_map/first_half/pallas_call | solution.py:159
  55.0 0.1 collective-permute-done.2.other_ref
  55.1 2.4 %attend.1 = bf16[512,128]{1,0:T(8,128)(2,1)S(1)} custom-call(s32[3]{0:T(128)S(1)} %pad_add_fusion.where_ref, bf16[16,32,128]{2,1,0:T(8,128)(2,1)S(1)} %broadcast_select_fusion.1.q_ref, bf16[64,48,128]{2,1,0:T(8,128)(2,1)S(1)} %collective-permute-done.2.other_ref, f32[64,512]{1,0:T(8,128)S(1)} %get-tuple-element.7.sum_ref, ...), custom_call_target="tpu_custom_call" | custom-call | tf_op jit(solution)/shard_map/attend/pallas_call | solution.py:206
  57.4 23.6 %all_to_all.21 = bf16[64,8,128]{2,1,0:T(8,128)(2,1)S(1)} all-to-all(bf16[64,8,128]{2,1,0:T(8,128)(2,1)S(1)} %bitcast.34), channel_id=1, replica_groups={{160,161,416,417,176,177,432,433,192,193,448,449,208,209,464,465,224,22..., dimensions={0} | all-to-all | bytes 262144 | tf_op jit(solution)/shard_map/all_to_all | solution.py:268
  81.1 0.0 copy-done.4
  81.1 0.8 finish.1
  (4 shorter events, 0.1 us)
Async XLA Ops:
  0.6 19.5 %copy-start.2 = (bf16[10,128,64]{1,2,0:T(8,128)(2,1)S(1)}, bf16[10,128,64]{1,2,0:T(8,128)(2,1)}, u32[]{:S(2)}) copy-start(bf16[10,128,64]{1,2,0:T(8,128)(2,1)} %param.14) | copy-start | bytes 491524
  2.7 30.1 %all-to-all-start = ((bf16[16,64,128]{2,1,0:T(8,128)(2,1)}), bf16[16,64,128]{2,1,0:T(8,128)(2,1)S(1)}, u32[]{:S(2)}, u32[]{:S(2)}) async-start(bf16[16,64,128]{2,1,0:T(8,128)(2,1)} %pack.1), calls=%async_computation | async-start | bytes 524288 | tf_op jit(solution)/shard_map/all_to_all | solution.py:254
  20.1 1.3 %copy-start = (bf16[1,512,10,128]{3,1,2,0:T(8,128)(2,1)S(1)}, bf16[1,512,10,128]{3,1,2,0:T(8,128)(2,1)}, u32[]{:S(2)}) copy-start(bf16[1,512,10,128]{3,1,2,0:T(8,128)(2,1)} %param.12) | copy-start | bytes 3932164
  21.4 1.3 %copy-start.1 = (bf16[1,512,10,128]{3,1,2,0:T(8,128)(2,1)S(1)}, bf16[1,512,10,128]{3,1,2,0:T(8,128)(2,1)}, u32[]{:S(2)}) copy-start(bf16[1,512,10,128]{3,1,2,0:T(8,128)(2,1)} %param.13) | copy-start | bytes 3932164
  22.7 0.9 %copy-start.3 = (bf16[1,32,10,128]{3,1,2,0:T(8,128)(2,1)S(1)}, bf16[1,32,10,128]{3,1,2,0:T(8,128)(2,1)}, u32[]{:S(2)}) copy-start(bf16[1,32,10,128]{3,1,2,0:T(8,128)(2,1)} %param.11) | copy-start | bytes 245764
  33.9 13.5 %all-to-all-start.1 = ((bf16[4,16,48,128]{3,2,1,0:T(8,128)(2,1)}), bf16[4,16,48,128]{3,2,1,0:T(8,128)(2,1)S(1)}, u32[]{:S(2)}, u32[]{:S(2)}) async-start(bf16[4,16,48,128]{3,2,1,0:T(8,128)(2,1)} %broadcast_in_dim.27), calls=%async_computation.1 | async-start | bytes 1572864 | tf_op jit(solution)/shard_map/all_to_all | solution.py:258
  37.9 2.0 %collective-permute-start.1 = (bf16[16,32,128]{2,1,0:T(8,128)(2,1)S(1)}, bf16[16,32,128]{2,1,0:T(8,128)(2,1)S(1)}, u32[]{:S(2)}, u32[]{:S(2)}) collective-permute-start(bf16[16,32,128]{2,1,0:T(8,128)(2,1)S(1)} %get-tuple-element.10), channel_id=1, source_target_pairs={{176,192},{224,240},{16,32},{64,80},{112,128},{177,193},{225,241},... | collective-permute-start | bytes 393224 | tf_op jit(solution)/shard_map/ppermute | solution.py:260
  38.6 7.4 %collective-permute-start = (bf16[16,32,128]{2,1,0:T(8,128)(2,1)S(1)}, bf16[16,32,128]{2,1,0:T(8,128)(2,1)S(1)}, u32[]{:S(2)}, u32[]{:S(2)}) collective-permute-start(bf16[16,32,128]{2,1,0:T(8,128)(2,1)S(1)} %get-tuple-element.11), channel_id=1, source_target_pairs={{176,160},{224,208},{16,0},{64,48},{112,96},{177,161},{225,209},{1... | collective-permute-start | bytes 393224 | tf_op jit(solution)/shard_map/ppermute | solution.py:259
  47.5 7.5 %collective-permute-start.2 = (bf16[64,48,128]{2,1,0:T(8,128)(2,1)S(1)}, bf16[64,48,128]{2,1,0:T(8,128)(2,1)S(1)}, u32[]{:S(2)}, u32[]{:S(2)}) collective-permute-start(bf16[64,48,128]{2,1,0:T(8,128)(2,1)S(1)} %broadcast_select_fusion), channel_id=1, source_target_pairs={{0,2},{2,0},{1,3},{3,1},{4,6},{6,4},{5,7},{7,5},{8,10},{10,8},{9,1... | collective-permute-start | bytes 2359304 | tf_op jit(solution)/shard_map/ppermute | solution.py:264
  53.3 27.8 %copy-start.4 = (f32[32,32]{1,0:T(8,128)S(1)}, f32[32,32]{1,0:T(8,128)}, u32[]{:S(2)}) copy-start(f32[32,32]{1,0:T(8,128)} %latent_ref.1) | copy-start | bytes 12292

commit v4 on v3

--- a/solution.py
+++ b/solution.py
@@ -12,10 +12,13 @@
 HEADS_HERE = 10
 ROWS = 32
 SPREAD = 16
-BLOCK = 64
+BLOCK = 56
 KV_ROWS = 48
 FIRST_PLANE = 10
+BACK_PLANE = 8
 PLANES = [(FIRST_PLANE + i) % SPREAD for i in range(SPREAD)]
+BACK_PLANES = [(BACK_PLANE + i) % SPREAD for i in range(SPREAD)]
+TURN = 32 * ((BACK_PLANE - FIRST_PLANE) % SPREAD)
 AXES = ("cfg", "z", "x", "c", "head")
 GUIDANCE = 5.0
 STEP = 0.1
@@ -44,14 +47,15 @@
     ]
     for load in loads:
         load.start()
-    for h in range(HEADS_HERE):
-        blocks[key_slot(h), KV_ROWS:BLOCK, :] = jnp.zeros((BLOCK - KV_ROWS, HEAD_DIM), jnp.bfloat16)
+    for pair in range(HEADS_HERE // 2):
+        blocks[3 * pair + 1, 48:BLOCK, :] = jnp.zeros((BLOCK - 48, HEAD_DIM), jnp.bfloat16)
     blocks[SPREAD - 1] = jnp.zeros((BLOCK, HEAD_DIM), jnp.bfloat16)
     for load in loads:
         load.wait()
     for h in range(HEADS_HERE):
         blocks[key_slot(h), 0:32, :] = k_scratch[h]
-        blocks[3 * (h // 2) + 1, 32 * (h % 2):32 * (h % 2) + 32, :] = q_scratch[h]
+        blocks[key_slot(h), KV_ROWS:BLOCK, :] = q_scratch[h, 0:8]
+        blocks[3 * (h // 2) + 1, 24 * (h % 2):24 * (h % 2) + 24, :] = q_scratch[h, 8:32]
         projected = lax.dot_general(
             v_scratch[h], w_scratch[h], (((1,), (1,)), ((), ())), preferred_element_type=jnp.float32
         )
@@ -128,11 +132,9 @@
     return [part.reshape(1024, HEAD_DIM) for part in (even, odd)], ref[:, 32:48, :].reshape(1024, HEAD_DIM)
 
 
-def half_attention(q, keys, value, found_top=None):
+def half_attention(q, keys, value):
     found = [scores(part, q) for part in keys]
     top = jnp.max(jnp.maximum(found[0], found[1]), axis=0, keepdims=True) * EXP2_SCALE
-    if found_top is not None:
-        top = jnp.maximum(top, found_top)
     weights = [jnp.exp2(s * EXP2_SCALE - top) for s in found]
     weight_sum = jnp.sum(weights[0] + weights[1], axis=0, keepdims=True)
     even, odd = [
@@ -147,39 +149,46 @@
 QUERIES = SPREAD * ROWS
 
 
-def first_kernel(q_ref, own_ref, sum_ref, stat_ref):
+STATE = 80
+
+
+def partial_kernel(where_ref, q_ref, own_ref, keep_ref, give_ref):
     keys, value = load_keys(own_ref)
-    summed, weight_sum, top = half_attention(q_ref[...].reshape(QUERIES, HEAD_DIM), keys, value)
-    sum_ref[...] = summed
-    stat_ref[0:8, :] = jnp.broadcast_to(weight_sum, (8, QUERIES))
-    stat_ref[8:16, :] = jnp.broadcast_to(top, (8, QUERIES))
-
-
-def first_half(q, own):
-    return pl.pallas_call(
-        first_kernel,
-        out_shape=(
-            jax.ShapeDtypeStruct((64, QUERIES), jnp.float32),
-            jax.ShapeDtypeStruct((16, QUERIES), jnp.float32),
-        ),
-        in_specs=[vmem()] * 2,
+    states = []
+    for core in range(2):
+        summed, weight_sum, top = half_attention(q_ref[core].reshape(QUERIES, HEAD_DIM), keys, value)
+        stats = [jnp.broadcast_to(x, (8, QUERIES)) for x in (weight_sum, top)]
+        states.append(jnp.concatenate([summed] + stats, axis=0))
+    first = where_ref[4] == 0
+    keep_ref[...] = jnp.where(first, states[0], states[1])
+    give_ref[...] = jnp.where(first, states[1], states[0])
+
+
+def partial_attention(where, q, own):
+    shape = jax.ShapeDtypeStruct((STATE, QUERIES), jnp.float32)
+    return pl.pallas_call(
+        partial_kernel,
+        out_shape=(shape, shape),
+        in_specs=[pl.BlockSpec(memory_space=pltpu.SMEM)] + [vmem()] * 2,
         out_specs=(vmem(), vmem()),
         compiler_params=params(),
-        cost_estimate=pl.CostEstimate(flops=540_000_000, bytes_accessed=1_600_000, transcendentals=1_000_000),
-        name="first_half",
-    )(q, own)
-
-
-def attend_kernel(where_ref, q_ref, other_ref, sum_ref, stat_ref, cross_ref, out_ref, blocks):
+        cost_estimate=pl.CostEstimate(flops=1_080_000_000, bytes_accessed=1_600_000, transcendentals=2_000_000),
+        name="partial_attention",
+    )(where, q, own)
+
+
+def join_kernel(where_ref, keep_ref, given_ref, cross_ref, out_ref, blocks):
     slot = where_ref[0]
     branch = where_ref[1]
     active = (slot < SPREAD - 1) & (where_ref[2] != 1)
-    keys, value = load_keys(other_ref)
-    first_sum, first_top = stat_ref[0:1, :], stat_ref[8:9, :]
-    summed, weight_sum, top = half_attention(q_ref[...].reshape(QUERIES, HEAD_DIM), keys, value, first_top)
-    scale = jnp.exp2(first_top - top)
+    given = given_ref[1 - where_ref[4]]
+    kept = keep_ref[...]
+    top = jnp.maximum(kept[72:73], given[72:73])
+    scales = [jnp.exp2(state[72:73] - top) for state in (kept, given)]
+    weight_sum = kept[64:65] * scales[0] + given[64:65] * scales[1]
     factor = jnp.where(branch == 0, GUIDANCE, 1.0 - GUIDANCE)
-    total = (summed + sum_ref[...] * scale) * (factor / (weight_sum + first_sum * scale))
+    share = factor / weight_sum
+    total = kept[0:64] * (scales[0] * share) + given[0:64] * (scales[1] * share)
     total = jnp.where(active, total, 0.0)
     lane_group = lax.broadcasted_iota(jnp.int32, (32, HEAD_DIM), 1) // 32
     halves = []
@@ -196,22 +205,25 @@
                     block = jnp.where(lane_group == g, pltpu.roll(groups[g], 32 * ((g - i) % 4), 1), block)
             places.append(block.reshape(4, 1, 1, 8, HEAD_DIM))
         halves.append(jnp.concatenate(places, axis=1))
-    blocks[...] = jnp.concatenate([halves[0], halves[0], halves[1], halves[1]], axis=2).reshape(QUERIES, HEAD_DIM)
-    mine = pl.ds(pl.multiple_of(slot * 32, 32), 32)
+    packed = jnp.concatenate([halves[0], halves[0], halves[1], halves[1]], axis=2).reshape(QUERIES, HEAD_DIM)
+    blocks[0:QUERIES - TURN, :] = packed[TURN:]
+    if TURN:
+        blocks[QUERIES - TURN:QUERIES, :] = packed[:TURN]
+    mine = pl.ds(pl.multiple_of(where_ref[3] * 32, 32), 32)
     blocks[mine, :] = blocks[mine, :] + cross_ref[...] * factor
     out_ref[...] = blocks[...].astype(jnp.bfloat16)
 
 
-def attend(where, q, other, summed, stat, cross):
-    return pl.pallas_call(
-        attend_kernel,
+def join(where, keep, given, cross):
+    return pl.pallas_call(
+        join_kernel,
         out_shape=jax.ShapeDtypeStruct((QUERIES, HEAD_DIM), jnp.bfloat16),
-        in_specs=[pl.BlockSpec(memory_space=pltpu.SMEM)] + [vmem()] * 5,
+        in_specs=[pl.BlockSpec(memory_space=pltpu.SMEM)] + [vmem()] * 3,
         out_specs=vmem(),
         scratch_shapes=[pltpu.VMEM((QUERIES, HEAD_DIM), jnp.float32)],
         compiler_params=params(),
-        name="attend",
-    )(where, q, other, summed, stat, cross)
+        name="join",
+    )(where, keep, given, cross)
 
 
 def finish_kernel(parts_ref, latent_ref, guided_ref, next_ref):
@@ -238,7 +250,7 @@
 def back_groups():
     index = np.arange(512).reshape(2, SPREAD, 4, 2, 2)
     return [
-        [int(index[f, z, x, c, h]) for z in PLANES for f in range(2) for h in range(2)]
+        [int(index[f, z, x, c, h]) for z in BACK_PLANES for f in range(2) for h in range(2)]
         for x in range(4)
         for c in range(2)
     ]
@@ -256,15 +268,15 @@
     kv = jnp.where(zero[0] == 0, recv[:, 0:KV_ROWS, :], jnp.zeros((), recv.dtype))
     kv = jnp.broadcast_to(kv[None], (4, SPREAD, KV_ROWS, HEAD_DIM))
     own = lax.all_to_all(kv, "x", 0, 0, tiled=True).reshape(64, KV_ROWS, HEAD_DIM)
-    left = lax.ppermute(recv[:, 0:32, :], "z", [(PLANES[3 * i + 1], PLANES[3 * i]) for i in range(5)])
-    right = lax.ppermute(recv[:, 32:64, :], "z", [(PLANES[3 * i + 1], PLANES[3 * i + 2]) for i in range(5)])
+    left = lax.ppermute(recv[:, 0:24, :], "z", [(PLANES[3 * i + 1], PLANES[3 * i]) for i in range(5)])
+    right = lax.ppermute(recv[:, 24:48, :], "z", [(PLANES[3 * i + 1], PLANES[3 * i + 2]) for i in range(5)])
     slot = lax.rem(lax.axis_index("z") + (SPREAD - FIRST_PLANE), SPREAD)
-    q = jnp.where(lax.rem(slot, 3) == 0, left, right)
-    ready = q[0:1, 0:1, :] == q[0:1, 0:1, :]
-    other = lax.ppermute(jnp.where(ready, own, jnp.zeros((), own.dtype)), "c", [(0, 1), (1, 0)])
-    where = jnp.stack([slot, lax.axis_index("cfg"), lax.rem(slot, 3)]).astype(jnp.int32)
-    summed, stat = first_half(q, own)
-    back = attend(where, q, other, summed, stat, crossed)
+    q = jnp.concatenate([recv[:, KV_ROWS:BLOCK, :], jnp.where(lax.rem(slot, 3) == 0, left, right)], axis=1)
+    both = lax.all_gather(q, "c")
+    back_slot = lax.rem(lax.axis_index("z") + (SPREAD - BACK_PLANE), SPREAD)
+    where = jnp.stack([slot, lax.axis_index("cfg"), lax.rem(slot, 3), back_slot, lax.axis_index("c")]).astype(jnp.int32)
+    keep, give = partial_attention(where, both, own)
+    back = join(where, keep, lax.all_gather(give, "c"), crossed)
     parts = lax.all_to_all(back, AXES, 0, 0, tiled=True, axis_index_groups=back_groups())
     return finish(parts, latent)
 

time: 82.4 us -> 80.9 us (0.982)
  blocking collectives: 23.6 us -> 30.8 us
  starting transfers between devices: 28.9 us -> 23.3 us
  waiting for transfers between devices: 12.3 us -> 7.98 us
  local copies, waits for them, and re-layouts: 4.55 us -> 5.54 us
    all_gather x0 -> x2, blocking collectives: none -> 7.11 us  [the longest x1 3.68 us: shards(): both = lax.all_gather(q, 'c')]
    ppermute x3 -> x2, starting transfers between devices: 7.59 us -> 1.96 us  [the longest x1 1.29 us: shards(): lax.ppermute(recv[:, 0:24, :], 'z', [(PLANES[3 * i + 1], PLANES[3 * i]) f...]
    all_to_all x1, waiting for transfers between devices: 4.72 us -> 2.33 us  [shards(): lax.all_to_all(packed, 'z', 0, 0, tiled=True, axis_index_groups=[PLANES])]
    all_to_all x1, waiting for transfers between devices: 1.42 us -> 0.01 us  [shards(): lax.all_to_all(kv, 'x', 0, 0, tiled=True).reshape(64, KV_ROWS, HEAD_DIM)]
    unnamed x10, local copies, waits for them, and re-layouts: 3.52 us -> 4.43 us
    ppermute x3 -> x2, waiting for transfers between devices: 6.15 us -> 5.65 us  [the longest x1 5.64 us: shards(): lax.ppermute(recv[:, 0:24, :], 'z', [(PLANES[3 * i + 1], PLANES[3 * i]) f...]
  transfers between devices with their start and end apart: 5 -> 4, of which waited for: 4 -> 2; matrix products, arithmetic and copies ran while one was open for 0% -> 0% of each run, Pallas kernels for 7% -> 5%
where the time goes in v4:
time: 80.9 us; the launch traced here: 80.4 us
  blocking collectives  30.8 us (38%)
  starting transfers between devices  23.3 us (29%)
  Pallas kernels  11.3 us (14%)
  waiting for transfers between devices  7.98 us (10%)
  local copies, waits for them, and re-layouts  5.54 us (7%)
  between operations  1.39 us (2%)
    all_to_all x1, blocking collectives, shards(): lax.all_to_all(back, AXES, 0, 0, tiled=True, axis_index_groups=back_group...  23.7 us
    all_to_all x1, starting transfers between devices, shards(): lax.all_to_all(packed, 'z', 0, 0, tiled=True, axis_index_groups=[PLANES])  17.3 us
    ppermute x1, waiting for transfers between devices, shards(): lax.ppermute(recv[:, 0:24, :], 'z', [(PLANES[3 * i + 1], PLANES[3 * i]) f...  5.64 us
    unnamed x10, local copies, waits for them, and re-layouts  4.43 us
    all_to_all x1, starting transfers between devices, shards(): lax.all_to_all(kv, 'x', 0, 0, tiled=True).reshape(64, KV_ROWS, HEAD_DIM)  4.01 us
    pallas_call x1, Pallas kernels, cross(): pl.pallas_call(cross_kernel, out_shape=(jax.ShapeDtypeStruct((ROWS, HEAD_...  3.88 us
    pallas_call x1, Pallas kernels, partial_attention(): pl.pallas_call(partial_kernel, out_shape=(shape, shape), in_specs=[pl.Blo...  3.81 us
    all_gather x1, blocking collectives, shards(): both = lax.all_gather(q, 'c')  3.68 us
  transfers between devices with their start and end apart: 4, of which 2 were waited for; matrix products, arithmetic and copies ran while one was open for 0% of the time, Pallas kernels for 5%

profile of v4, /device:TPU:1, one launch (start us, length us, event | category | flops | bytes accessed | tf_op | source)
XLA Modules:
  0.0 80.4 jit_solution(13426161802062733120)
XLA Ops:
  0.6 2.1 %pack.1 = bf16[16,56,128]{2,1,0:T(8,128)(2,1)} custom-call(bf16[10,32,128]{2,1,0:T(8,128)(2,1)} %bitcast.40, bf16[10,32,128]{2,1,0:T(8,128)(2,1)} %bitcast.41, bf16[10,32,128]{2,1,0:T(8,128)(2,1)} %bitcast.42, bf16[10,64,128]{2,1,0:T(8,128)(2,1)} %bitcast.34), custom_call_target="tpu_custom_call" | custom-call | tf_op jit(solution)/shard_map/pack/pallas_call | solution.py:71
  2.7 17.3 %all-to-all-start = ((bf16[16,56,128]{2,1,0:T(8,128)(2,1)}), bf16[16,56,128]{2,1,0:T(8,128)(2,1)S(1)}, u32[]{:S(2)}, u32[]{:S(2)}) async-start(bf16[16,56,128]{2,1,0:T(8,128)(2,1)} %pack.1), calls=%async_computation | async-start | bytes 458752 | tf_op jit(solution)/shard_map/all_to_all | solution.py:266
  20.0 0.0 copy-start
  20.0 1.3 %copy-done = bf16[1,512,10,128]{3,1,2,0:T(8,128)(2,1)S(1)} copy-done((bf16[1,512,10,128]{3,1,2,0:T(8,128)(2,1)S(1)}, bf16[1,512,10,128]{3,1,2,0:T(8,128)(2,1)}, u32[]{:S(2)}) %copy-start) | copy-done | bytes 1310744
  21.3 0.0 copy-start.1
  21.3 1.3 %copy-done.1 = bf16[1,512,10,128]{3,1,2,0:T(8,128)(2,1)S(1)} copy-done((bf16[1,512,10,128]{3,1,2,0:T(8,128)(2,1)S(1)}, bf16[1,512,10,128]{3,1,2,0:T(8,128)(2,1)}, u32[]{:S(2)}) %copy-start.1) | copy-done | bytes 1310744
  22.7 0.0 copy-start.2
  22.7 0.9 %copy-done.2 = bf16[10,128,64]{1,2,0:T(8,128)(2,1)S(1)} copy-done((bf16[10,128,64]{1,2,0:T(8,128)(2,1)S(1)}, bf16[10,128,64]{1,2,0:T(8,128)(2,1)}, u32[]{:S(2)}) %copy-start.2) | copy-done | bytes 163864
  23.6 0.0 copy-start.3
  23.6 0.9 %copy-done.3 = bf16[1,32,10,128]{3,1,2,0:T(8,128)(2,1)S(1)} copy-done((bf16[1,32,10,128]{3,1,2,0:T(8,128)(2,1)S(1)}, bf16[1,32,10,128]{3,1,2,0:T(8,128)(2,1)}, u32[]{:S(2)}) %copy-start.3) | copy-done | bytes 81944
  24.5 3.9 %cross.1 = (f32[32,128]{1,0:T(8,128)S(1)}, s32[1]{0:T(128)}) custom-call(bf16[10,32,128]{2,1,0:T(8,128)(2,1)S(1)} %bitcast.39, bf16[10,512,128]{2,1,0:T(8,128)(2,1)S(1)} %bitcast.30, bf16[10,512,128]{2,1,0:T(8,128)(2,1)S(1)} %bitcast.31, bf16[10,64,128]{2,1,0:T(8,128)(2,1)S(1)} %bitcast.35), custom_call_target="tpu_custom_call" | custom-call | flops 90000000 | bytes 3200000 | tf_op jit(solution)/shard_map/cross/pallas_call | solution.py:112
  29.0 2.3 %all-to-all-done = bf16[16,56,128]{2,1,0:T(8,128)(2,1)S(1)} async-done(((bf16[16,56,128]{2,1,0:T(8,128)(2,1)}), bf16[16,56,128]{2,1,0:T(8,128)(2,1)S(1)}, u32[]{:S(2)}, u32[]{:S(2)}) %all-to-all-start) | async-done | bytes 229408 | tf_op jit(solution)/shard_map/all_to_all | solution.py:266
  31.4 1.0 %broadcast_in_dim.11 = bf16[4,16,48,128]{3,2,1,0:T(8,128)(2,1)} broadcast(bf16[16,48,128]{2,1,0:T(8,128)(2,1)S(1)} %slice_select_fusion), dimensions={1,2,3} | broadcast | bytes 983040 | tf_op jit(solution)/shard_map/broadcast_in_dim | solution.py:269
  32.4 4.0 %all-to-all-start.1 = ((bf16[4,16,48,128]{3,2,1,0:T(8,128)(2,1)}), bf16[4,16,48,128]{3,2,1,0:T(8,128)(2,1)S(1)}, u32[]{:S(2)}, u32[]{:S(2)}) async-start(bf16[4,16,48,128]{3,2,1,0:T(8,128)(2,1)} %broadcast_in_dim.11), calls=%async_computation.1 | async-start | bytes 1572864 | tf_op jit(solution)/shard_map/all_to_all | solution.py:270
  36.4 0.7 collective-permute-start.1
  37.1 1.3 %collective-permute-start = (bf16[16,24,128]{2,1,0:T(8,128)(2,1)S(1)}, bf16[16,24,128]{2,1,0:T(8,128)(2,1)S(1)}, u32[]{:S(2)}, u32[]{:S(2)}) collective-permute-start(bf16[16,24,128]{2,1,0:T(8,128)(2,1)S(1)} %get-tuple-element.11), channel_id=1, source_target_pairs={{176,160},{224,208},{16,0},{64,48},{112,96},{177,161},{225,209},{1... | collective-permute-start | bytes 294920 | tf_op jit(solution)/shard_map/ppermute | solution.py:271
  38.4 0.1 stack.23.where_ref
  38.5 0.0 collective-permute-done.1
  38.5 5.6 %collective-permute-done = bf16[16,24,128]{2,1,0:T(8,128)(2,1)S(1)} collective-permute-done((bf16[16,24,128]{2,1,0:T(8,128)(2,1)S(1)}, bf16[16,24,128]{2,1,0:T(8,128)(2,1)S(1)}, u32[]{:S(2)}, u32[]{:S(2)}) %collective-permute-start) | collective-permute-done | bytes 98336 | tf_op jit(solution)/shard_map/ppermute | solution.py:271
  44.2 3.7 %all-gather = bf16[32,32,128]{2,1,0:T(8,128)(2,1)S(1)} all-gather(bf16[16,32,128]{2,1,0:T(8,128)(2,1)S(1)} %pad_maximum_fusion), channel_id=2, replica_groups=mesh['cfg'=2,'z'=16,'x'=4,'c'=2,'head'=2] {'c'}, dimensions={0}, use_global_device_ids=true | all-gather | bytes 393216 | tf_op jit(solution)/shard_map/all_gather | solution.py:275
  47.8 0.0 all-to-all-done.1
  47.8 3.8 %partial_attention.1 = (f32[80,512]{1,0:T(8,128)S(1)}, f32[80,512]{1,0:T(8,128)S(1)}) custom-call(s32[5]{0:T(128)S(1)} %stack.23.where_ref, bf16[2,16,32,128]{3,2,1,0:T(8,128)(2,1)S(1)} %bitcast.38, bf16[64,48,128]{2,1,0:T(8,128)(2,1)S(1)} %bitcast.33), custom_call_target="tpu_custom_call" | custom-call | flops 1080000000 | bytes 1600000 | tf_op jit(solution)/shard_map/partial_attention/pallas_call | solution.py:169
  51.7 0.0 copy-start.4
  51.7 3.4 %all-gather.1 = f32[160,512]{1,0:T(8,128)S(1)} all-gather(f32[80,512]{1,0:T(8,128)S(1)} %get-tuple-element.8), channel_id=3, replica_groups=mesh['cfg'=2,'z'=16,'x'=4,'c'=2,'head'=2] {'c'}, dimensions={0}, use_global_device_ids=true | all-gather | bytes 491520 | tf_op jit(solution)/shard_map/all_gather | solution.py:279
  55.1 0.7 join.1
  55.9 23.7 %all_to_all.21 = bf16[64,8,128]{2,1,0:T(8,128)(2,1)S(1)} all-to-all(bf16[64,8,128]{2,1,0:T(8,128)(2,1)S(1)} %bitcast.37), channel_id=1, replica_groups={{128,129,384,385,144,145,400,401,160,161,416,417,176,177,432,433,192,19..., dimensions={0} | all-to-all | bytes 262144 | tf_op jit(solution)/shard_map/all_to_all | solution.py:280
  79.6 0.0 copy-done.4
  79.6 0.8 %finish.1 = (f32[32,32]{1,0:T(8,128)}, f32[32,32]{1,0:T(8,128)}) custom-call(bf16[512,128]{1,0:T(8,128)(2,1)S(1)} %bitcast.36, f32[32,32]{1,0:T(8,128)S(1)} %copy-done.4), custom_call_target="tpu_custom_call" | custom-call | tf_op jit(solution)/shard_map/finish/pallas_call | solution.py:240
  (5 shorter events, 0.1 us)
Async XLA Ops:
  2.7 28.6 %all-to-all-start = ((bf16[16,56,128]{2,1,0:T(8,128)(2,1)}), bf16[16,56,128]{2,1,0:T(8,128)(2,1)S(1)}, u32[]{:S(2)}, u32[]{:S(2)}) async-start(bf16[16,56,128]{2,1,0:T(8,128)(2,1)} %pack.1), calls=%async_computation | async-start | bytes 458752 | tf_op jit(solution)/shard_map/all_to_all | solution.py:266
  20.0 1.3 %copy-start = (bf16[1,512,10,128]{3,1,2,0:T(8,128)(2,1)S(1)}, bf16[1,512,10,128]{3,1,2,0:T(8,128)(2,1)}, u32[]{:S(2)}) copy-start(bf16[1,512,10,128]{3,1,2,0:T(8,128)(2,1)} %param.12) | copy-start | bytes 3932164
  21.3 1.3 %copy-start.1 = (bf16[1,512,10,128]{3,1,2,0:T(8,128)(2,1)S(1)}, bf16[1,512,10,128]{3,1,2,0:T(8,128)(2,1)}, u32[]{:S(2)}) copy-start(bf16[1,512,10,128]{3,1,2,0:T(8,128)(2,1)} %param.13) | copy-start | bytes 3932164
  22.7 0.9 %copy-start.2 = (bf16[10,128,64]{1,2,0:T(8,128)(2,1)S(1)}, bf16[10,128,64]{1,2,0:T(8,128)(2,1)}, u32[]{:S(2)}) copy-start(bf16[10,128,64]{1,2,0:T(8,128)(2,1)} %param.14) | copy-start | bytes 491524
  23.6 0.9 %copy-start.3 = (bf16[1,32,10,128]{3,1,2,0:T(8,128)(2,1)S(1)}, bf16[1,32,10,128]{3,1,2,0:T(8,128)(2,1)}, u32[]{:S(2)}) copy-start(bf16[1,32,10,128]{3,1,2,0:T(8,128)(2,1)} %param.11) | copy-start | bytes 245764
  32.4 15.5 %all-to-all-start.1 = ((bf16[4,16,48,128]{3,2,1,0:T(8,128)(2,1)}), bf16[4,16,48,128]{3,2,1,0:T(8,128)(2,1)S(1)}, u32[]{:S(2)}, u32[]{:S(2)}) async-start(bf16[4,16,48,128]{3,2,1,0:T(8,128)(2,1)} %broadcast_in_dim.11), calls=%async_computation.1 | async-start | bytes 1572864 | tf_op jit(solution)/shard_map/all_to_all | solution.py:270
  36.4 2.1 %collective-permute-start.1 = (bf16[16,24,128]{2,1,0:T(8,128)(2,1)S(1)}, bf16[16,24,128]{2,1,0:T(8,128)(2,1)S(1)}, u32[]{:S(2)}, u32[]{:S(2)}) collective-permute-start(bf16[16,24,128]{2,1,0:T(8,128)(2,1)S(1)} %get-tuple-element.10), channel_id=1, source_target_pairs={{176,192},{224,240},{16,32},{64,80},{112,128},{177,193},{225,241},... | collective-permute-start | bytes 294920 | tf_op jit(solution)/shard_map/ppermute | solution.py:272
  37.1 7.1 %collective-permute-start = (bf16[16,24,128]{2,1,0:T(8,128)(2,1)S(1)}, bf16[16,24,128]{2,1,0:T(8,128)(2,1)S(1)}, u32[]{:S(2)}, u32[]{:S(2)}) collective-permute-start(bf16[16,24,128]{2,1,0:T(8,128)(2,1)S(1)} %get-tuple-element.11), channel_id=1, source_target_pairs={{176,160},{224,208},{16,0},{64,48},{112,96},{177,161},{225,209},{1... | collective-permute-start | bytes 294920 | tf_op jit(solution)/shard_map/ppermute | solution.py:271
  51.7 27.9 %copy-start.4 = (f32[32,32]{1,0:T(8,128)S(1)}, f32[32,32]{1,0:T(8,128)}, u32[]{:S(2)}) copy-start(f32[32,32]{1,0:T(8,128)} %latent_ref.1) | copy-start | bytes 12292

commit v5 on v3

--- a/solution.py
+++ b/solution.py
@@ -12,10 +12,13 @@
 HEADS_HERE = 10
 ROWS = 32
 SPREAD = 16
-BLOCK = 64
+BLOCK = 56
 KV_ROWS = 48
-FIRST_PLANE = 10
+FIRST_PLANE = 11
+BACK_PLANE = 9
 PLANES = [(FIRST_PLANE + i) % SPREAD for i in range(SPREAD)]
+BACK_PLANES = [(BACK_PLANE + i) % SPREAD for i in range(SPREAD)]
+TURN = 32 * ((BACK_PLANE - FIRST_PLANE) % SPREAD)
 AXES = ("cfg", "z", "x", "c", "head")
 GUIDANCE = 5.0
 STEP = 0.1
@@ -44,14 +47,15 @@
     ]
     for load in loads:
         load.start()
-    for h in range(HEADS_HERE):
-        blocks[key_slot(h), KV_ROWS:BLOCK, :] = jnp.zeros((BLOCK - KV_ROWS, HEAD_DIM), jnp.bfloat16)
+    for pair in range(HEADS_HERE // 2):
+        blocks[3 * pair + 1, 48:BLOCK, :] = jnp.zeros((BLOCK - 48, HEAD_DIM), jnp.bfloat16)
     blocks[SPREAD - 1] = jnp.zeros((BLOCK, HEAD_DIM), jnp.bfloat16)
     for load in loads:
         load.wait()
     for h in range(HEADS_HERE):
         blocks[key_slot(h), 0:32, :] = k_scratch[h]
-        blocks[3 * (h // 2) + 1, 32 * (h % 2):32 * (h % 2) + 32, :] = q_scratch[h]
+        blocks[key_slot(h), KV_ROWS:BLOCK, :] = q_scratch[h, 0:8]
+        blocks[3 * (h // 2) + 1, 24 * (h % 2):24 * (h % 2) + 24, :] = q_scratch[h, 8:32]
         projected = lax.dot_general(
             v_scratch[h], w_scratch[h], (((1,), (1,)), ((), ())), preferred_element_type=jnp.float32
         )
@@ -196,8 +200,11 @@
                     block = jnp.where(lane_group == g, pltpu.roll(groups[g], 32 * ((g - i) % 4), 1), block)
             places.append(block.reshape(4, 1, 1, 8, HEAD_DIM))
         halves.append(jnp.concatenate(places, axis=1))
-    blocks[...] = jnp.concatenate([halves[0], halves[0], halves[1], halves[1]], axis=2).reshape(QUERIES, HEAD_DIM)
-    mine = pl.ds(pl.multiple_of(slot * 32, 32), 32)
+    packed = jnp.concatenate([halves[0], halves[0], halves[1], halves[1]], axis=2).reshape(QUERIES, HEAD_DIM)
+    blocks[0:QUERIES - TURN, :] = packed[TURN:]
+    if TURN:
+        blocks[QUERIES - TURN:QUERIES, :] = packed[:TURN]
+    mine = pl.ds(pl.multiple_of(where_ref[3] * 32, 32), 32)
     blocks[mine, :] = blocks[mine, :] + cross_ref[...] * factor
     out_ref[...] = blocks[...].astype(jnp.bfloat16)
 
@@ -238,7 +245,7 @@
 def back_groups():
     index = np.arange(512).reshape(2, SPREAD, 4, 2, 2)
     return [
-        [int(index[f, z, x, c, h]) for z in PLANES for f in range(2) for h in range(2)]
+        [int(index[f, z, x, c, h]) for z in BACK_PLANES for f in range(2) for h in range(2)]
         for x in range(4)
         for c in range(2)
     ]
@@ -256,13 +263,15 @@
     kv = jnp.where(zero[0] == 0, recv[:, 0:KV_ROWS, :], jnp.zeros((), recv.dtype))
     kv = jnp.broadcast_to(kv[None], (4, SPREAD, KV_ROWS, HEAD_DIM))
     own = lax.all_to_all(kv, "x", 0, 0, tiled=True).reshape(64, KV_ROWS, HEAD_DIM)
-    left = lax.ppermute(recv[:, 0:32, :], "z", [(PLANES[3 * i + 1], PLANES[3 * i]) for i in range(5)])
-    right = lax.ppermute(recv[:, 32:64, :], "z", [(PLANES[3 * i + 1], PLANES[3 * i + 2]) for i in range(5)])
+    left = lax.ppermute(recv[:, 0:24, :], "z", [(PLANES[3 * i + 1], PLANES[3 * i]) for i in range(5)])
+    right = lax.ppermute(recv[:, 24:48, :], "z", [(PLANES[3 * i + 1], PLANES[3 * i + 2]) for i in range(5)])
     slot = lax.rem(lax.axis_index("z") + (SPREAD - FIRST_PLANE), SPREAD)
-    q = jnp.where(lax.rem(slot, 3) == 0, left, right)
-    ready = q[0:1, 0:1, :] == q[0:1, 0:1, :]
+    moved = jnp.where(lax.rem(slot, 3) == 0, left, right)
+    q = jnp.concatenate([recv[:, KV_ROWS:BLOCK, :], moved], axis=1)
+    ready = moved[0:1, 0:1, :] == moved[0:1, 0:1, :]
     other = lax.ppermute(jnp.where(ready, own, jnp.zeros((), own.dtype)), "c", [(0, 1), (1, 0)])
-    where = jnp.stack([slot, lax.axis_index("cfg"), lax.rem(slot, 3)]).astype(jnp.int32)
+    back_slot = lax.rem(lax.axis_index("z") + (SPREAD - BACK_PLANE), SPREAD)
+    where = jnp.stack([slot, lax.axis_index("cfg"), lax.rem(slot, 3), back_slot]).astype(jnp.int32)
     summed, stat = first_half(q, own)
     back = attend(where, q, other, summed, stat, crossed)
     parts = lax.all_to_all(back, AXES, 0, 0, tiled=True, axis_index_groups=back_groups())

time: 82.4 us -> 80.6 us (0.978)
  starting transfers between devices: 28.9 us -> 26.6 us
  blocking collectives: 23.6 us -> 22.2 us
  waiting for transfers between devices: 12.3 us -> 13.3 us
  local copies, waits for them, and re-layouts: 4.55 us -> 5.47 us
    all_to_all x1, waiting for transfers between devices: 1.42 us -> 3.99 us  [shards(): lax.all_to_all(kv, 'x', 0, 0, tiled=True).reshape(64, KV_ROWS, HEAD_DIM)]
    all_to_all x1, blocking collectives: 23.6 us -> 22.2 us  [shards(): lax.all_to_all(back, AXES, 0, 0, tiled=True, axis_index_groups=back_group...]
    ppermute x1, starting transfers between devices: 5.63 us -> 4.23 us  [shards(): lax.ppermute(jnp.where(ready, own, jnp.zeros((), own.dtype)), 'c', [(0, 1...]
    ppermute x2, waiting for transfers between devices: 6.05 us -> 4.88 us  [the longest x1 4.87 us: shards(): lax.ppermute(recv[:, 24:48, :], 'z', [(PLANES[3 * i + 1], PLANES[3 * i +...]
    unnamed x10, local copies, waits for them, and re-layouts: 3.52 us -> 4.43 us
    all_to_all x1, starting transfers between devices: 17.3 us -> 16.4 us  [shards(): lax.all_to_all(packed, 'z', 0, 0, tiled=True, axis_index_groups=[PLANES])]
where the time goes in v5:
time: 80.6 us; the launch traced here: 80.1 us
  starting transfers between devices  26.6 us (33%)
  blocking collectives  22.2 us (28%)
  waiting for transfers between devices  13.3 us (17%)
  Pallas kernels  10.8 us (13%)
  local copies, waits for them, and re-layouts  5.47 us (7%)
  between operations  1.41 us (2%)
    all_to_all x1, blocking collectives, shards(): lax.all_to_all(back, AXES, 0, 0, tiled=True, axis_index_groups=back_group...  22.2 us
    all_to_all x1, starting transfers between devices, shards(): lax.all_to_all(packed, 'z', 0, 0, tiled=True, axis_index_groups=[PLANES])  16.4 us
    ppermute x1, waiting for transfers between devices, shards(): lax.ppermute(recv[:, 24:48, :], 'z', [(PLANES[3 * i + 1], PLANES[3 * i +...  4.87 us
    unnamed x10, local copies, waits for them, and re-layouts  4.43 us
    all_to_all x1, waiting for transfers between devices, shards(): lax.all_to_all(packed, 'z', 0, 0, tiled=True, axis_index_groups=[PLANES])  4.4 us
    ppermute x1, starting transfers between devices, shards(): lax.ppermute(jnp.where(ready, own, jnp.zeros((), own.dtype)), 'c', [(0, 1...  4.23 us
    all_to_all x1, starting transfers between devices, shards(): lax.all_to_all(kv, 'x', 0, 0, tiled=True).reshape(64, KV_ROWS, HEAD_DIM)  4.01 us
    all_to_all x1, waiting for transfers between devices, shards(): lax.all_to_all(kv, 'x', 0, 0, tiled=True).reshape(64, KV_ROWS, HEAD_DIM)  3.99 us
  transfers between devices with their start and end apart: 5, of which 4 were waited for; matrix products, arithmetic and copies ran while one was open for 0% of the time, Pallas kernels for 7%

profile of v5, /device:TPU:1, one launch (start us, length us, event | category | flops | bytes accessed | tf_op | source)
XLA Modules:
  0.0 80.1 jit_solution(10620994772066195717)
XLA Ops:
  0.6 2.0 %pack.1 = bf16[16,56,128]{2,1,0:T(8,128)(2,1)} custom-call(bf16[10,32,128]{2,1,0:T(8,128)(2,1)} %bitcast.38, bf16[10,32,128]{2,1,0:T(8,128)(2,1)} %bitcast.39, bf16[10,32,128]{2,1,0:T(8,128)(2,1)} %bitcast.40, bf16[10,64,128]{2,1,0:T(8,128)(2,1)} %bitcast.33), custom_call_target="tpu_custom_call" | custom-call | tf_op jit(solution)/shard_map/pack/pallas_call | solution.py:71
  2.7 16.4 %all-to-all-start = ((bf16[16,56,128]{2,1,0:T(8,128)(2,1)}), bf16[16,56,128]{2,1,0:T(8,128)(2,1)S(1)}, u32[]{:S(2)}, u32[]{:S(2)}) async-start(bf16[16,56,128]{2,1,0:T(8,128)(2,1)} %pack.1), calls=%async_computation | async-start | bytes 458752 | tf_op jit(solution)/shard_map/all_to_all | solution.py:261
  19.1 0.0 copy-start
  19.1 1.3 %copy-done = bf16[1,512,10,128]{3,1,2,0:T(8,128)(2,1)S(1)} copy-done((bf16[1,512,10,128]{3,1,2,0:T(8,128)(2,1)S(1)}, bf16[1,512,10,128]{3,1,2,0:T(8,128)(2,1)}, u32[]{:S(2)}) %copy-start) | copy-done | bytes 1310744
  20.4 0.0 copy-start.1
  20.4 1.3 %copy-done.1 = bf16[1,512,10,128]{3,1,2,0:T(8,128)(2,1)S(1)} copy-done((bf16[1,512,10,128]{3,1,2,0:T(8,128)(2,1)S(1)}, bf16[1,512,10,128]{3,1,2,0:T(8,128)(2,1)}, u32[]{:S(2)}) %copy-start.1) | copy-done | bytes 1310744
  21.8 0.0 copy-start.2
  21.8 0.9 %copy-done.2 = bf16[10,128,64]{1,2,0:T(8,128)(2,1)S(1)} copy-done((bf16[10,128,64]{1,2,0:T(8,128)(2,1)S(1)}, bf16[10,128,64]{1,2,0:T(8,128)(2,1)}, u32[]{:S(2)}) %copy-start.2) | copy-done | bytes 163864
  22.7 0.0 copy-start.3
  22.7 0.9 %copy-done.3 = bf16[1,32,10,128]{3,1,2,0:T(8,128)(2,1)S(1)} copy-done((bf16[1,32,10,128]{3,1,2,0:T(8,128)(2,1)S(1)}, bf16[1,32,10,128]{3,1,2,0:T(8,128)(2,1)}, u32[]{:S(2)}) %copy-start.3) | copy-done | bytes 81944
  23.6 3.9 %cross.1 = (f32[32,128]{1,0:T(8,128)S(1)}, s32[1]{0:T(128)}) custom-call(bf16[10,32,128]{2,1,0:T(8,128)(2,1)S(1)} %bitcast.37, bf16[10,512,128]{2,1,0:T(8,128)(2,1)S(1)} %bitcast.31, bf16[10,512,128]{2,1,0:T(8,128)(2,1)S(1)} %bitcast.32, bf16[10,64,128]{2,1,0:T(8,128)(2,1)S(1)} %bitcast.34), custom_call_target="tpu_custom_call" | custom-call | flops 90000000 | bytes 3200000 | tf_op jit(solution)/shard_map/cross/pallas_call | solution.py:112
  28.1 4.4 %all-to-all-done = bf16[16,56,128]{2,1,0:T(8,128)(2,1)S(1)} async-done(((bf16[16,56,128]{2,1,0:T(8,128)(2,1)}), bf16[16,56,128]{2,1,0:T(8,128)(2,1)S(1)}, u32[]{:S(2)}, u32[]{:S(2)}) %all-to-all-start) | async-done | bytes 229408 | tf_op jit(solution)/shard_map/all_to_all | solution.py:261
  32.5 1.0 %broadcast_in_dim.27 = bf16[4,16,48,128]{3,2,1,0:T(8,128)(2,1)} broadcast(bf16[16,48,128]{2,1,0:T(8,128)(2,1)S(1)} %slice_select_fusion), dimensions={1,2,3} | broadcast | bytes 983040 | tf_op jit(solution)/shard_map/broadcast_in_dim | solution.py:264
  33.5 4.0 %all-to-all-start.1 = ((bf16[4,16,48,128]{3,2,1,0:T(8,128)(2,1)}), bf16[4,16,48,128]{3,2,1,0:T(8,128)(2,1)S(1)}, u32[]{:S(2)}, u32[]{:S(2)}) async-start(bf16[4,16,48,128]{3,2,1,0:T(8,128)(2,1)} %broadcast_in_dim.27), calls=%async_computation.1 | async-start | bytes 1572864 | tf_op jit(solution)/shard_map/all_to_all | solution.py:265
  37.6 1.3 %collective-permute-start.1 = (bf16[16,24,128]{2,1,0:T(8,128)(2,1)S(1)}, bf16[16,24,128]{2,1,0:T(8,128)(2,1)S(1)}, u32[]{:S(2)}, u32[]{:S(2)}) collective-permute-start(bf16[16,24,128]{2,1,0:T(8,128)(2,1)S(1)} %get-tuple-element.10), channel_id=1, source_target_pairs={{192,208},{240,0},{32,48},{80,96},{128,144},{193,209},{241,1},{33,... | collective-permute-start | bytes 294920 | tf_op jit(solution)/shard_map/ppermute | solution.py:267
  38.9 0.7 collective-permute-start
  39.6 4.9 %collective-permute-done.1 = bf16[16,24,128]{2,1,0:T(8,128)(2,1)S(1)} collective-permute-done((bf16[16,24,128]{2,1,0:T(8,128)(2,1)S(1)}, bf16[16,24,128]{2,1,0:T(8,128)(2,1)S(1)}, u32[]{:S(2)}, u32[]{:S(2)}) %collective-permute-start.1) | collective-permute-done | bytes 98336 | tf_op jit(solution)/shard_map/ppermute | solution.py:267
  44.4 0.0 collective-permute-done
  44.5 4.0 %all-to-all-done.1 = bf16[4,16,48,128]{3,2,1,0:T(8,128)(2,1)S(1)} async-done(((bf16[4,16,48,128]{3,2,1,0:T(8,128)(2,1)}), bf16[4,16,48,128]{3,2,1,0:T(8,128)(2,1)S(1)}, u32[]{:S(2)}, u32[]{:S(2)}) %all-to-all-start.1) | async-done | bytes 786464 | tf_op jit(solution)/shard_map/all_to_all | solution.py:265
  48.5 0.1 broadcast_select_fusion
  48.6 4.2 %collective-permute-start.2 = (bf16[64,48,128]{2,1,0:T(8,128)(2,1)S(1)}, bf16[64,48,128]{2,1,0:T(8,128)(2,1)S(1)}, u32[]{:S(2)}, u32[]{:S(2)}) collective-permute-start(bf16[64,48,128]{2,1,0:T(8,128)(2,1)S(1)} %broadcast_select_fusion), channel_id=1, source_target_pairs={{0,2},{2,0},{1,3},{3,1},{4,6},{6,4},{5,7},{7,5},{8,10},{10,8},{9,1... | collective-permute-start | bytes 2359304 | tf_op jit(solution)/shard_map/ppermute | solution.py:272
  52.8 0.1 pad_add_fusion.where_ref
  52.9 0.0 copy-start.4
  52.9 1.7 %first_half.1 = (f32[64,512]{1,0:T(8,128)S(1)}, f32[16,512]{1,0:T(8,128)S(1)}) custom-call(bf16[16,32,128]{2,1,0:T(8,128)(2,1)S(1)} %pad_maximum_fusion.q_ref, bf16[64,48,128]{2,1,0:T(8,128)(2,1)S(1)} %bitcast.30), custom_call_target="tpu_custom_call" | custom-call | flops 540000000 | bytes 1600000 | tf_op jit(solution)/shard_map/first_half/pallas_call | solution.py:163
  54.6 0.1 collective-permute-done.2.other_ref
  54.7 2.4 %attend.1 = bf16[512,128]{1,0:T(8,128)(2,1)S(1)} custom-call(s32[4]{0:T(128)S(1)} %pad_add_fusion.where_ref, bf16[16,32,128]{2,1,0:T(8,128)(2,1)S(1)} %pad_maximum_fusion.q_ref, bf16[64,48,128]{2,1,0:T(8,128)(2,1)S(1)} %collective-permute-done.2.other_ref, f32[64,512]{1,0:T(8,128)S(1)} %get-tuple-element.7.sum_ref, f32[16,512]{1,0:T(8,128)S(1)} %get-tuple-element.8.stat_ref, ...), custom_call_target="tpu_custom_call" | custom-call | tf_op jit(solution)/shard_map/attend/pallas_call | solution.py:213
  57.1 22.2 %all_to_all.21 = bf16[64,8,128]{2,1,0:T(8,128)(2,1)S(1)} all-to-all(bf16[64,8,128]{2,1,0:T(8,128)(2,1)S(1)} %bitcast.35), channel_id=1, replica_groups={{144,145,400,401,160,161,416,417,176,177,432,433,192,193,448,449,208,20..., dimensions={0} | all-to-all | bytes 262144 | tf_op jit(solution)/shard_map/all_to_all | solution.py:277
  79.3 0.0 copy-done.4
  79.3 0.8 %finish.1 = (f32[32,32]{1,0:T(8,128)}, f32[32,32]{1,0:T(8,128)}) custom-call(bf16[512,128]{1,0:T(8,128)(2,1)S(1)} %bitcast.36, f32[32,32]{1,0:T(8,128)S(1)} %copy-done.4), custom_call_target="tpu_custom_call" | custom-call | tf_op jit(solution)/shard_map/finish/pallas_call | solution.py:235
  (6 shorter events, 0.1 us)
Async XLA Ops:
  2.7 29.8 %all-to-all-start = ((bf16[16,56,128]{2,1,0:T(8,128)(2,1)}), bf16[16,56,128]{2,1,0:T(8,128)(2,1)S(1)}, u32[]{:S(2)}, u32[]{:S(2)}) async-start(bf16[16,56,128]{2,1,0:T(8,128)(2,1)} %pack.1), calls=%async_computation | async-start | bytes 458752 | tf_op jit(solution)/shard_map/all_to_all | solution.py:261
  19.1 1.3 %copy-start = (bf16[1,512,10,128]{3,1,2,0:T(8,128)(2,1)S(1)}, bf16[1,512,10,128]{3,1,2,0:T(8,128)(2,1)}, u32[]{:S(2)}) copy-start(bf16[1,512,10,128]{3,1,2,0:T(8,128)(2,1)} %param.12) | copy-start | bytes 3932164
  20.4 1.3 %copy-start.1 = (bf16[1,512,10,128]{3,1,2,0:T(8,128)(2,1)S(1)}, bf16[1,512,10,128]{3,1,2,0:T(8,128)(2,1)}, u32[]{:S(2)}) copy-start(bf16[1,512,10,128]{3,1,2,0:T(8,128)(2,1)} %param.13) | copy-start | bytes 3932164
  21.8 0.9 %copy-start.2 = (bf16[10,128,64]{1,2,0:T(8,128)(2,1)S(1)}, bf16[10,128,64]{1,2,0:T(8,128)(2,1)}, u32[]{:S(2)}) copy-start(bf16[10,128,64]{1,2,0:T(8,128)(2,1)} %param.14) | copy-start | bytes 491524
  22.7 0.9 %copy-start.3 = (bf16[1,32,10,128]{3,1,2,0:T(8,128)(2,1)S(1)}, bf16[1,32,10,128]{3,1,2,0:T(8,128)(2,1)}, u32[]{:S(2)}) copy-start(bf16[1,32,10,128]{3,1,2,0:T(8,128)(2,1)} %param.11) | copy-start | bytes 245764
  33.5 14.9 %all-to-all-start.1 = ((bf16[4,16,48,128]{3,2,1,0:T(8,128)(2,1)}), bf16[4,16,48,128]{3,2,1,0:T(8,128)(2,1)S(1)}, u32[]{:S(2)}, u32[]{:S(2)}) async-start(bf16[4,16,48,128]{3,2,1,0:T(8,128)(2,1)} %broadcast_in_dim.27), calls=%async_computation.1 | async-start | bytes 1572864 | tf_op jit(solution)/shard_map/all_to_all | solution.py:265
  37.6 6.9 %collective-permute-start.1 = (bf16[16,24,128]{2,1,0:T(8,128)(2,1)S(1)}, bf16[16,24,128]{2,1,0:T(8,128)(2,1)S(1)}, u32[]{:S(2)}, u32[]{:S(2)}) collective-permute-start(bf16[16,24,128]{2,1,0:T(8,128)(2,1)S(1)} %get-tuple-element.10), channel_id=1, source_target_pairs={{192,208},{240,0},{32,48},{80,96},{128,144},{193,209},{241,1},{33,... | collective-permute-start | bytes 294920 | tf_op jit(solution)/shard_map/ppermute | solution.py:267
  38.9 5.6 %collective-permute-start = (bf16[16,24,128]{2,1,0:T(8,128)(2,1)S(1)}, bf16[16,24,128]{2,1,0:T(8,128)(2,1)S(1)}, u32[]{:S(2)}, u32[]{:S(2)}) collective-permute-start(bf16[16,24,128]{2,1,0:T(8,128)(2,1)S(1)} %get-tuple-element.11), channel_id=1, source_target_pairs={{192,176},{240,224},{32,16},{80,64},{128,112},{193,177},{241,225},... | collective-permute-start | bytes 294920 | tf_op jit(solution)/shard_map/ppermute | solution.py:266
  48.6 6.1 %collective-permute-start.2 = (bf16[64,48,128]{2,1,0:T(8,128)(2,1)S(1)}, bf16[64,48,128]{2,1,0:T(8,128)(2,1)S(1)}, u32[]{:S(2)}, u32[]{:S(2)}) collective-permute-start(bf16[64,48,128]{2,1,0:T(8,128)(2,1)S(1)} %broadcast_select_fusion), channel_id=1, source_target_pairs={{0,2},{2,0},{1,3},{3,1},{4,6},{6,4},{5,7},{7,5},{8,10},{10,8},{9,1... | collective-permute-start | bytes 2359304 | tf_op jit(solution)/shard_map/ppermute | solution.py:272
  52.9 26.4 %copy-start.4 = (f32[32,32]{1,0:T(8,128)S(1)}, f32[32,32]{1,0:T(8,128)}, u32[]{:S(2)}) copy-start(f32[32,32]{1,0:T(8,128)} %latent_ref.1) | copy-start | bytes 12292

commit v6 on v5

--- a/solution.py
+++ b/solution.py
@@ -18,7 +18,7 @@
 BACK_PLANE = 9
 PLANES = [(FIRST_PLANE + i) % SPREAD for i in range(SPREAD)]
 BACK_PLANES = [(BACK_PLANE + i) % SPREAD for i in range(SPREAD)]
-TURN = 32 * ((BACK_PLANE - FIRST_PLANE) % SPREAD)
+OUT_PLANES = [11, 12, 10, 13, 9, 14, 8, 15, 7, 0, 6, 1, 5, 2, 4, 3]
 AXES = ("cfg", "z", "x", "c", "head")
 GUIDANCE = 5.0
 STEP = 0.1
@@ -35,7 +35,11 @@
 
 
 def key_slot(head):
-    return 3 * (head // 2) + 2 * (head % 2)
+    return OUT_PLANES.index(PLANES[3 * (head // 2) + 2 * (head % 2)])
+
+
+def query_slot(pair):
+    return OUT_PLANES.index(PLANES[3 * pair + 1])
 
 
 def pack_kernel(q_ref, k_ref, v_ref, w_ref, out_ref, blocks, q_scratch, k_scratch, v_scratch, w_scratch, sems):
@@ -48,14 +52,14 @@
     for load in loads:
         load.start()
     for pair in range(HEADS_HERE // 2):
-        blocks[3 * pair + 1, 48:BLOCK, :] = jnp.zeros((BLOCK - 48, HEAD_DIM), jnp.bfloat16)
-    blocks[SPREAD - 1] = jnp.zeros((BLOCK, HEAD_DIM), jnp.bfloat16)
+        blocks[query_slot(pair), 48:BLOCK, :] = jnp.zeros((BLOCK - 48, HEAD_DIM), jnp.bfloat16)
+    blocks[OUT_PLANES.index(PLANES[SPREAD - 1])] = jnp.zeros((BLOCK, HEAD_DIM), jnp.bfloat16)
     for load in loads:
         load.wait()
     for h in range(HEADS_HERE):
         blocks[key_slot(h), 0:32, :] = k_scratch[h]
         blocks[key_slot(h), KV_ROWS:BLOCK, :] = q_scratch[h, 0:8]
-        blocks[3 * (h // 2) + 1, 24 * (h % 2):24 * (h % 2) + 24, :] = q_scratch[h, 8:32]
+        blocks[query_slot(h // 2), 24 * (h % 2):24 * (h % 2) + 24, :] = q_scratch[h, 8:32]
         projected = lax.dot_general(
             v_scratch[h], w_scratch[h], (((1,), (1,)), ((), ())), preferred_element_type=jnp.float32
         )
@@ -201,9 +205,9 @@
             places.append(block.reshape(4, 1, 1, 8, HEAD_DIM))
         halves.append(jnp.concatenate(places, axis=1))
     packed = jnp.concatenate([halves[0], halves[0], halves[1], halves[1]], axis=2).reshape(QUERIES, HEAD_DIM)
-    blocks[0:QUERIES - TURN, :] = packed[TURN:]
-    if TURN:
-        blocks[QUERIES - TURN:QUERIES, :] = packed[:TURN]
+    for at, plane in enumerate(BACK_PLANES):
+        held = 32 * OUT_PLANES.index(plane)
+        blocks[32 * at:32 * at + 32, :] = packed[held:held + 32]
     mine = pl.ds(pl.multiple_of(where_ref[3] * 32, 32), 32)
     blocks[mine, :] = blocks[mine, :] + cross_ref[...] * factor
     out_ref[...] = blocks[...].astype(jnp.bfloat16)
@@ -258,7 +262,7 @@
 def shards(queries, self_keys, self_values, cross_queries, text_keys, text_values, out_weight, latent):
     w = jnp.transpose(out_weight, (0, 2, 1))
     packed = pack(heads_first(queries[0]), heads_first(self_keys[0]), heads_first(self_values[0]), w)
-    recv = lax.all_to_all(packed, "z", 0, 0, tiled=True, axis_index_groups=[PLANES])
+    recv = lax.all_to_all(packed, "z", 0, 0, tiled=True, axis_index_groups=[OUT_PLANES])
     crossed, zero = cross(heads_first(cross_queries[0]), heads_first(text_keys[0]), heads_first(text_values[0]), w)
     kv = jnp.where(zero[0] == 0, recv[:, 0:KV_ROWS, :], jnp.zeros((), recv.dtype))
     kv = jnp.broadcast_to(kv[None], (4, SPREAD, KV_ROWS, HEAD_DIM))

time: 80.6 us -> 79.6 us (0.988)
  waiting for transfers between devices: 13.3 us -> 7.33 us
  starting transfers between devices: 26.6 us -> 30 us
  blocking collectives: 22.2 us -> 23.9 us
    all_to_all x1, waiting for transfers between devices: 4.4 us -> 0.96 us  [shards(): lax.all_to_all(packed, 'z', 0, 0, tiled=True, axis_index_groups=[OUT_PLAN...]
    ppermute x1, starting transfers between devices: 4.23 us -> 7.55 us  [shards(): lax.ppermute(jnp.where(ready, own, jnp.zeros((), own.dtype)), 'c', [(0, 1...]
    all_to_all x1, waiting for transfers between devices: 3.99 us -> 1.71 us  [shards(): lax.all_to_all(kv, 'x', 0, 0, tiled=True).reshape(64, KV_ROWS, HEAD_DIM)]
    all_to_all x1, blocking collectives: 22.2 us -> 23.9 us  [shards(): lax.all_to_all(back, AXES, 0, 0, tiled=True, axis_index_groups=back_group...]
where the time goes in v6:
time: 79.6 us; the launch traced here: 79.1 us
  starting transfers between devices  30 us (38%)
  blocking collectives  23.9 us (30%)
  Pallas kernels  10.8 us (14%)
  waiting for transfers between devices  7.33 us (9%)
  local copies, waits for them, and re-layouts  5.47 us (7%)
  between operations  1.41 us (2%)
    all_to_all x1, blocking collectives, shards(): lax.all_to_all(back, AXES, 0, 0, tiled=True, axis_index_groups=back_group...  23.9 us
    all_to_all x1, starting transfers between devices, shards(): lax.all_to_all(packed, 'z', 0, 0, tiled=True, axis_index_groups=[OUT_PLAN...  16.4 us
    ppermute x1, starting transfers between devices, shards(): lax.ppermute(jnp.where(ready, own, jnp.zeros((), own.dtype)), 'c', [(0, 1...  7.55 us
    ppermute x1, waiting for transfers between devices, shards(): lax.ppermute(recv[:, 24:48, :], 'z', [(PLANES[3 * i + 1], PLANES[3 * i +...  4.58 us
    unnamed x10, local copies, waits for them, and re-layouts  4.43 us
    all_to_all x1, starting transfers between devices, shards(): lax.all_to_all(kv, 'x', 0, 0, tiled=True).reshape(64, KV_ROWS, HEAD_DIM)  4.01 us
    pallas_call x1, Pallas kernels, cross(): pl.pallas_call(cross_kernel, out_shape=(jax.ShapeDtypeStruct((ROWS, HEAD_...  3.88 us
    pallas_call x1, Pallas kernels, attend(): pl.pallas_call(attend_kernel, out_shape=jax.ShapeDtypeStruct((QUERIES, HE...  2.35 us
  transfers between devices with their start and end apart: 5, of which 4 were waited for; matrix products, arithmetic and copies ran while one was open for 0% of the time, Pallas kernels for 7%

profile of v6, /device:TPU:1, one launch (start us, length us, event | category | flops | bytes accessed | tf_op | source)
XLA Modules:
  0.0 79.1 jit_solution(8680467716738520651)
XLA Ops:
  0.6 2.0 %pack.1 = bf16[16,56,128]{2,1,0:T(8,128)(2,1)} custom-call(bf16[10,32,128]{2,1,0:T(8,128)(2,1)} %bitcast.38, bf16[10,32,128]{2,1,0:T(8,128)(2,1)} %bitcast.39, bf16[10,32,128]{2,1,0:T(8,128)(2,1)} %bitcast.40, bf16[10,64,128]{2,1,0:T(8,128)(2,1)} %bitcast.33), custom_call_target="tpu_custom_call" | custom-call | tf_op jit(solution)/shard_map/pack/pallas_call | solution.py:75
  2.7 16.4 %all-to-all-start = ((bf16[16,56,128]{2,1,0:T(8,128)(2,1)}), bf16[16,56,128]{2,1,0:T(8,128)(2,1)S(1)}, u32[]{:S(2)}, u32[]{:S(2)}) async-start(bf16[16,56,128]{2,1,0:T(8,128)(2,1)} %pack.1), calls=%async_computation | async-start | bytes 458752 | tf_op jit(solution)/shard_map/all_to_all | solution.py:265
  19.1 0.0 copy-start
  19.1 1.3 %copy-done = bf16[1,512,10,128]{3,1,2,0:T(8,128)(2,1)S(1)} copy-done((bf16[1,512,10,128]{3,1,2,0:T(8,128)(2,1)S(1)}, bf16[1,512,10,128]{3,1,2,0:T(8,128)(2,1)}, u32[]{:S(2)}) %copy-start) | copy-done | bytes 1310744
  20.4 0.0 copy-start.1
  20.4 1.3 %copy-done.1 = bf16[1,512,10,128]{3,1,2,0:T(8,128)(2,1)S(1)} copy-done((bf16[1,512,10,128]{3,1,2,0:T(8,128)(2,1)S(1)}, bf16[1,512,10,128]{3,1,2,0:T(8,128)(2,1)}, u32[]{:S(2)}) %copy-start.1) | copy-done | bytes 1310744
  21.8 0.0 copy-start.2
  21.8 0.9 %copy-done.2 = bf16[10,128,64]{1,2,0:T(8,128)(2,1)S(1)} copy-done((bf16[10,128,64]{1,2,0:T(8,128)(2,1)S(1)}, bf16[10,128,64]{1,2,0:T(8,128)(2,1)}, u32[]{:S(2)}) %copy-start.2) | copy-done | bytes 163864
  22.7 0.0 copy-start.3
  22.7 0.9 %copy-done.3 = bf16[1,32,10,128]{3,1,2,0:T(8,128)(2,1)S(1)} copy-done((bf16[1,32,10,128]{3,1,2,0:T(8,128)(2,1)S(1)}, bf16[1,32,10,128]{3,1,2,0:T(8,128)(2,1)}, u32[]{:S(2)}) %copy-start.3) | copy-done | bytes 81944
  23.6 3.9 %cross.1 = (f32[32,128]{1,0:T(8,128)S(1)}, s32[1]{0:T(128)}) custom-call(bf16[10,32,128]{2,1,0:T(8,128)(2,1)S(1)} %bitcast.37, bf16[10,512,128]{2,1,0:T(8,128)(2,1)S(1)} %bitcast.31, bf16[10,512,128]{2,1,0:T(8,128)(2,1)S(1)} %bitcast.32, bf16[10,64,128]{2,1,0:T(8,128)(2,1)S(1)} %bitcast.34), custom_call_target="tpu_custom_call" | custom-call | flops 90000000 | bytes 3200000 | tf_op jit(solution)/shard_map/cross/pallas_call | solution.py:116
  28.1 1.0 %all-to-all-done = bf16[16,56,128]{2,1,0:T(8,128)(2,1)S(1)} async-done(((bf16[16,56,128]{2,1,0:T(8,128)(2,1)}), bf16[16,56,128]{2,1,0:T(8,128)(2,1)S(1)}, u32[]{:S(2)}, u32[]{:S(2)}) %all-to-all-start) | async-done | bytes 229408 | tf_op jit(solution)/shard_map/all_to_all | solution.py:265
  29.1 1.0 %broadcast_in_dim.27 = bf16[4,16,48,128]{3,2,1,0:T(8,128)(2,1)} broadcast(bf16[16,48,128]{2,1,0:T(8,128)(2,1)S(1)} %slice_select_fusion), dimensions={1,2,3} | broadcast | bytes 983040 | tf_op jit(solution)/shard_map/broadcast_in_dim | solution.py:268
  30.1 4.0 %all-to-all-start.1 = ((bf16[4,16,48,128]{3,2,1,0:T(8,128)(2,1)}), bf16[4,16,48,128]{3,2,1,0:T(8,128)(2,1)S(1)}, u32[]{:S(2)}, u32[]{:S(2)}) async-start(bf16[4,16,48,128]{3,2,1,0:T(8,128)(2,1)} %broadcast_in_dim.27), calls=%async_computation.1 | async-start | bytes 1572864 | tf_op jit(solution)/shard_map/all_to_all | solution.py:269
  34.1 1.3 %collective-permute-start.1 = (bf16[16,24,128]{2,1,0:T(8,128)(2,1)S(1)}, bf16[16,24,128]{2,1,0:T(8,128)(2,1)S(1)}, u32[]{:S(2)}, u32[]{:S(2)}) collective-permute-start(bf16[16,24,128]{2,1,0:T(8,128)(2,1)S(1)} %get-tuple-element.10), channel_id=1, source_target_pairs={{192,208},{240,0},{32,48},{80,96},{128,144},{193,209},{241,1},{33,... | collective-permute-start | bytes 294920 | tf_op jit(solution)/shard_map/ppermute | solution.py:271
  35.4 0.7 collective-permute-start
  36.1 4.6 %collective-permute-done.1 = bf16[16,24,128]{2,1,0:T(8,128)(2,1)S(1)} collective-permute-done((bf16[16,24,128]{2,1,0:T(8,128)(2,1)S(1)}, bf16[16,24,128]{2,1,0:T(8,128)(2,1)S(1)}, u32[]{:S(2)}, u32[]{:S(2)}) %collective-permute-start.1) | collective-permute-done | bytes 98336 | tf_op jit(solution)/shard_map/ppermute | solution.py:271
  40.7 0.0 collective-permute-done
  40.7 1.7 %all-to-all-done.1 = bf16[4,16,48,128]{3,2,1,0:T(8,128)(2,1)S(1)} async-done(((bf16[4,16,48,128]{3,2,1,0:T(8,128)(2,1)}), bf16[4,16,48,128]{3,2,1,0:T(8,128)(2,1)S(1)}, u32[]{:S(2)}, u32[]{:S(2)}) %all-to-all-start.1) | async-done | bytes 786464 | tf_op jit(solution)/shard_map/all_to_all | solution.py:269
  42.4 0.1 broadcast_select_fusion
  42.6 7.5 %collective-permute-start.2 = (bf16[64,48,128]{2,1,0:T(8,128)(2,1)S(1)}, bf16[64,48,128]{2,1,0:T(8,128)(2,1)S(1)}, u32[]{:S(2)}, u32[]{:S(2)}) collective-permute-start(bf16[64,48,128]{2,1,0:T(8,128)(2,1)S(1)} %broadcast_select_fusion), channel_id=1, source_target_pairs={{0,2},{2,0},{1,3},{3,1},{4,6},{6,4},{5,7},{7,5},{8,10},{10,8},{9,1... | collective-permute-start | bytes 2359304 | tf_op jit(solution)/shard_map/ppermute | solution.py:276
  50.1 0.1 pad_add_fusion.where_ref
  50.2 0.0 copy-start.4
  50.2 1.7 %first_half.1 = (f32[64,512]{1,0:T(8,128)S(1)}, f32[16,512]{1,0:T(8,128)S(1)}) custom-call(bf16[16,32,128]{2,1,0:T(8,128)(2,1)S(1)} %pad_maximum_fusion.q_ref, bf16[64,48,128]{2,1,0:T(8,128)(2,1)S(1)} %bitcast.30), custom_call_target="tpu_custom_call" | custom-call | flops 540000000 | bytes 1600000 | tf_op jit(solution)/shard_map/first_half/pallas_call | solution.py:167
  51.9 0.1 collective-permute-done.2.other_ref
  52.0 2.4 %attend.1 = bf16[512,128]{1,0:T(8,128)(2,1)S(1)} custom-call(s32[4]{0:T(128)S(1)} %pad_add_fusion.where_ref, bf16[16,32,128]{2,1,0:T(8,128)(2,1)S(1)} %pad_maximum_fusion.q_ref, bf16[64,48,128]{2,1,0:T(8,128)(2,1)S(1)} %collective-permute-done.2.other_ref, f32[64,512]{1,0:T(8,128)S(1)} %get-tuple-element.7.sum_ref, f32[16,512]{1,0:T(8,128)S(1)} %get-tuple-element.8.stat_ref, ...), custom_call_target="tpu_custom_call" | custom-call | tf_op jit(solution)/shard_map/attend/pallas_call | solution.py:217
  54.4 23.9 %all_to_all.21 = bf16[64,8,128]{2,1,0:T(8,128)(2,1)S(1)} all-to-all(bf16[64,8,128]{2,1,0:T(8,128)(2,1)S(1)} %bitcast.35), channel_id=1, replica_groups={{144,145,400,401,160,161,416,417,176,177,432,433,192,193,448,449,208,20..., dimensions={0} | all-to-all | bytes 262144 | tf_op jit(solution)/shard_map/all_to_all | solution.py:281
  78.3 0.0 copy-done.4
  78.3 0.8 %finish.1 = (f32[32,32]{1,0:T(8,128)}, f32[32,32]{1,0:T(8,128)}) custom-call(bf16[512,128]{1,0:T(8,128)(2,1)S(1)} %bitcast.36, f32[32,32]{1,0:T(8,128)S(1)} %copy-done.4), custom_call_target="tpu_custom_call" | custom-call | tf_op jit(solution)/shard_map/finish/pallas_call | solution.py:239
  (6 shorter events, 0.1 us)
Async XLA Ops:
  2.7 26.4 %all-to-all-start = ((bf16[16,56,128]{2,1,0:T(8,128)(2,1)}), bf16[16,56,128]{2,1,0:T(8,128)(2,1)S(1)}, u32[]{:S(2)}, u32[]{:S(2)}) async-start(bf16[16,56,128]{2,1,0:T(8,128)(2,1)} %pack.1), calls=%async_computation | async-start | bytes 458752 | tf_op jit(solution)/shard_map/all_to_all | solution.py:265
  19.1 1.3 %copy-start = (bf16[1,512,10,128]{3,1,2,0:T(8,128)(2,1)S(1)}, bf16[1,512,10,128]{3,1,2,0:T(8,128)(2,1)}, u32[]{:S(2)}) copy-start(bf16[1,512,10,128]{3,1,2,0:T(8,128)(2,1)} %param.12) | copy-start | bytes 3932164
  20.4 1.3 %copy-start.1 = (bf16[1,512,10,128]{3,1,2,0:T(8,128)(2,1)S(1)}, bf16[1,512,10,128]{3,1,2,0:T(8,128)(2,1)}, u32[]{:S(2)}) copy-start(bf16[1,512,10,128]{3,1,2,0:T(8,128)(2,1)} %param.13) | copy-start | bytes 3932164
  21.8 0.9 %copy-start.2 = (bf16[10,128,64]{1,2,0:T(8,128)(2,1)S(1)}, bf16[10,128,64]{1,2,0:T(8,128)(2,1)}, u32[]{:S(2)}) copy-start(bf16[10,128,64]{1,2,0:T(8,128)(2,1)} %param.14) | copy-start | bytes 491524
  22.7 0.9 %copy-start.3 = (bf16[1,32,10,128]{3,1,2,0:T(8,128)(2,1)S(1)}, bf16[1,32,10,128]{3,1,2,0:T(8,128)(2,1)}, u32[]{:S(2)}) copy-start(bf16[1,32,10,128]{3,1,2,0:T(8,128)(2,1)} %param.11) | copy-start | bytes 245764
  30.1 12.4 %all-to-all-start.1 = ((bf16[4,16,48,128]{3,2,1,0:T(8,128)(2,1)}), bf16[4,16,48,128]{3,2,1,0:T(8,128)(2,1)S(1)}, u32[]{:S(2)}, u32[]{:S(2)}) async-start(bf16[4,16,48,128]{3,2,1,0:T(8,128)(2,1)} %broadcast_in_dim.27), calls=%async_computation.1 | async-start | bytes 1572864 | tf_op jit(solution)/shard_map/all_to_all | solution.py:269
  34.1 6.6 %collective-permute-start.1 = (bf16[16,24,128]{2,1,0:T(8,128)(2,1)S(1)}, bf16[16,24,128]{2,1,0:T(8,128)(2,1)S(1)}, u32[]{:S(2)}, u32[]{:S(2)}) collective-permute-start(bf16[16,24,128]{2,1,0:T(8,128)(2,1)S(1)} %get-tuple-element.10), channel_id=1, source_target_pairs={{192,208},{240,0},{32,48},{80,96},{128,144},{193,209},{241,1},{33,... | collective-permute-start | bytes 294920 | tf_op jit(solution)/shard_map/ppermute | solution.py:271
  35.4 5.3 %collective-permute-start = (bf16[16,24,128]{2,1,0:T(8,128)(2,1)S(1)}, bf16[16,24,128]{2,1,0:T(8,128)(2,1)S(1)}, u32[]{:S(2)}, u32[]{:S(2)}) collective-permute-start(bf16[16,24,128]{2,1,0:T(8,128)(2,1)S(1)} %get-tuple-element.11), channel_id=1, source_target_pairs={{192,176},{240,224},{32,16},{80,64},{128,112},{193,177},{241,225},... | collective-permute-start | bytes 294920 | tf_op jit(solution)/shard_map/ppermute | solution.py:270
  42.6 9.4 %collective-permute-start.2 = (bf16[64,48,128]{2,1,0:T(8,128)(2,1)S(1)}, bf16[64,48,128]{2,1,0:T(8,128)(2,1)S(1)}, u32[]{:S(2)}, u32[]{:S(2)}) collective-permute-start(bf16[64,48,128]{2,1,0:T(8,128)(2,1)S(1)} %broadcast_select_fusion), channel_id=1, source_target_pairs={{0,2},{2,0},{1,3},{3,1},{4,6},{6,4},{5,7},{7,5},{8,10},{10,8},{9,1... | collective-permute-start | bytes 2359304 | tf_op jit(solution)/shard_map/ppermute | solution.py:276
  50.2 28.1 %copy-start.4 = (f32[32,32]{1,0:T(8,128)S(1)}, f32[32,32]{1,0:T(8,128)}, u32[]{:S(2)}) copy-start(f32[32,32]{1,0:T(8,128)} %latent_ref.1) | copy-start | bytes 12292

commit v7 on v6

--- a/solution.py
+++ b/solution.py
@@ -264,8 +264,8 @@
     packed = pack(heads_first(queries[0]), heads_first(self_keys[0]), heads_first(self_values[0]), w)
     recv = lax.all_to_all(packed, "z", 0, 0, tiled=True, axis_index_groups=[OUT_PLANES])
     crossed, zero = cross(heads_first(cross_queries[0]), heads_first(text_keys[0]), heads_first(text_values[0]), w)
-    kv = jnp.where(zero[0] == 0, recv[:, 0:KV_ROWS, :], jnp.zeros((), recv.dtype))
-    kv = jnp.broadcast_to(kv[None], (4, SPREAD, KV_ROWS, HEAD_DIM))
+    kv = jnp.broadcast_to(recv[None, :, 0:KV_ROWS, :], (4, SPREAD, KV_ROWS, HEAD_DIM))
+    kv = jnp.where(zero[0] == 0, kv, jnp.zeros((), recv.dtype))
     own = lax.all_to_all(kv, "x", 0, 0, tiled=True).reshape(64, KV_ROWS, HEAD_DIM)
     left = lax.ppermute(recv[:, 0:24, :], "z", [(PLANES[3 * i + 1], PLANES[3 * i]) for i in range(5)])
     right = lax.ppermute(recv[:, 24:48, :], "z", [(PLANES[3 * i + 1], PLANES[3 * i + 2]) for i in range(5)])
@@ -273,7 +273,9 @@
     moved = jnp.where(lax.rem(slot, 3) == 0, left, right)
     q = jnp.concatenate([recv[:, KV_ROWS:BLOCK, :], moved], axis=1)
     ready = moved[0:1, 0:1, :] == moved[0:1, 0:1, :]
-    other = lax.ppermute(jnp.where(ready, own, jnp.zeros((), own.dtype)), "c", [(0, 1), (1, 0)])
+    tile = jnp.where(ready, own[0:1, 0:16, :], jnp.zeros((), own.dtype))
+    own = lax.dynamic_update_slice(own, tile, (0, 0, 0))
+    other = lax.ppermute(own, "c", [(0, 1), (1, 0)])
     back_slot = lax.rem(lax.axis_index("z") + (SPREAD - BACK_PLANE), SPREAD)
     where = jnp.stack([slot, lax.axis_index("cfg"), lax.rem(slot, 3), back_slot]).astype(jnp.int32)
     summed, stat = first_half(q, own)

time: 79.6 us -> 79.5 us (level)
    all_to_all x1, waiting for transfers between devices: 1.71 us -> 0.64 us  [shards(): lax.all_to_all(kv, 'x', 0, 0, tiled=True).reshape(64, KV_ROWS, HEAD_DIM)]
    ppermute x1, waiting for transfers between devices: 4.58 us -> 5.64 us  [shards(): lax.ppermute(recv[:, 24:48, :], 'z', [(PLANES[3 * i + 1], PLANES[3 * i +...]
where the time goes in v7:
time: 79.5 us; the launch traced here: 79 us
  starting transfers between devices  29.9 us (38%)
  blocking collectives  23.9 us (30%)
  Pallas kernels  10.8 us (14%)
  waiting for transfers between devices  7.32 us (9%)
  local copies, waits for them, and re-layouts  5.47 us (7%)
  between operations  1.41 us (2%)
    all_to_all x1, blocking collectives, shards(): lax.all_to_all(back, AXES, 0, 0, tiled=True, axis_index_groups=back_group...  23.9 us
    all_to_all x1, starting transfers between devices, shards(): lax.all_to_all(packed, 'z', 0, 0, tiled=True, axis_index_groups=[OUT_PLAN...  16.4 us
    ppermute x1, starting transfers between devices, shards(): other = lax.ppermute(own, 'c', [(0, 1), (1, 0)])  7.53 us
    ppermute x1, waiting for transfers between devices, shards(): lax.ppermute(recv[:, 24:48, :], 'z', [(PLANES[3 * i + 1], PLANES[3 * i +...  5.64 us
    unnamed x10, local copies, waits for them, and re-layouts  4.43 us
    all_to_all x1, starting transfers between devices, shards(): lax.all_to_all(kv, 'x', 0, 0, tiled=True).reshape(64, KV_ROWS, HEAD_DIM)  4.01 us
    pallas_call x1, Pallas kernels, cross(): pl.pallas_call(cross_kernel, out_shape=(jax.ShapeDtypeStruct((ROWS, HEAD_...  3.88 us
    pallas_call x1, Pallas kernels, attend(): pl.pallas_call(attend_kernel, out_shape=jax.ShapeDtypeStruct((QUERIES, HE...  2.35 us
  transfers between devices with their start and end apart: 5, of which 4 were waited for; matrix products, arithmetic and copies ran while one was open for 0% of the time, Pallas kernels for 7%

profile of v7, /device:TPU:1, one launch (start us, length us, event | category | flops | bytes accessed | tf_op | source)
XLA Modules:
  0.0 79.0 jit_solution(1769526722153013544)
XLA Ops:
  0.6 2.0 %pack.1 = bf16[16,56,128]{2,1,0:T(8,128)(2,1)} custom-call(bf16[10,32,128]{2,1,0:T(8,128)(2,1)} %bitcast.37, bf16[10,32,128]{2,1,0:T(8,128)(2,1)} %bitcast.38, bf16[10,32,128]{2,1,0:T(8,128)(2,1)} %bitcast.39, bf16[10,64,128]{2,1,0:T(8,128)(2,1)} %bitcast.32), custom_call_target="tpu_custom_call" | custom-call | tf_op jit(solution)/shard_map/pack/pallas_call | solution.py:75
  2.7 16.4 %all-to-all-start = ((bf16[16,56,128]{2,1,0:T(8,128)(2,1)}), bf16[16,56,128]{2,1,0:T(8,128)(2,1)S(1)}, u32[]{:S(2)}, u32[]{:S(2)}) async-start(bf16[16,56,128]{2,1,0:T(8,128)(2,1)} %pack.1), calls=%async_computation | async-start | bytes 458752 | tf_op jit(solution)/shard_map/all_to_all | solution.py:265
  19.1 0.0 copy-start
  19.1 1.3 %copy-done = bf16[1,512,10,128]{3,1,2,0:T(8,128)(2,1)S(1)} copy-done((bf16[1,512,10,128]{3,1,2,0:T(8,128)(2,1)S(1)}, bf16[1,512,10,128]{3,1,2,0:T(8,128)(2,1)}, u32[]{:S(2)}) %copy-start) | copy-done | bytes 1310744
  20.4 0.0 copy-start.1
  20.4 1.3 %copy-done.1 = bf16[1,512,10,128]{3,1,2,0:T(8,128)(2,1)S(1)} copy-done((bf16[1,512,10,128]{3,1,2,0:T(8,128)(2,1)S(1)}, bf16[1,512,10,128]{3,1,2,0:T(8,128)(2,1)}, u32[]{:S(2)}) %copy-start.1) | copy-done | bytes 1310744
  21.8 0.0 copy-start.2
  21.8 0.9 %copy-done.2 = bf16[10,128,64]{1,2,0:T(8,128)(2,1)S(1)} copy-done((bf16[10,128,64]{1,2,0:T(8,128)(2,1)S(1)}, bf16[10,128,64]{1,2,0:T(8,128)(2,1)}, u32[]{:S(2)}) %copy-start.2) | copy-done | bytes 163864
  22.7 0.0 copy-start.3
  22.7 0.9 %copy-done.3 = bf16[1,32,10,128]{3,1,2,0:T(8,128)(2,1)S(1)} copy-done((bf16[1,32,10,128]{3,1,2,0:T(8,128)(2,1)S(1)}, bf16[1,32,10,128]{3,1,2,0:T(8,128)(2,1)}, u32[]{:S(2)}) %copy-start.3) | copy-done | bytes 81944
  23.6 3.9 %cross.1 = (f32[32,128]{1,0:T(8,128)S(1)}, s32[1]{0:T(128)}) custom-call(bf16[10,32,128]{2,1,0:T(8,128)(2,1)S(1)} %bitcast.36, bf16[10,512,128]{2,1,0:T(8,128)(2,1)S(1)} %bitcast.29, bf16[10,512,128]{2,1,0:T(8,128)(2,1)S(1)} %bitcast.30, bf16[10,64,128]{2,1,0:T(8,128)(2,1)S(1)} %bitcast.33), custom_call_target="tpu_custom_call" | custom-call | flops 90000000 | bytes 3200000 | tf_op jit(solution)/shard_map/cross/pallas_call | solution.py:116
  28.1 1.0 %all-to-all-done = bf16[16,56,128]{2,1,0:T(8,128)(2,1)S(1)} async-done(((bf16[16,56,128]{2,1,0:T(8,128)(2,1)}), bf16[16,56,128]{2,1,0:T(8,128)(2,1)S(1)}, u32[]{:S(2)}, u32[]{:S(2)}) %all-to-all-start) | async-done | bytes 229408 | tf_op jit(solution)/shard_map/all_to_all | solution.py:265
  29.1 1.0 %broadcast_in_dim.25 = bf16[4,16,48,128]{3,2,1,0:T(8,128)(2,1)} broadcast(bf16[16,48,128]{2,1,0:T(8,128)(2,1)S(1)} %slice_select_fusion), dimensions={1,2,3} | broadcast | bytes 983040 | tf_op jit(solution)/shard_map/broadcast_in_dim | solution.py:267
  30.1 4.0 %all-to-all-start.1 = ((bf16[4,16,48,128]{3,2,1,0:T(8,128)(2,1)}), bf16[4,16,48,128]{3,2,1,0:T(8,128)(2,1)S(1)}, u32[]{:S(2)}, u32[]{:S(2)}) async-start(bf16[4,16,48,128]{3,2,1,0:T(8,128)(2,1)} %broadcast_in_dim.25), calls=%async_computation.1 | async-start | bytes 1572864 | tf_op jit(solution)/shard_map/all_to_all | solution.py:269
  34.1 0.7 collective-permute-start
  34.8 1.3 %collective-permute-start.1 = (bf16[16,24,128]{2,1,0:T(8,128)(2,1)S(1)}, bf16[16,24,128]{2,1,0:T(8,128)(2,1)S(1)}, u32[]{:S(2)}, u32[]{:S(2)}) collective-permute-start(bf16[16,24,128]{2,1,0:T(8,128)(2,1)S(1)} %get-tuple-element.10), channel_id=1, source_target_pairs={{192,208},{240,0},{32,48},{80,96},{128,144},{193,209},{241,1},{33,... | collective-permute-start | bytes 294920 | tf_op jit(solution)/shard_map/ppermute | solution.py:271
  36.1 0.0 collective-permute-done
  36.1 5.6 %collective-permute-done.1 = bf16[16,24,128]{2,1,0:T(8,128)(2,1)S(1)} collective-permute-done((bf16[16,24,128]{2,1,0:T(8,128)(2,1)S(1)}, bf16[16,24,128]{2,1,0:T(8,128)(2,1)S(1)}, u32[]{:S(2)}, u32[]{:S(2)}) %collective-permute-start.1) | collective-permute-done | bytes 98336 | tf_op jit(solution)/shard_map/ppermute | solution.py:271
  41.8 0.6 all-to-all-done.1
  42.5 7.5 %collective-permute-start.2 = (bf16[64,48,128]{2,1,0:T(8,128)(2,1)S(1)}, bf16[64,48,128]{2,1,0:T(8,128)(2,1)S(1)}, u32[]{:S(2)}, u32[]{:S(2)}) collective-permute-start(bf16[64,48,128]{2,1,0:T(8,128)(2,1)S(1)} %fusion.own_ref), channel_id=1, source_target_pairs={{0,2},{2,0},{1,3},{3,1},{4,6},{6,4},{5,7},{7,5},{8,10},{10,8},{9,1... | collective-permute-start | bytes 2359304 | tf_op jit(solution)/shard_map/ppermute | solution.py:278
  50.0 0.1 pad_add_fusion.where_ref
  50.1 0.0 copy-start.4
  50.1 1.7 %first_half.1 = (f32[64,512]{1,0:T(8,128)S(1)}, f32[16,512]{1,0:T(8,128)S(1)}) custom-call(bf16[16,32,128]{2,1,0:T(8,128)(2,1)S(1)} %pad_maximum_fusion.q_ref, bf16[64,48,128]{2,1,0:T(8,128)(2,1)S(1)} %fusion.own_ref), custom_call_target="tpu_custom_call" | custom-call | flops 540000000 | bytes 1600000 | tf_op jit(solution)/shard_map/first_half/pallas_call | solution.py:167
  51.8 0.1 collective-permute-done.2.other_ref
  51.9 2.4 %attend.1 = bf16[512,128]{1,0:T(8,128)(2,1)S(1)} custom-call(s32[4]{0:T(128)S(1)} %pad_add_fusion.where_ref, bf16[16,32,128]{2,1,0:T(8,128)(2,1)S(1)} %pad_maximum_fusion.q_ref, bf16[64,48,128]{2,1,0:T(8,128)(2,1)S(1)} %collective-permute-done.2.other_ref, f32[64,512]{1,0:T(8,128)S(1)} %get-tuple-element.7.sum_ref, f32[16,512]{1,0:T(8,128)S(1)} %get-tuple-element.8.stat_ref, ...), custom_call_target="tpu_custom_call" | custom-call | tf_op jit(solution)/shard_map/attend/pallas_call | solution.py:217
  54.2 23.9 %all_to_all.21 = bf16[64,8,128]{2,1,0:T(8,128)(2,1)S(1)} all-to-all(bf16[64,8,128]{2,1,0:T(8,128)(2,1)S(1)} %bitcast.34), channel_id=1, replica_groups={{144,145,400,401,160,161,416,417,176,177,432,433,192,193,448,449,208,20..., dimensions={0} | all-to-all | bytes 262144 | tf_op jit(solution)/shard_map/all_to_all | solution.py:283
  78.2 0.0 copy-done.4
  78.2 0.8 %finish.1 = (f32[32,32]{1,0:T(8,128)}, f32[32,32]{1,0:T(8,128)}) custom-call(bf16[512,128]{1,0:T(8,128)(2,1)S(1)} %bitcast.35, f32[32,32]{1,0:T(8,128)S(1)} %copy-done.4), custom_call_target="tpu_custom_call" | custom-call | tf_op jit(solution)/shard_map/finish/pallas_call | solution.py:239
  (7 shorter events, 0.1 us)
Async XLA Ops:
  2.7 26.4 %all-to-all-start = ((bf16[16,56,128]{2,1,0:T(8,128)(2,1)}), bf16[16,56,128]{2,1,0:T(8,128)(2,1)S(1)}, u32[]{:S(2)}, u32[]{:S(2)}) async-start(bf16[16,56,128]{2,1,0:T(8,128)(2,1)} %pack.1), calls=%async_computation | async-start | bytes 458752 | tf_op jit(solution)/shard_map/all_to_all | solution.py:265
  19.1 1.3 %copy-start = (bf16[1,512,10,128]{3,1,2,0:T(8,128)(2,1)S(1)}, bf16[1,512,10,128]{3,1,2,0:T(8,128)(2,1)}, u32[]{:S(2)}) copy-start(bf16[1,512,10,128]{3,1,2,0:T(8,128)(2,1)} %param.12) | copy-start | bytes 3932164
  20.4 1.3 %copy-start.1 = (bf16[1,512,10,128]{3,1,2,0:T(8,128)(2,1)S(1)}, bf16[1,512,10,128]{3,1,2,0:T(8,128)(2,1)}, u32[]{:S(2)}) copy-start(bf16[1,512,10,128]{3,1,2,0:T(8,128)(2,1)} %param.13) | copy-start | bytes 3932164
  21.8 0.9 %copy-start.2 = (bf16[10,128,64]{1,2,0:T(8,128)(2,1)S(1)}, bf16[10,128,64]{1,2,0:T(8,128)(2,1)}, u32[]{:S(2)}) copy-start(bf16[10,128,64]{1,2,0:T(8,128)(2,1)} %param.14) | copy-start | bytes 491524
  22.7 0.9 %copy-start.3 = (bf16[1,32,10,128]{3,1,2,0:T(8,128)(2,1)S(1)}, bf16[1,32,10,128]{3,1,2,0:T(8,128)(2,1)}, u32[]{:S(2)}) copy-start(bf16[1,32,10,128]{3,1,2,0:T(8,128)(2,1)} %param.11) | copy-start | bytes 245764
  30.1 12.4 %all-to-all-start.1 = ((bf16[4,16,48,128]{3,2,1,0:T(8,128)(2,1)}), bf16[4,16,48,128]{3,2,1,0:T(8,128)(2,1)S(1)}, u32[]{:S(2)}, u32[]{:S(2)}) async-start(bf16[4,16,48,128]{3,2,1,0:T(8,128)(2,1)} %broadcast_in_dim.25), calls=%async_computation.1 | async-start | bytes 1572864 | tf_op jit(solution)/shard_map/all_to_all | solution.py:269
  34.1 2.0 %collective-permute-start = (bf16[16,24,128]{2,1,0:T(8,128)(2,1)S(1)}, bf16[16,24,128]{2,1,0:T(8,128)(2,1)S(1)}, u32[]{:S(2)}, u32[]{:S(2)}) collective-permute-start(bf16[16,24,128]{2,1,0:T(8,128)(2,1)S(1)} %get-tuple-element.11), channel_id=1, source_target_pairs={{192,176},{240,224},{32,16},{80,64},{128,112},{193,177},{241,225},... | collective-permute-start | bytes 294920 | tf_op jit(solution)/shard_map/ppermute | solution.py:270
  34.8 7.0 %collective-permute-start.1 = (bf16[16,24,128]{2,1,0:T(8,128)(2,1)S(1)}, bf16[16,24,128]{2,1,0:T(8,128)(2,1)S(1)}, u32[]{:S(2)}, u32[]{:S(2)}) collective-permute-start(bf16[16,24,128]{2,1,0:T(8,128)(2,1)S(1)} %get-tuple-element.10), channel_id=1, source_target_pairs={{192,208},{240,0},{32,48},{80,96},{128,144},{193,209},{241,1},{33,... | collective-permute-start | bytes 294920 | tf_op jit(solution)/shard_map/ppermute | solution.py:271
  42.5 9.4 %collective-permute-start.2 = (bf16[64,48,128]{2,1,0:T(8,128)(2,1)S(1)}, bf16[64,48,128]{2,1,0:T(8,128)(2,1)S(1)}, u32[]{:S(2)}, u32[]{:S(2)}) collective-permute-start(bf16[64,48,128]{2,1,0:T(8,128)(2,1)S(1)} %fusion.own_ref), channel_id=1, source_target_pairs={{0,2},{2,0},{1,3},{3,1},{4,6},{6,4},{5,7},{7,5},{8,10},{10,8},{9,1... | collective-permute-start | bytes 2359304 | tf_op jit(solution)/shard_map/ppermute | solution.py:278
  50.1 28.1 %copy-start.4 = (f32[32,32]{1,0:T(8,128)S(1)}, f32[32,32]{1,0:T(8,128)}, u32[]{:S(2)}) copy-start(f32[32,32]{1,0:T(8,128)} %latent_ref.1) | copy-start | bytes 12292

commit v8 on v7

--- a/solution.py
+++ b/solution.py
@@ -18,7 +18,7 @@
 BACK_PLANE = 9
 PLANES = [(FIRST_PLANE + i) % SPREAD for i in range(SPREAD)]
 BACK_PLANES = [(BACK_PLANE + i) % SPREAD for i in range(SPREAD)]
-OUT_PLANES = [11, 12, 10, 13, 9, 14, 8, 15, 7, 0, 6, 1, 5, 2, 4, 3]
+OUT_PLANES = [11, 12, 10, 13, 9, 8, 7, 6, 5, 4, 3, 2, 1, 0, 15, 14]
 AXES = ("cfg", "z", "x", "c", "head")
 GUIDANCE = 5.0
 STEP = 0.1

time: 79.5 us -> 79.5 us (level)
  waiting for transfers between devices: 7.32 us -> 11.2 us
  starting transfers between devices: 29.9 us -> 27.8 us
  blocking collectives: 23.9 us -> 22.2 us
    all_to_all x1, waiting for transfers between devices: 0.96 us -> 3.5 us  [shards(): lax.all_to_all(packed, 'z', 0, 0, tiled=True, axis_index_groups=[OUT_PLAN...]
    ppermute x1, starting transfers between devices: 7.53 us -> 5.42 us  [shards(): other = lax.ppermute(own, 'c', [(0, 1), (1, 0)])]
    all_to_all x1, blocking collectives: 23.9 us -> 22.2 us  [shards(): lax.all_to_all(back, AXES, 0, 0, tiled=True, axis_index_groups=back_group...]
    all_to_all x1, waiting for transfers between devices: 0.64 us -> 2.13 us  [shards(): lax.all_to_all(kv, 'x', 0, 0, tiled=True).reshape(64, KV_ROWS, HEAD_DIM)]
where the time goes in v8:
time: 79.5 us; the launch traced here: 79.1 us
  starting transfers between devices  27.8 us (35%)
  blocking collectives  22.2 us (28%)
  waiting for transfers between devices  11.2 us (14%)
  Pallas kernels  10.8 us (14%)
  local copies, waits for them, and re-layouts  5.47 us (7%)
  between operations  1.41 us (2%)
    all_to_all x1, blocking collectives, shards(): lax.all_to_all(back, AXES, 0, 0, tiled=True, axis_index_groups=back_group...  22.2 us
    all_to_all x1, starting transfers between devices, shards(): lax.all_to_all(packed, 'z', 0, 0, tiled=True, axis_index_groups=[OUT_PLAN...  16.4 us
    ppermute x1, waiting for transfers between devices, shards(): lax.ppermute(recv[:, 24:48, :], 'z', [(PLANES[3 * i + 1], PLANES[3 * i +...  5.54 us
    ppermute x1, starting transfers between devices, shards(): other = lax.ppermute(own, 'c', [(0, 1), (1, 0)])  5.42 us
    unnamed x10, local copies, waits for them, and re-layouts  4.43 us
    all_to_all x1, starting transfers between devices, shards(): lax.all_to_all(kv, 'x', 0, 0, tiled=True).reshape(64, KV_ROWS, HEAD_DIM)  4.01 us
    pallas_call x1, Pallas kernels, cross(): pl.pallas_call(cross_kernel, out_shape=(jax.ShapeDtypeStruct((ROWS, HEAD_...  3.88 us
    all_to_all x1, waiting for transfers between devices, shards(): lax.all_to_all(packed, 'z', 0, 0, tiled=True, axis_index_groups=[OUT_PLAN...  3.5 us
  transfers between devices with their start and end apart: 5, of which 4 were waited for; matrix products, arithmetic and copies ran while one was open for 0% of the time, Pallas kernels for 7%

profile of v8, /device:TPU:1, one launch (start us, length us, event | category | flops | bytes accessed | tf_op | source)
XLA Modules:
  0.0 79.1 jit_solution(12680981819061787713)
XLA Ops:
  0.6 2.0 %pack.1 = bf16[16,56,128]{2,1,0:T(8,128)(2,1)} custom-call(bf16[10,32,128]{2,1,0:T(8,128)(2,1)} %bitcast.37, bf16[10,32,128]{2,1,0:T(8,128)(2,1)} %bitcast.38, bf16[10,32,128]{2,1,0:T(8,128)(2,1)} %bitcast.39, bf16[10,64,128]{2,1,0:T(8,128)(2,1)} %bitcast.32), custom_call_target="tpu_custom_call" | custom-call | tf_op jit(solution)/shard_map/pack/pallas_call | solution.py:75
  2.7 16.4 %all-to-all-start = ((bf16[16,56,128]{2,1,0:T(8,128)(2,1)}), bf16[16,56,128]{2,1,0:T(8,128)(2,1)S(1)}, u32[]{:S(2)}, u32[]{:S(2)}) async-start(bf16[16,56,128]{2,1,0:T(8,128)(2,1)} %pack.1), calls=%async_computation | async-start | bytes 458752 | tf_op jit(solution)/shard_map/all_to_all | solution.py:265
  19.1 0.0 copy-start
  19.1 1.3 %copy-done = bf16[1,512,10,128]{3,1,2,0:T(8,128)(2,1)S(1)} copy-done((bf16[1,512,10,128]{3,1,2,0:T(8,128)(2,1)S(1)}, bf16[1,512,10,128]{3,1,2,0:T(8,128)(2,1)}, u32[]{:S(2)}) %copy-start) | copy-done | bytes 1310744
  20.4 0.0 copy-start.1
  20.4 1.3 %copy-done.1 = bf16[1,512,10,128]{3,1,2,0:T(8,128)(2,1)S(1)} copy-done((bf16[1,512,10,128]{3,1,2,0:T(8,128)(2,1)S(1)}, bf16[1,512,10,128]{3,1,2,0:T(8,128)(2,1)}, u32[]{:S(2)}) %copy-start.1) | copy-done | bytes 1310744
  21.8 0.0 copy-start.2
  21.8 0.9 %copy-done.2 = bf16[10,128,64]{1,2,0:T(8,128)(2,1)S(1)} copy-done((bf16[10,128,64]{1,2,0:T(8,128)(2,1)S(1)}, bf16[10,128,64]{1,2,0:T(8,128)(2,1)}, u32[]{:S(2)}) %copy-start.2) | copy-done | bytes 163864
  22.7 0.0 copy-start.3
  22.7 0.9 %copy-done.3 = bf16[1,32,10,128]{3,1,2,0:T(8,128)(2,1)S(1)} copy-done((bf16[1,32,10,128]{3,1,2,0:T(8,128)(2,1)S(1)}, bf16[1,32,10,128]{3,1,2,0:T(8,128)(2,1)}, u32[]{:S(2)}) %copy-start.3) | copy-done | bytes 81944
  23.6 3.9 %cross.1 = (f32[32,128]{1,0:T(8,128)S(1)}, s32[1]{0:T(128)}) custom-call(bf16[10,32,128]{2,1,0:T(8,128)(2,1)S(1)} %bitcast.36, bf16[10,512,128]{2,1,0:T(8,128)(2,1)S(1)} %bitcast.29, bf16[10,512,128]{2,1,0:T(8,128)(2,1)S(1)} %bitcast.30, bf16[10,64,128]{2,1,0:T(8,128)(2,1)S(1)} %bitcast.33), custom_call_target="tpu_custom_call" | custom-call | flops 90000000 | bytes 3200000 | tf_op jit(solution)/shard_map/cross/pallas_call | solution.py:116
  28.1 3.5 %all-to-all-done = bf16[16,56,128]{2,1,0:T(8,128)(2,1)S(1)} async-done(((bf16[16,56,128]{2,1,0:T(8,128)(2,1)}), bf16[16,56,128]{2,1,0:T(8,128)(2,1)S(1)}, u32[]{:S(2)}, u32[]{:S(2)}) %all-to-all-start) | async-done | bytes 229408 | tf_op jit(solution)/shard_map/all_to_all | solution.py:265
  31.6 1.0 %broadcast_in_dim.25 = bf16[4,16,48,128]{3,2,1,0:T(8,128)(2,1)} broadcast(bf16[16,48,128]{2,1,0:T(8,128)(2,1)S(1)} %slice_select_fusion), dimensions={1,2,3} | broadcast | bytes 983040 | tf_op jit(solution)/shard_map/broadcast_in_dim | solution.py:267
  32.6 4.0 %all-to-all-start.1 = ((bf16[4,16,48,128]{3,2,1,0:T(8,128)(2,1)}), bf16[4,16,48,128]{3,2,1,0:T(8,128)(2,1)S(1)}, u32[]{:S(2)}, u32[]{:S(2)}) async-start(bf16[4,16,48,128]{3,2,1,0:T(8,128)(2,1)} %broadcast_in_dim.25), calls=%async_computation.1 | async-start | bytes 1572864 | tf_op jit(solution)/shard_map/all_to_all | solution.py:269
  36.7 0.7 collective-permute-start
  37.3 1.3 %collective-permute-start.1 = (bf16[16,24,128]{2,1,0:T(8,128)(2,1)S(1)}, bf16[16,24,128]{2,1,0:T(8,128)(2,1)S(1)}, u32[]{:S(2)}, u32[]{:S(2)}) collective-permute-start(bf16[16,24,128]{2,1,0:T(8,128)(2,1)S(1)} %get-tuple-element.10), channel_id=1, source_target_pairs={{192,208},{240,0},{32,48},{80,96},{128,144},{193,209},{241,1},{33,... | collective-permute-start | bytes 294920 | tf_op jit(solution)/shard_map/ppermute | solution.py:271
  38.7 0.0 collective-permute-done
  38.7 5.5 %collective-permute-done.1 = bf16[16,24,128]{2,1,0:T(8,128)(2,1)S(1)} collective-permute-done((bf16[16,24,128]{2,1,0:T(8,128)(2,1)S(1)}, bf16[16,24,128]{2,1,0:T(8,128)(2,1)S(1)}, u32[]{:S(2)}, u32[]{:S(2)}) %collective-permute-start.1) | collective-permute-done | bytes 98336 | tf_op jit(solution)/shard_map/ppermute | solution.py:271
  44.2 2.1 %all-to-all-done.1 = bf16[4,16,48,128]{3,2,1,0:T(8,128)(2,1)S(1)} async-done(((bf16[4,16,48,128]{3,2,1,0:T(8,128)(2,1)}), bf16[4,16,48,128]{3,2,1,0:T(8,128)(2,1)S(1)}, u32[]{:S(2)}, u32[]{:S(2)}) %all-to-all-start.1) | async-done | bytes 786464 | tf_op jit(solution)/shard_map/all_to_all | solution.py:269
  46.4 5.4 %collective-permute-start.2 = (bf16[64,48,128]{2,1,0:T(8,128)(2,1)S(1)}, bf16[64,48,128]{2,1,0:T(8,128)(2,1)S(1)}, u32[]{:S(2)}, u32[]{:S(2)}) collective-permute-start(bf16[64,48,128]{2,1,0:T(8,128)(2,1)S(1)} %fusion.own_ref), channel_id=1, source_target_pairs={{0,2},{2,0},{1,3},{3,1},{4,6},{6,4},{5,7},{7,5},{8,10},{10,8},{9,1... | collective-permute-start | bytes 2359304 | tf_op jit(solution)/shard_map/ppermute | solution.py:278
  51.8 0.1 pad_add_fusion.where_ref
  51.9 0.0 copy-start.4
  51.9 1.7 %first_half.1 = (f32[64,512]{1,0:T(8,128)S(1)}, f32[16,512]{1,0:T(8,128)S(1)}) custom-call(bf16[16,32,128]{2,1,0:T(8,128)(2,1)S(1)} %pad_maximum_fusion.q_ref, bf16[64,48,128]{2,1,0:T(8,128)(2,1)S(1)} %fusion.own_ref), custom_call_target="tpu_custom_call" | custom-call | flops 540000000 | bytes 1600000 | tf_op jit(solution)/shard_map/first_half/pallas_call | solution.py:167
  53.6 0.1 collective-permute-done.2.other_ref
  53.7 2.4 %attend.1 = bf16[512,128]{1,0:T(8,128)(2,1)S(1)} custom-call(s32[4]{0:T(128)S(1)} %pad_add_fusion.where_ref, bf16[16,32,128]{2,1,0:T(8,128)(2,1)S(1)} %pad_maximum_fusion.q_ref, bf16[64,48,128]{2,1,0:T(8,128)(2,1)S(1)} %collective-permute-done.2.other_ref, f32[64,512]{1,0:T(8,128)S(1)} %get-tuple-element.7.sum_ref, f32[16,512]{1,0:T(8,128)S(1)} %get-tuple-element.8.stat_ref, ...), custom_call_target="tpu_custom_call" | custom-call | tf_op jit(solution)/shard_map/attend/pallas_call | solution.py:217
  56.1 22.2 %all_to_all.21 = bf16[64,8,128]{2,1,0:T(8,128)(2,1)S(1)} all-to-all(bf16[64,8,128]{2,1,0:T(8,128)(2,1)S(1)} %bitcast.34), channel_id=1, replica_groups={{144,145,400,401,160,161,416,417,176,177,432,433,192,193,448,449,208,20..., dimensions={0} | all-to-all | bytes 262144 | tf_op jit(solution)/shard_map/all_to_all | solution.py:283
  78.2 0.0 copy-done.4
  78.2 0.8 %finish.1 = (f32[32,32]{1,0:T(8,128)}, f32[32,32]{1,0:T(8,128)}) custom-call(bf16[512,128]{1,0:T(8,128)(2,1)S(1)} %bitcast.35, f32[32,32]{1,0:T(8,128)S(1)} %copy-done.4), custom_call_target="tpu_custom_call" | custom-call | tf_op jit(solution)/shard_map/finish/pallas_call | solution.py:239
  (7 shorter events, 0.1 us)
Async XLA Ops:
  2.7 28.9 %all-to-all-start = ((bf16[16,56,128]{2,1,0:T(8,128)(2,1)}), bf16[16,56,128]{2,1,0:T(8,128)(2,1)S(1)}, u32[]{:S(2)}, u32[]{:S(2)}) async-start(bf16[16,56,128]{2,1,0:T(8,128)(2,1)} %pack.1), calls=%async_computation | async-start | bytes 458752 | tf_op jit(solution)/shard_map/all_to_all | solution.py:265
  19.1 1.3 %copy-start = (bf16[1,512,10,128]{3,1,2,0:T(8,128)(2,1)S(1)}, bf16[1,512,10,128]{3,1,2,0:T(8,128)(2,1)}, u32[]{:S(2)}) copy-start(bf16[1,512,10,128]{3,1,2,0:T(8,128)(2,1)} %param.12) | copy-start | bytes 3932164
  20.4 1.3 %copy-start.1 = (bf16[1,512,10,128]{3,1,2,0:T(8,128)(2,1)S(1)}, bf16[1,512,10,128]{3,1,2,0:T(8,128)(2,1)}, u32[]{:S(2)}) copy-start(bf16[1,512,10,128]{3,1,2,0:T(8,128)(2,1)} %param.13) | copy-start | bytes 3932164
  21.8 0.9 %copy-start.2 = (bf16[10,128,64]{1,2,0:T(8,128)(2,1)S(1)}, bf16[10,128,64]{1,2,0:T(8,128)(2,1)}, u32[]{:S(2)}) copy-start(bf16[10,128,64]{1,2,0:T(8,128)(2,1)} %param.14) | copy-start | bytes 491524
  22.7 0.9 %copy-start.3 = (bf16[1,32,10,128]{3,1,2,0:T(8,128)(2,1)S(1)}, bf16[1,32,10,128]{3,1,2,0:T(8,128)(2,1)}, u32[]{:S(2)}) copy-start(bf16[1,32,10,128]{3,1,2,0:T(8,128)(2,1)} %param.11) | copy-start | bytes 245764
  32.6 13.7 %all-to-all-start.1 = ((bf16[4,16,48,128]{3,2,1,0:T(8,128)(2,1)}), bf16[4,16,48,128]{3,2,1,0:T(8,128)(2,1)S(1)}, u32[]{:S(2)}, u32[]{:S(2)}) async-start(bf16[4,16,48,128]{3,2,1,0:T(8,128)(2,1)} %broadcast_in_dim.25), calls=%async_computation.1 | async-start | bytes 1572864 | tf_op jit(solution)/shard_map/all_to_all | solution.py:269
  36.7 2.0 %collective-permute-start = (bf16[16,24,128]{2,1,0:T(8,128)(2,1)S(1)}, bf16[16,24,128]{2,1,0:T(8,128)(2,1)S(1)}, u32[]{:S(2)}, u32[]{:S(2)}) collective-permute-start(bf16[16,24,128]{2,1,0:T(8,128)(2,1)S(1)} %get-tuple-element.11), channel_id=1, source_target_pairs={{192,176},{240,224},{32,16},{80,64},{128,112},{193,177},{241,225},... | collective-permute-start | bytes 294920 | tf_op jit(solution)/shard_map/ppermute | solution.py:270
  37.3 6.9 %collective-permute-start.1 = (bf16[16,24,128]{2,1,0:T(8,128)(2,1)S(1)}, bf16[16,24,128]{2,1,0:T(8,128)(2,1)S(1)}, u32[]{:S(2)}, u32[]{:S(2)}) collective-permute-start(bf16[16,24,128]{2,1,0:T(8,128)(2,1)S(1)} %get-tuple-element.10), channel_id=1, source_target_pairs={{192,208},{240,0},{32,48},{80,96},{128,144},{193,209},{241,1},{33,... | collective-permute-start | bytes 294920 | tf_op jit(solution)/shard_map/ppermute | solution.py:271
  46.4 7.3 %collective-permute-start.2 = (bf16[64,48,128]{2,1,0:T(8,128)(2,1)S(1)}, bf16[64,48,128]{2,1,0:T(8,128)(2,1)S(1)}, u32[]{:S(2)}, u32[]{:S(2)}) collective-permute-start(bf16[64,48,128]{2,1,0:T(8,128)(2,1)S(1)} %fusion.own_ref), channel_id=1, source_target_pairs={{0,2},{2,0},{1,3},{3,1},{4,6},{6,4},{5,7},{7,5},{8,10},{10,8},{9,1... | collective-permute-start | bytes 2359304 | tf_op jit(solution)/shard_map/ppermute | solution.py:278
  51.9 26.3 %copy-start.4 = (f32[32,32]{1,0:T(8,128)S(1)}, f32[32,32]{1,0:T(8,128)}, u32[]{:S(2)}) copy-start(f32[32,32]{1,0:T(8,128)} %latent_ref.1) | copy-start | bytes 12292

commit v9 on v8

--- a/solution.py
+++ b/solution.py
@@ -18,7 +18,7 @@
 BACK_PLANE = 9
 PLANES = [(FIRST_PLANE + i) % SPREAD for i in range(SPREAD)]
 BACK_PLANES = [(BACK_PLANE + i) % SPREAD for i in range(SPREAD)]
-OUT_PLANES = [11, 12, 10, 13, 9, 8, 7, 6, 5, 4, 3, 2, 1, 0, 15, 14]
+OUT_PLANES = [10, 9, 11, 8, 12, 7, 13, 6, 14, 5, 15, 4, 0, 3, 1, 2]
 AXES = ("cfg", "z", "x", "c", "head")
 GUIDANCE = 5.0
 STEP = 0.1

time: 79.5 us -> 79.8 us (level)
  waiting for transfers between devices: 11.2 us -> 7.93 us
  starting transfers between devices: 27.8 us -> 30.4 us
  blocking collectives: 22.2 us -> 23.1 us
    all_to_all x1, waiting for transfers between devices: 3.5 us -> 1.23 us  [shards(): lax.all_to_all(packed, 'z', 0, 0, tiled=True, axis_index_groups=[OUT_PLAN...]
    ppermute x1, starting transfers between devices: 5.42 us -> 7.05 us  [shards(): other = lax.ppermute(own, 'c', [(0, 1), (1, 0)])]
    all_to_all x1, blocking collectives: 22.2 us -> 23.1 us  [shards(): lax.all_to_all(back, AXES, 0, 0, tiled=True, axis_index_groups=back_group...]
    all_to_all x1, starting transfers between devices: 16.4 us -> 17.3 us  [shards(): lax.all_to_all(packed, 'z', 0, 0, tiled=True, axis_index_groups=[OUT_PLAN...]
where the time goes in v9:
time: 79.8 us; the launch traced here: 79.2 us
  starting transfers between devices  30.4 us (38%)
  blocking collectives  23.1 us (29%)
  Pallas kernels  10.8 us (14%)
  waiting for transfers between devices  7.93 us (10%)
  local copies, waits for them, and re-layouts  5.47 us (7%)
  between operations  1.41 us (2%)
    all_to_all x1, blocking collectives, shards(): lax.all_to_all(back, AXES, 0, 0, tiled=True, axis_index_groups=back_group...  23.1 us
    all_to_all x1, starting transfers between devices, shards(): lax.all_to_all(packed, 'z', 0, 0, tiled=True, axis_index_groups=[OUT_PLAN...  17.3 us
    ppermute x1, starting transfers between devices, shards(): other = lax.ppermute(own, 'c', [(0, 1), (1, 0)])  7.05 us
    ppermute x1, waiting for transfers between devices, shards(): lax.ppermute(recv[:, 24:48, :], 'z', [(PLANES[3 * i + 1], PLANES[3 * i +...  5.24 us
    unnamed x10, local copies, waits for them, and re-layouts  4.43 us
    all_to_all x1, starting transfers between devices, shards(): lax.all_to_all(kv, 'x', 0, 0, tiled=True).reshape(64, KV_ROWS, HEAD_DIM)  4.01 us
    pallas_call x1, Pallas kernels, cross(): pl.pallas_call(cross_kernel, out_shape=(jax.ShapeDtypeStruct((ROWS, HEAD_...  3.88 us
    pallas_call x1, Pallas kernels, attend(): pl.pallas_call(attend_kernel, out_shape=jax.ShapeDtypeStruct((QUERIES, HE...  2.35 us
  transfers between devices with their start and end apart: 5, of which 4 were waited for; matrix products, arithmetic and copies ran while one was open for 0% of the time, Pallas kernels for 7%

profile of v9, /device:TPU:1, one launch (start us, length us, event | category | flops | bytes accessed | tf_op | source)
XLA Modules:
  0.0 79.2 jit_solution(9480754942298334483)
XLA Ops:
  0.6 2.0 %pack.1 = bf16[16,56,128]{2,1,0:T(8,128)(2,1)} custom-call(bf16[10,32,128]{2,1,0:T(8,128)(2,1)} %bitcast.37, bf16[10,32,128]{2,1,0:T(8,128)(2,1)} %bitcast.38, bf16[10,32,128]{2,1,0:T(8,128)(2,1)} %bitcast.39, bf16[10,64,128]{2,1,0:T(8,128)(2,1)} %bitcast.32), custom_call_target="tpu_custom_call" | custom-call | tf_op jit(solution)/shard_map/pack/pallas_call | solution.py:75
  2.7 17.3 %all-to-all-start = ((bf16[16,56,128]{2,1,0:T(8,128)(2,1)}), bf16[16,56,128]{2,1,0:T(8,128)(2,1)S(1)}, u32[]{:S(2)}, u32[]{:S(2)}) async-start(bf16[16,56,128]{2,1,0:T(8,128)(2,1)} %pack.1), calls=%async_computation | async-start | bytes 458752 | tf_op jit(solution)/shard_map/all_to_all | solution.py:265
  20.0 0.0 copy-start
  20.0 1.3 %copy-done = bf16[1,512,10,128]{3,1,2,0:T(8,128)(2,1)S(1)} copy-done((bf16[1,512,10,128]{3,1,2,0:T(8,128)(2,1)S(1)}, bf16[1,512,10,128]{3,1,2,0:T(8,128)(2,1)}, u32[]{:S(2)}) %copy-start) | copy-done | bytes 1310744
  21.3 0.0 copy-start.1
  21.3 1.3 %copy-done.1 = bf16[1,512,10,128]{3,1,2,0:T(8,128)(2,1)S(1)} copy-done((bf16[1,512,10,128]{3,1,2,0:T(8,128)(2,1)S(1)}, bf16[1,512,10,128]{3,1,2,0:T(8,128)(2,1)}, u32[]{:S(2)}) %copy-start.1) | copy-done | bytes 1310744
  22.7 0.0 copy-start.2
  22.7 0.9 %copy-done.2 = bf16[10,128,64]{1,2,0:T(8,128)(2,1)S(1)} copy-done((bf16[10,128,64]{1,2,0:T(8,128)(2,1)S(1)}, bf16[10,128,64]{1,2,0:T(8,128)(2,1)}, u32[]{:S(2)}) %copy-start.2) | copy-done | bytes 163864
  23.6 0.0 copy-start.3
  23.6 0.9 %copy-done.3 = bf16[1,32,10,128]{3,1,2,0:T(8,128)(2,1)S(1)} copy-done((bf16[1,32,10,128]{3,1,2,0:T(8,128)(2,1)S(1)}, bf16[1,32,10,128]{3,1,2,0:T(8,128)(2,1)}, u32[]{:S(2)}) %copy-start.3) | copy-done | bytes 81944
  24.5 3.9 %cross.1 = (f32[32,128]{1,0:T(8,128)S(1)}, s32[1]{0:T(128)}) custom-call(bf16[10,32,128]{2,1,0:T(8,128)(2,1)S(1)} %bitcast.36, bf16[10,512,128]{2,1,0:T(8,128)(2,1)S(1)} %bitcast.29, bf16[10,512,128]{2,1,0:T(8,128)(2,1)S(1)} %bitcast.30, bf16[10,64,128]{2,1,0:T(8,128)(2,1)S(1)} %bitcast.33), custom_call_target="tpu_custom_call" | custom-call | flops 90000000 | bytes 3200000 | tf_op jit(solution)/shard_map/cross/pallas_call | solution.py:116
  29.0 1.2 %all-to-all-done = bf16[16,56,128]{2,1,0:T(8,128)(2,1)S(1)} async-done(((bf16[16,56,128]{2,1,0:T(8,128)(2,1)}), bf16[16,56,128]{2,1,0:T(8,128)(2,1)S(1)}, u32[]{:S(2)}, u32[]{:S(2)}) %all-to-all-start) | async-done | bytes 229408 | tf_op jit(solution)/shard_map/all_to_all | solution.py:265
  30.2 1.0 %broadcast_in_dim.25 = bf16[4,16,48,128]{3,2,1,0:T(8,128)(2,1)} broadcast(bf16[16,48,128]{2,1,0:T(8,128)(2,1)S(1)} %slice_select_fusion), dimensions={1,2,3} | broadcast | bytes 983040 | tf_op jit(solution)/shard_map/broadcast_in_dim | solution.py:267
  31.3 4.0 %all-to-all-start.1 = ((bf16[4,16,48,128]{3,2,1,0:T(8,128)(2,1)}), bf16[4,16,48,128]{3,2,1,0:T(8,128)(2,1)S(1)}, u32[]{:S(2)}, u32[]{:S(2)}) async-start(bf16[4,16,48,128]{3,2,1,0:T(8,128)(2,1)} %broadcast_in_dim.25), calls=%async_computation.1 | async-start | bytes 1572864 | tf_op jit(solution)/shard_map/all_to_all | solution.py:269
  35.3 0.7 collective-permute-start
  36.0 1.3 %collective-permute-start.1 = (bf16[16,24,128]{2,1,0:T(8,128)(2,1)S(1)}, bf16[16,24,128]{2,1,0:T(8,128)(2,1)S(1)}, u32[]{:S(2)}, u32[]{:S(2)}) collective-permute-start(bf16[16,24,128]{2,1,0:T(8,128)(2,1)S(1)} %get-tuple-element.10), channel_id=1, source_target_pairs={{192,208},{240,0},{32,48},{80,96},{128,144},{193,209},{241,1},{33,... | collective-permute-start | bytes 294920 | tf_op jit(solution)/shard_map/ppermute | solution.py:271
  37.3 0.0 collective-permute-done
  37.3 5.2 %collective-permute-done.1 = bf16[16,24,128]{2,1,0:T(8,128)(2,1)S(1)} collective-permute-done((bf16[16,24,128]{2,1,0:T(8,128)(2,1)S(1)}, bf16[16,24,128]{2,1,0:T(8,128)(2,1)S(1)}, u32[]{:S(2)}, u32[]{:S(2)}) %collective-permute-start.1) | collective-permute-done | bytes 98336 | tf_op jit(solution)/shard_map/ppermute | solution.py:271
  42.6 1.4 %all-to-all-done.1 = bf16[4,16,48,128]{3,2,1,0:T(8,128)(2,1)S(1)} async-done(((bf16[4,16,48,128]{3,2,1,0:T(8,128)(2,1)}), bf16[4,16,48,128]{3,2,1,0:T(8,128)(2,1)S(1)}, u32[]{:S(2)}, u32[]{:S(2)}) %all-to-all-start.1) | async-done | bytes 786464 | tf_op jit(solution)/shard_map/all_to_all | solution.py:269
  44.0 7.1 %collective-permute-start.2 = (bf16[64,48,128]{2,1,0:T(8,128)(2,1)S(1)}, bf16[64,48,128]{2,1,0:T(8,128)(2,1)S(1)}, u32[]{:S(2)}, u32[]{:S(2)}) collective-permute-start(bf16[64,48,128]{2,1,0:T(8,128)(2,1)S(1)} %fusion.own_ref), channel_id=1, source_target_pairs={{0,2},{2,0},{1,3},{3,1},{4,6},{6,4},{5,7},{7,5},{8,10},{10,8},{9,1... | collective-permute-start | bytes 2359304 | tf_op jit(solution)/shard_map/ppermute | solution.py:278
  51.0 0.1 pad_add_fusion.where_ref
  51.1 0.0 copy-start.4
  51.1 1.7 %first_half.1 = (f32[64,512]{1,0:T(8,128)S(1)}, f32[16,512]{1,0:T(8,128)S(1)}) custom-call(bf16[16,32,128]{2,1,0:T(8,128)(2,1)S(1)} %pad_maximum_fusion.q_ref, bf16[64,48,128]{2,1,0:T(8,128)(2,1)S(1)} %fusion.own_ref), custom_call_target="tpu_custom_call" | custom-call | flops 540000000 | bytes 1600000 | tf_op jit(solution)/shard_map/first_half/pallas_call | solution.py:167
  52.8 0.1 collective-permute-done.2.other_ref
  52.9 2.4 %attend.1 = bf16[512,128]{1,0:T(8,128)(2,1)S(1)} custom-call(s32[4]{0:T(128)S(1)} %pad_add_fusion.where_ref, bf16[16,32,128]{2,1,0:T(8,128)(2,1)S(1)} %pad_maximum_fusion.q_ref, bf16[64,48,128]{2,1,0:T(8,128)(2,1)S(1)} %collective-permute-done.2.other_ref, f32[64,512]{1,0:T(8,128)S(1)} %get-tuple-element.7.sum_ref, f32[16,512]{1,0:T(8,128)S(1)} %get-tuple-element.8.stat_ref, ...), custom_call_target="tpu_custom_call" | custom-call | tf_op jit(solution)/shard_map/attend/pallas_call | solution.py:217
  55.3 23.1 %all_to_all.21 = bf16[64,8,128]{2,1,0:T(8,128)(2,1)S(1)} all-to-all(bf16[64,8,128]{2,1,0:T(8,128)(2,1)S(1)} %bitcast.34), channel_id=1, replica_groups={{144,145,400,401,160,161,416,417,176,177,432,433,192,193,448,449,208,20..., dimensions={0} | all-to-all | bytes 262144 | tf_op jit(solution)/shard_map/all_to_all | solution.py:283
  78.4 0.0 copy-done.4
  78.4 0.8 %finish.1 = (f32[32,32]{1,0:T(8,128)}, f32[32,32]{1,0:T(8,128)}) custom-call(bf16[512,128]{1,0:T(8,128)(2,1)S(1)} %bitcast.35, f32[32,32]{1,0:T(8,128)S(1)} %copy-done.4), custom_call_target="tpu_custom_call" | custom-call | tf_op jit(solution)/shard_map/finish/pallas_call | solution.py:239
  (7 shorter events, 0.1 us)
Async XLA Ops:
  2.7 27.5 %all-to-all-start = ((bf16[16,56,128]{2,1,0:T(8,128)(2,1)}), bf16[16,56,128]{2,1,0:T(8,128)(2,1)S(1)}, u32[]{:S(2)}, u32[]{:S(2)}) async-start(bf16[16,56,128]{2,1,0:T(8,128)(2,1)} %pack.1), calls=%async_computation | async-start | bytes 458752 | tf_op jit(solution)/shard_map/all_to_all | solution.py:265
  20.0 1.3 %copy-start = (bf16[1,512,10,128]{3,1,2,0:T(8,128)(2,1)S(1)}, bf16[1,512,10,128]{3,1,2,0:T(8,128)(2,1)}, u32[]{:S(2)}) copy-start(bf16[1,512,10,128]{3,1,2,0:T(8,128)(2,1)} %param.12) | copy-start | bytes 3932164
  21.3 1.3 %copy-start.1 = (bf16[1,512,10,128]{3,1,2,0:T(8,128)(2,1)S(1)}, bf16[1,512,10,128]{3,1,2,0:T(8,128)(2,1)}, u32[]{:S(2)}) copy-start(bf16[1,512,10,128]{3,1,2,0:T(8,128)(2,1)} %param.13) | copy-start | bytes 3932164
  22.7 0.9 %copy-start.2 = (bf16[10,128,64]{1,2,0:T(8,128)(2,1)S(1)}, bf16[10,128,64]{1,2,0:T(8,128)(2,1)}, u32[]{:S(2)}) copy-start(bf16[10,128,64]{1,2,0:T(8,128)(2,1)} %param.14) | copy-start | bytes 491524
  23.6 0.9 %copy-start.3 = (bf16[1,32,10,128]{3,1,2,0:T(8,128)(2,1)S(1)}, bf16[1,32,10,128]{3,1,2,0:T(8,128)(2,1)}, u32[]{:S(2)}) copy-start(bf16[1,32,10,128]{3,1,2,0:T(8,128)(2,1)} %param.11) | copy-start | bytes 245764
  31.3 12.7 %all-to-all-start.1 = ((bf16[4,16,48,128]{3,2,1,0:T(8,128)(2,1)}), bf16[4,16,48,128]{3,2,1,0:T(8,128)(2,1)S(1)}, u32[]{:S(2)}, u32[]{:S(2)}) async-start(bf16[4,16,48,128]{3,2,1,0:T(8,128)(2,1)} %broadcast_in_dim.25), calls=%async_computation.1 | async-start | bytes 1572864 | tf_op jit(solution)/shard_map/all_to_all | solution.py:269
  35.3 2.0 %collective-permute-start = (bf16[16,24,128]{2,1,0:T(8,128)(2,1)S(1)}, bf16[16,24,128]{2,1,0:T(8,128)(2,1)S(1)}, u32[]{:S(2)}, u32[]{:S(2)}) collective-permute-start(bf16[16,24,128]{2,1,0:T(8,128)(2,1)S(1)} %get-tuple-element.11), channel_id=1, source_target_pairs={{192,176},{240,224},{32,16},{80,64},{128,112},{193,177},{241,225},... | collective-permute-start | bytes 294920 | tf_op jit(solution)/shard_map/ppermute | solution.py:270
  36.0 6.6 %collective-permute-start.1 = (bf16[16,24,128]{2,1,0:T(8,128)(2,1)S(1)}, bf16[16,24,128]{2,1,0:T(8,128)(2,1)S(1)}, u32[]{:S(2)}, u32[]{:S(2)}) collective-permute-start(bf16[16,24,128]{2,1,0:T(8,128)(2,1)S(1)} %get-tuple-element.10), channel_id=1, source_target_pairs={{192,208},{240,0},{32,48},{80,96},{128,144},{193,209},{241,1},{33,... | collective-permute-start | bytes 294920 | tf_op jit(solution)/shard_map/ppermute | solution.py:271
  44.0 9.0 %collective-permute-start.2 = (bf16[64,48,128]{2,1,0:T(8,128)(2,1)S(1)}, bf16[64,48,128]{2,1,0:T(8,128)(2,1)S(1)}, u32[]{:S(2)}, u32[]{:S(2)}) collective-permute-start(bf16[64,48,128]{2,1,0:T(8,128)(2,1)S(1)} %fusion.own_ref), channel_id=1, source_target_pairs={{0,2},{2,0},{1,3},{3,1},{4,6},{6,4},{5,7},{7,5},{8,10},{10,8},{9,1... | collective-permute-start | bytes 2359304 | tf_op jit(solution)/shard_map/ppermute | solution.py:278
  51.1 27.2 %copy-start.4 = (f32[32,32]{1,0:T(8,128)S(1)}, f32[32,32]{1,0:T(8,128)}, u32[]{:S(2)}) copy-start(f32[32,32]{1,0:T(8,128)} %latent_ref.1) | copy-start | bytes 12292
